TPU v7x, 32 devices: a whole 2x2x4 slice. The times are simulated.
32 devices in a mesh: section: 2 (over y), dp: 4 (over z), tensor: 4 (over x, core).
Axes of the slice: x: 2, y: 2, z: 4, core: 2. Of those that a mesh axis runs over, the one named last changes fastest.
Arguments:
- inputs: bfloat16 [8, 640, 768], P('dp'), may hold values from -6 to 6
- plan: int32 [4, 2], P('dp'), may hold values from 0 to 1, each once within a row
- cotangent: bfloat16 [8, 640, 768], P('dp'), may hold values from -6 to 6
- w_qkv: bfloat16 [2, 3, 768, 768], P('section', None, 'dp', 'tensor'), may hold values from -0.21875 to 0.21875
- w_out: bfloat16 [2, 768, 768], P('section', 'tensor', 'dp'), may hold values from -1.75 to 1.75
- w_fc1: bfloat16 [2, 768, 3072], P('section', 'dp', 'tensor'), may hold values from -0.21875 to 0.21875
- w_fc2: bfloat16 [2, 3072, 768], P('section', 'tensor', 'dp'), may hold values from -0.109375 to 0.109375
- ln_gains: bfloat16 [2, 2, 768], P('section', None, 'dp'), may hold values from 0.099609375 to 1.8984375
- biases: bfloat16 [2, 4, 768], P('section', None, 'dp'), may hold values from -2 to 2
- qv_bias: bfloat16 [2, 2, 4, 192], P('section', None, 'tensor', 'dp'), may hold values from -2 to 2
- fc1_bias: bfloat16 [2, 4, 768], P('section', 'tensor', 'dp'), may hold values from -2 to 2
Outputs:
- hidden_states: bfloat16 [2, 8, 640, 768], P('section', 'dp')
- grad_inputs: float32 [2, 8, 640, 768], P('section', 'dp')
- grad_w_qkv: float32 [2, 3, 768, 768], P('section', None, 'dp', 'tensor')
- grad_w_out: float32 [2, 768, 768], P('section', 'tensor', 'dp')
- grad_w_fc1: float32 [2, 768, 3072], P('section', 'dp', 'tensor')
- grad_w_fc2: float32 [2, 3072, 768], P('section', 'tensor', 'dp')
- grad_ln_gains: float32 [2, 2, 768], P('section', None, 'dp')
- grad_biases: float32 [2, 4, 768], P('section', None, 'dp')
- grad_qv_bias: float32 [2, 2, 4, 192], P('section', None, 'tensor', 'dp')
- grad_fc1_bias: float32 [2, 4, 768], P('section', 'tensor', 'dp')
Inputs may be any that keep to these rules, and one draw needn't show every extreme that they name: `plan`: each row holds every clip index of its data shard once, 0 to 1.
All inputs are finite; a program needn't handle non-finite values.
Results may differ from a plain program's by a relative error of at most 0.015.
Values may be sent and summed in bfloat16 or wider, within the bound.
No kernel may reach another device: no remote copies, remote signals or barrier semaphores. Data moves between devices by JAX's collectives and lax.ppermute only.
A program may use at most 128 MiB of HBM per device.

v0:
```python
import jax
import jax.numpy as jnp
from jax import lax
from jax.sharding import PartitionSpec as P

HD = 64


eps = 1e-05


def from_behind(value, axis, steps):
    count = lax.axis_size(axis)
    leading, last = (max(0, -steps), min(count, count - steps))
    return lax.ppermute(value, axis, [(source, source + steps) for source in range(leading, last)])


def fetch_weights(shards):
    return (
        lax.all_gather(shards[0], "dp", axis=2, tiled=True),
        lax.all_gather(shards[1], "dp", axis=2, tiled=True),
        lax.all_gather(shards[2], "dp", axis=1, tiled=True),
        lax.all_gather(shards[3], "dp", axis=2, tiled=True),
        lax.all_gather(shards[4], "dp", axis=2, tiled=True),
        lax.all_gather(shards[5], "dp", axis=2, tiled=True),
        lax.all_gather(shards[6], "dp", axis=3, tiled=True),
        lax.all_gather(shards[7], "dp", axis=2, tiled=True),
    )


def forward_total(partial_value):
    return lax.psum(partial_value, "tensor")


def backward_total(partial_value):
    return lax.psum(partial_value, "tensor")


def unpack(gathered):
    w_qkv, w_out, w_fc1, w_fc2, gains, offsets, qv_bias, fc1_bias = gathered
    return (
        w_qkv[0],
        w_out[0],
        w_fc1[0],
        w_fc2[0],
        gains[0].astype(jnp.float32),
        offsets[0].astype(jnp.float32),
        qv_bias[0, :, 0].astype(jnp.float32),
        fc1_bias[0, 0].astype(jnp.float32),
    )


def norm_forward(tensor_in, gains, offset):
    average = jnp.mean(tensor_in, axis=-1, keepdims=True)
    centered = tensor_in - average
    spread = jnp.mean(centered * centered, axis=-1, keepdims=True)
    inv_std = lax.rsqrt(spread + eps)
    normal = centered * inv_std
    return (normal * gains + offset, normal, inv_std)


def norm_backward(upstream, normal, inv_std, gains):
    scaled = upstream * gains
    centered_grad = (
        scaled
        - jnp.mean(scaled, axis=-1, keepdims=True)
        - normal * jnp.mean(scaled * normal, axis=-1, keepdims=True)
    )
    return (inv_std * centered_grad, jnp.sum(upstream * normal, axis=0), jnp.sum(upstream, axis=0))


def exact_gelu(tensor_in):
    return jax.nn.gelu(tensor_in, approximate=False)


def layer_forward(tensor_in, weights, head_size):
    w_qkv, w_out, w_fc1, w_fc2, gains, offsets, qv_bias, fc1_bias = weights
    frames = tensor_in.shape[0]
    head_count = w_qkv.shape[2] // head_size
    score_scale = head_size ** (-0.5)
    normed, normal_one, inv_std_one = norm_forward(tensor_in, gains[0], offsets[0])
    normed_low = normed.astype(jnp.bfloat16)
    projected = jnp.einsum("fd,ide->ife", normed_low, w_qkv, preferred_element_type=jnp.float32)
    queries = (projected[0] + qv_bias[0]).astype(jnp.bfloat16)
    key_rows = projected[1].astype(jnp.bfloat16)
    value_rows = (projected[2] + qv_bias[1]).astype(jnp.bfloat16)
    query_heads = queries.reshape(frames, head_count, head_size)
    key_heads = key_rows.reshape(frames, head_count, head_size)
    value_heads = value_rows.reshape(frames, head_count, head_size)
    scores = (
        jnp.einsum("qhd,khd->hqk", query_heads, key_heads, preferred_element_type=jnp.float32)
        * score_scale
    )
    row_max = jnp.max(scores, axis=-1, keepdims=True)
    exp_scores = jnp.exp(scores - row_max)
    row_total = jnp.sum(exp_scores, axis=-1, keepdims=True)
    attn_probs = exp_scores / row_total
    logsum = row_max + jnp.log(row_total)
    mixed_heads = jnp.einsum(
        "hqk,khd->qhd",
        attn_probs.astype(jnp.bfloat16),
        value_heads,
        preferred_element_type=jnp.float32,
    )
    mixed_heads = mixed_heads.reshape(frames, -1).astype(jnp.bfloat16)
    attn_part = jnp.dot(mixed_heads, w_out, preferred_element_type=jnp.float32)
    residual = tensor_in + forward_total(attn_part) + offsets[2]
    normed_two, normal_two, inv_std_two = norm_forward(residual, gains[1], offsets[1])
    normed_two_low = normed_two.astype(jnp.bfloat16)
    hidden = jnp.dot(normed_two_low, w_fc1, preferred_element_type=jnp.float32) + fc1_bias
    active = exact_gelu(hidden).astype(jnp.bfloat16)
    result = (
        residual
        + forward_total(jnp.dot(active, w_fc2, preferred_element_type=jnp.float32))
        + offsets[3]
    )
    stored = (
        normal_one,
        inv_std_one,
        normed_low,
        queries,
        key_rows,
        value_rows,
        logsum,
        mixed_heads,
        normal_two,
        inv_std_two,
        normed_two_low,
        hidden,
        active,
    )
    return (result, stored)


def layer_backward(upstream, stored, weights, head_size):
    w_qkv, w_out, w_fc1, w_fc2, gains, offsets, qv_bias, fc1_bias = weights
    (
        normal_one,
        inv_std_one,
        normed_low,
        queries,
        key_rows,
        value_rows,
        logsum,
        mixed_heads,
        normal_two,
        inv_std_two,
        normed_two_low,
        hidden,
        active,
    ) = stored
    frames = upstream.shape[0]
    head_count = w_qkv.shape[2] // head_size
    score_scale = head_size ** (-0.5)
    upstream_low = upstream.astype(jnp.bfloat16)
    grad_fc2 = jnp.einsum("fa,fd->ad", active, upstream_low, preferred_element_type=jnp.float32)
    grad_bias_fc2 = jnp.sum(upstream_low.astype(jnp.float32), axis=0)
    grad_active = jnp.einsum("fd,ad->fa", upstream_low, w_fc2, preferred_element_type=jnp.float32)
    gelu_value, gelu_pull = jax.vjp(exact_gelu, hidden)
    grad_hidden = gelu_pull(grad_active)[0].astype(jnp.bfloat16)
    grad_fc1_bias = jnp.sum(grad_hidden.astype(jnp.float32), axis=0)
    grad_fc1 = jnp.einsum(
        "fd,fa->da", normed_two_low, grad_hidden, preferred_element_type=jnp.float32
    )
    partial_two = jnp.einsum("fa,da->fd", grad_hidden, w_fc1, preferred_element_type=jnp.float32)
    back_two, grad_gain_two, grad_shift_two = norm_backward(
        backward_total(partial_two), normal_two, inv_std_two, gains[1]
    )
    grad_residual = upstream + back_two
    residual_low = grad_residual.astype(jnp.bfloat16)
    grad_bias_out = jnp.sum(residual_low.astype(jnp.float32), axis=0)
    grad_out = jnp.einsum(
        "fa,fd->ad", mixed_heads, residual_low, preferred_element_type=jnp.float32
    )
    grad_mixed = jnp.einsum(
        "fd,ad->fa", residual_low, w_out, preferred_element_type=jnp.float32
    ).astype(jnp.bfloat16)
    query_heads = queries.reshape(frames, head_count, head_size)
    key_heads = key_rows.reshape(frames, head_count, head_size)
    value_heads = value_rows.reshape(frames, head_count, head_size)
    grad_heads = grad_mixed.reshape(frames, head_count, head_size)
    scores = (
        jnp.einsum("qhd,khd->hqk", query_heads, key_heads, preferred_element_type=jnp.float32)
        * score_scale
    )
    attn_probs = jnp.exp(scores - logsum)
    probs_low = attn_probs.astype(jnp.bfloat16)
    grad_values = jnp.einsum(
        "hqk,qhd->khd", probs_low, grad_heads, preferred_element_type=jnp.float32
    )
    grad_probs = jnp.einsum(
        "qhd,khd->hqk", grad_heads, value_heads, preferred_element_type=jnp.float32
    )
    grad_scores = attn_probs * (
        grad_probs - jnp.sum(attn_probs * grad_probs, axis=-1, keepdims=True)
    )
    scores_low = grad_scores.astype(jnp.bfloat16)
    grad_queries = (
        jnp.einsum("hqk,khd->qhd", scores_low, key_heads, preferred_element_type=jnp.float32)
        * score_scale
    )
    grad_keys = (
        jnp.einsum("hqk,qhd->khd", scores_low, query_heads, preferred_element_type=jnp.float32)
        * score_scale
    )
    grad_queries = grad_queries.reshape(frames, -1).astype(jnp.bfloat16)
    grad_keys = grad_keys.reshape(frames, -1).astype(jnp.bfloat16)
    grad_values = grad_values.reshape(frames, -1).astype(jnp.bfloat16)
    grad_proj = jnp.stack([grad_queries, grad_keys, grad_values])
    grad_qkv = jnp.einsum("fd,ife->ide", normed_low, grad_proj, preferred_element_type=jnp.float32)
    grad_qv_bias = jnp.stack(
        [
            jnp.sum(grad_queries.astype(jnp.float32), axis=0),
            jnp.sum(grad_values.astype(jnp.float32), axis=0),
        ]
    )
    partial_one = jnp.einsum("ife,ide->fd", grad_proj, w_qkv, preferred_element_type=jnp.float32)
    back_one, grad_gain_one, grad_shift_one = norm_backward(
        backward_total(partial_one), normal_one, inv_std_one, gains[0]
    )
    grad_input = grad_residual + back_one
    gradients = (
        grad_qkv,
        grad_out,
        grad_fc1,
        grad_fc2,
        jnp.stack([grad_gain_one, grad_gain_two]),
        jnp.stack([grad_shift_one, grad_shift_two, grad_bias_out, grad_bias_fc2]),
        grad_qv_bias,
        grad_fc1_bias,
    )
    return (grad_input, gradients)


def local(inputs, plan, cotangent, w_qkv, w_out, w_fc1, w_fc2, ln_gains, biases, qv_bias, fc1_bias):
    shards = (w_qkv, w_out, w_fc1, w_fc2, ln_gains, biases, qv_bias, fc1_bias)
    micro_count = inputs.shape[0]
    head_size = HD
    first_section = lax.axis_index("section") == 0

    def weights_now():
        return unpack(fetch_weights(shards))

    received = jnp.zeros(inputs.shape[1:], jnp.bfloat16)
    caches = []
    results = []
    for moment in range(micro_count + 1):
        if moment < micro_count:
            clip_now = lax.dynamic_index_in_dim(inputs, plan[0, moment], 0, keepdims=False)
        else:
            clip_now = jnp.zeros_like(received)
        current = jnp.where(first_section, clip_now, received).astype(jnp.float32)
        result, stored = layer_forward(current, weights_now(), head_size)
        caches.append(stored)
        results.append(result)
        if moment < micro_count:
            received = from_behind(result.astype(jnp.bfloat16), "section", 1)
    hidden_states = jnp.stack(
        [
            jnp.where(first_section, results[slot_index], results[slot_index + 1])
            for slot_index in range(micro_count)
        ]
    ).astype(jnp.bfloat16)[None]
    totals = None
    sent_back = jnp.zeros(inputs.shape[1:], jnp.bfloat16)
    grads_in = []
    for moment in range(micro_count + 1):
        if moment < micro_count:
            outside = cotangent[moment].astype(jnp.float32)
        else:
            outside = jnp.zeros(inputs.shape[1:], jnp.float32)
        incoming = jnp.where(first_section, sent_back.astype(jnp.float32), outside)
        active_flag = jnp.where(first_section, float(moment >= 1), float(moment < micro_count))
        stored = jax.tree.map(
            lambda early_cache, late_cache: jnp.where(first_section, early_cache, late_cache),
            caches[max(moment - 1, 0)],
            caches[min(moment + 1, micro_count)],
        )
        grad_input, gradients = layer_backward(
            incoming * active_flag, stored, weights_now(), head_size
        )
        totals = gradients if totals is None else jax.tree.map(jnp.add, totals, gradients)
        grads_in.append(grad_input)
        if moment < micro_count:
            sent_back = from_behind(grad_input.astype(jnp.bfloat16), "section", -1)
    grad_inputs = jnp.stack(
        [
            jnp.where(first_section, grads_in[slot_index + 1], grads_in[slot_index])
            for slot_index in range(micro_count)
        ]
    )[None]
    summed = (
        lax.psum_scatter(totals[0][None], "dp", scatter_dimension=2, tiled=True),
        lax.psum_scatter(totals[1][None], "dp", scatter_dimension=2, tiled=True),
        lax.psum_scatter(totals[2][None], "dp", scatter_dimension=1, tiled=True),
        lax.psum_scatter(totals[3][None], "dp", scatter_dimension=2, tiled=True),
        lax.psum_scatter(totals[4][None], "dp", scatter_dimension=2, tiled=True),
        lax.psum_scatter(totals[5][None], "dp", scatter_dimension=2, tiled=True),
        lax.psum_scatter(totals[6][None, :, None], "dp", scatter_dimension=3, tiled=True),
        lax.psum_scatter(totals[7][None, None], "dp", scatter_dimension=2, tiled=True),
    )
    return (
        hidden_states,
        grad_inputs,
        summed[0],
        summed[1],
        summed[2],
        summed[3],
        summed[4],
        summed[5],
        summed[6],
        summed[7],
    )


def solution(mesh):
    placed = (
        P("dp", None, None),
        P("dp", None),
        P("dp", None, None),
        P("section", None, "dp", "tensor"),
        P("section", "tensor", "dp"),
        P("section", "dp", "tensor"),
        P("section", "tensor", "dp"),
        P("section", None, "dp"),
        P("section", None, "dp"),
        P("section", None, "tensor", "dp"),
        P("section", "tensor", "dp"),
    )
    return jax.shard_map(
        local,
        mesh=mesh,
        in_specs=placed,
        out_specs=(
            P("section", "dp", None, None),
            P("section", "dp", None, None),
            P("section", None, "dp", "tensor"),
            P("section", "tensor", "dp"),
            P("section", "dp", "tensor"),
            P("section", "tensor", "dp"),
            P("section", None, "dp"),
            P("section", None, "dp"),
            P("section", None, "tensor", "dp"),
            P("section", "tensor", "dp"),
        ),
        check_vma=False,
    )
```

profile of v0, /device:TPU:0, one launch (start us, length us, event | category | flops | bytes accessed | tf_op | source)
XLA Modules:
  0.0 1126.5 jit_solution(7311334126329515601)
XLA Ops:
  14.7 16.2 %all_gather.16 = bf16[1,2,768]{1,0,2:T(2,128)(2,1)S(1)} all-gather(bf16[1,2,192]{1,0,2:T(2,128)(2,1)S(1)} %copy.57), channel_id=1, replica_groups=mesh['section'=2,'dp'=4,'tensor'=4] {'dp'}, dimensions={2}, use_global_device_ids=true | all-gather | bytes 3840 | tf_op jit(solution)/shard_map/all_gather | solution.py:24
  36.0 15.6 %all_gather.17 = bf16[1,4,768]{1,0,2:T(2,128)(2,1)S(1)} all-gather(bf16[1,4,192]{1,0,2:T(2,128)(2,1)S(1)} %copy.58), channel_id=1, replica_groups=mesh['section'=2,'dp'=4,'tensor'=4] {'dp'}, dimensions={2}, use_global_device_ids=true | all-gather | bytes 7680 | tf_op jit(solution)/shard_map/all_gather | solution.py:25
  52.1 10.9 slice_reduce_fusion.1
  63.3 26.8 %all_gather.18 = bf16[1,3,768,192]{3,1,0,2:T(4,128)(2,1)} all-gather(bf16[1,3,192,192]{3,1,0,2:T(4,128)(2,1)S(1)} %copy.59), channel_id=1, replica_groups=mesh['section'=2,'dp'=4,'tensor'=4] {'dp'}, dimensions={2}, use_global_device_ids=true | all-gather | bytes 1105920 | tf_op jit(solution)/shard_map/all_gather | solution.py:20
  94.6 13.3 %all_gather.19 = bf16[1,2,1,192]{2,1,0,3:T(2,128)(2,1)S(1)} all-gather(bf16[1,2,1,48]{2,1,0,3:T(2,128)(2,1)S(1)} %copy.61), channel_id=1, replica_groups=mesh['section'=2,'dp'=4,'tensor'=4] {'dp'}, dimensions={3}, use_global_device_ids=true | all-gather | bytes 960 | tf_op jit(solution)/shard_map/all_gather | solution.py:26
  109.5 16.0 %all_gather.20 = bf16[1,192,768]{1,0,2:T(2,128)(2,1)S(1)} all-gather(bf16[1,192,192]{1,0,2:T(2,128)(2,1)S(1)} %copy.63), channel_id=1, replica_groups=mesh['section'=2,'dp'=4,'tensor'=4] {'dp'}, dimensions={2}, use_global_device_ids=true | all-gather | bytes 368640 | tf_op jit(solution)/shard_map/all_gather | solution.py:21
  133.8 10.8 all-reduce
  144.5 35.7 %all-reduce.16.cloned.1.call-done = f32[640,768]{1,0:T(8,128)} async-done(((f32[640,768]{1,0:T(8,128)}), f32[640,768]{1,0:T(8,128)}) %all-reduce.16.cloned.1.call-update) | async-done | bytes 1966096 | tf_op jit(solution)/shard_map/psum | solution.py:32
  197.5 48.6 %all-reduce.18.cloned.1.call-done = f32[640,768]{1,0:T(8,128)} async-done(((f32[640,768]{1,0:T(8,128)}), f32[640,768]{1,0:T(8,128)}) %all-reduce.18.cloned.1.call-update) | async-done | bytes 1966096 | tf_op jit(solution)/shard_map/psum | solution.py:32
  254.2 18.0 %collective-permute-done = bf16[640,768]{1,0:T(8,128)(2,1)} collective-permute-done((bf16[640,768]{1,0:T(8,128)(2,1)S(1)}, bf16[640,768]{1,0:T(8,128)(2,1)}, u32[]{:S(2)}, u32[]{:S(2)}) %collective-permute-start) | collective-permute-done | bytes 983072 | tf_op jit(solution)/shard_map/ppermute | solution.py:15
  281.8 50.8 %all-reduce.20.cloned.1.call-done = f32[640,768]{1,0:T(8,128)} async-done(((f32[640,768]{1,0:T(8,128)}), f32[640,768]{1,0:T(8,128)}) %all-reduce.20.cloned.1.call-update) | async-done | bytes 1966096 | tf_op jit(solution)/shard_map/psum | solution.py:32
  356.6 77.6 %all-reduce.34.cloned.1.call-done = (f32[640,768]{1,0:T(8,128)}, f32[640,768]{1,0:T(8,128)}) async-done(((f32[640,768]{1,0:T(8,128)}, f32[640,768]{1,0:T(8,128)}), (f32[640,768]{1,0:T(8,128)}, f32[640,768]{1,0:T(8,128)})) %all-reduce.34.cloned.1.call-update) | async-done | bytes 3932176 | tf_op jit(solution)/shard_map/psum | solution.py:32
  446.1 16.8 %collective-permute-done.1 = bf16[640,768]{1,0:T(8,128)(2,1)S(1)} collective-permute-done((bf16[640,768]{1,0:T(8,128)(2,1)S(1)}, bf16[640,768]{1,0:T(8,128)(2,1)S(1)}, u32[]{:S(2)}, u32[]{:S(2)}) %collective-permute-start.1) | collective-permute-done | bytes 983072 | tf_op jit(solution)/shard_map/ppermute | solution.py:15
  481.8 82.9 %all-reduce.32.cloned.1.call-done = (f32[640,768]{1,0:T(8,128)}, f32[640,768]{1,0:T(8,128)}) async-done(((f32[640,768]{1,0:T(8,128)}, f32[640,768]{1,0:T(8,128)}), (f32[640,768]{1,0:T(8,128)}, f32[640,768]{1,0:T(8,128)})) %all-reduce.32.cloned.1.call-update) | async-done | bytes 3932176 | tf_op jit(solution)/shard_map/psum | solution.py:32
  582.3 15.2 %collective-permute-done.2 = bf16[640,768]{1,0:T(8,128)(2,1)S(1)} collective-permute-done((bf16[640,768]{1,0:T(8,128)(2,1)S(1)}, bf16[640,768]{1,0:T(8,128)(2,1)S(1)}, u32[]{:S(2)}, u32[]{:S(2)}) %collective-permute-start.2) | collective-permute-done | bytes 983072 | tf_op jit(solution)/shard_map/ppermute | solution.py:15
  611.6 44.6 %all-reduce.22.cloned.1.call-done = f32[640,768]{1,0:T(8,128)} async-done(((f32[640,768]{1,0:T(8,128)}), f32[640,768]{1,0:T(8,128)}) %all-reduce.22.cloned.1.call-update) | async-done | bytes 1966096 | tf_op jit(solution)/shard_map/psum | solution.py:36
  672.3 49.4 %all-reduce.24.cloned.1.call-done = f32[640,768]{1,0:T(8,128)} async-done(((f32[640,768]{1,0:T(8,128)}), f32[640,768]{1,0:T(8,128)}) %all-reduce.24.cloned.1.call-update) | async-done | bytes 1966096 | tf_op jit(solution)/shard_map/psum | solution.py:36
  733.0 24.3 %collective-permute-done.3 = bf16[640,768]{1,0:T(8,128)(2,1)} collective-permute-done((bf16[640,768]{1,0:T(8,128)(2,1)}, bf16[640,768]{1,0:T(8,128)(2,1)}, u32[]{:S(2)}, u32[]{:S(2)}) %collective-permute-start.3) | collective-permute-done | bytes 983072 | tf_op jit(solution)/shard_map/ppermute | solution.py:15
  757.4 8.3 convert_reduce_fusion.3
  776.3 41.3 %all-reduce.26.cloned.1.call-done = f32[640,768]{1,0:T(8,128)} async-done(((f32[640,768]{1,0:T(8,128)}), f32[640,768]{1,0:T(8,128)}) %all-reduce.26.cloned.1.call-update) | async-done | bytes 1966096 | tf_op jit(solution)/shard_map/psum | solution.py:36
  886.5 30.9 %all-reduce.30.cloned.1.call-done = (f32[640,768]{1,0:T(8,128)}, f32[640,768]{1,0:T(8,128)}) async-done(((f32[640,768]{1,0:T(8,128)}, f32[640,768]{1,0:T(8,128)}), (f32[640,768]{1,0:T(8,128)}, f32[640,768]{1,0:T(8,128)})) %all-reduce.30.cloned.1.call-update) | async-done | bytes 3932176 | tf_op jit(solution)/shard_map/psum | solution.py:32
  951.5 72.5 %all-reduce.28.cloned.1.call-done = f32[1,768,768]{1,0,2:T(1,128)} async-done(((f32[1,768,768]{1,0,2:T(1,128)}), f32[1,768,768]{1,0,2:T(1,128)}) %all-reduce.28.cloned.1.call-update) | async-done | bytes 2359312
  1038.3 30.7 %reduce-scatter.22.cloned.1.call-done = f32[192,576]{1,0:T(8,128)} async-done(((f32[768,576]{1,0:T(8,128)}), f32[192,576]{1,0:T(8,128)}) %reduce-scatter.22.cloned.1.call-update) | async-done | bytes 442384
  1071.3 47.4 %reduce-scatter.20.cloned.1.call-done = f32[1,192,768]{2,1,0:T(8,128)} async-done(((f32[1,768,768]{2,1,0:T(8,128)}), f32[1,192,768]{2,1,0:T(8,128)}) %reduce-scatter.20.cloned.1.call-update) | async-done | bytes 589840 | tf_op jit(solution)/shard_map/reduce_scatter | solution.py:295
  (663 shorter events, 297.7 us)
Async XLA Ops:
  8.0 172.2 %all-reduce.16.cloned.1.call-start = ((), (), s32[]{:S(2)}) async-start(), calls=%async_computation.7 | async-start | bytes 3932160 | tf_op jit(solution)/shard_map/psum | solution.py:32
  12.8 712.9 %copy-start.96 = (f32[640]{0:T(1024)}, f32[640]{0:T(1024)S(1)}, u32[]{:S(2)}) copy-start(f32[640]{0:T(1024)S(1)} %broadcast_multiply_fusion.17) | copy-start | bytes 7684
  130.9 51.9 %all-gather.3.cloned.1.call-start = ((), (), s32[]{:S(2)}) async-start(), calls=%async_computation.8 | async-start | bytes 1474560 | tf_op jit(solution)/shard_map/all_gather | solution.py:22
  131.5 62.4 %all-gather.5.cloned.1.call-start = ((), (), s32[]{:S(2)}) async-start(), calls=%async_computation.9 | async-start | bytes 1474560 | tf_op jit(solution)/shard_map/all_gather | solution.py:23
  132.1 114.0 %all-reduce.18.cloned.1.call-start = ((), (), s32[]{:S(2)}) async-start(), calls=%async_computation.10 | async-start | bytes 3932160 | tf_op jit(solution)/shard_map/psum | solution.py:32
  197.5 135.2 %all-reduce.20.cloned.1.call-start = ((), (), s32[]{:S(2)}) async-start(), calls=%async_computation.11 | async-start | bytes 3932160 | tf_op jit(solution)/shard_map/psum | solution.py:32
  247.9 24.3 %collective-permute-start = (bf16[640,768]{1,0:T(8,128)(2,1)S(1)}, bf16[640,768]{1,0:T(8,128)(2,1)}, u32[]{:S(2)}, u32[]{:S(2)}) collective-permute-start(bf16[640,768]{1,0:T(8,128)(2,1)S(1)} %fusion.217), channel_id=1, source_target_pairs={{0,16},{1,17},{2,18},{3,19},{4,20},{5,21},{6,22},{7,23},{8,24},{9,... | collective-permute-start | bytes 2949128 | tf_op jit(solution)/shard_map/ppermute | solution.py:15
  281.6 152.6 %all-reduce.34.cloned.1.call-start = ((), (), s32[]{:S(2)}) async-start(), calls=%async_computation.25 | async-start | bytes 7864320 | tf_op jit(solution)/shard_map/psum | solution.py:32
  352.5 212.2 %all-reduce.32.cloned.1.call-start = ((), (), s32[]{:S(2)}) async-start(), calls=%async_computation.24 | async-start | bytes 7864320 | tf_op jit(solution)/shard_map/psum | solution.py:32
  438.7 24.2 %collective-permute-start.1 = (bf16[640,768]{1,0:T(8,128)(2,1)S(1)}, bf16[640,768]{1,0:T(8,128)(2,1)S(1)}, u32[]{:S(2)}, u32[]{:S(2)}) collective-permute-start(bf16[640,768]{1,0:T(8,128)(2,1)S(1)} %get-tuple-element.89), channel_id=1, source_target_pairs={{0,16},{1,17},{2,18},{3,19},{4,20},{5,21},{6,22},{7,23},{8,24},{9,... | collective-permute-start | bytes 2949128 | tf_op jit(solution)/shard_map/ppermute | solution.py:15
  481.8 174.4 %all-reduce.22.cloned.1.call-start = ((), (), s32[]{:S(2)}) async-start(), calls=%async_computation.12 | async-start | bytes 3932160 | tf_op jit(solution)/shard_map/psum | solution.py:36
  572.3 25.2 %collective-permute-start.2 = (bf16[640,768]{1,0:T(8,128)(2,1)S(1)}, bf16[640,768]{1,0:T(8,128)(2,1)S(1)}, u32[]{:S(2)}, u32[]{:S(2)}) collective-permute-start(bf16[640,768]{1,0:T(8,128)(2,1)S(1)} %get-tuple-element.92), channel_id=1, source_target_pairs={{16,0},{17,1},{18,2},{19,3},{20,4},{21,5},{22,6},{23,7},{24,8},{25... | collective-permute-start | bytes 2949128 | tf_op jit(solution)/shard_map/ppermute | solution.py:15
  607.3 114.5 %all-reduce.24.cloned.1.call-start = ((), (), s32[]{:S(2)}) async-start(), calls=%async_computation.13 | async-start | bytes 3932160 | tf_op jit(solution)/shard_map/psum | solution.py:36
  672.3 145.3 %all-reduce.26.cloned.1.call-start = ((), (), s32[]{:S(2)}) async-start(), calls=%async_computation.14 | async-start | bytes 3932160 | tf_op jit(solution)/shard_map/psum | solution.py:36
  731.7 25.6 %collective-permute-start.3 = (bf16[640,768]{1,0:T(8,128)(2,1)}, bf16[640,768]{1,0:T(8,128)(2,1)}, u32[]{:S(2)}, u32[]{:S(2)}) collective-permute-start(bf16[640,768]{1,0:T(8,128)(2,1)} %convert_element_type.566), channel_id=1, source_target_pairs={{16,0},{17,1},{18,2},{19,3},{20,4},{21,5},{22,6},{23,7},{24,8},{25... | collective-permute-start | bytes 2949128 | tf_op jit(solution)/shard_map/ppermute | solution.py:15
  768.9 148.5 %all-reduce.30.cloned.1.call-start = ((), (), s32[]{:S(2)}) async-start(), calls=%async_computation.23 | async-start | bytes 7864320 | tf_op jit(solution)/shard_map/psum | solution.py:32
  835.7 110.9 %reduce-scatter.32.cloned.1.call-start = ((), (), s32[]{:S(2)}) async-start(), calls=%async_computation.21 | async-start | bytes 491520
  847.4 100.8 %reduce-scatter.30.cloned.1.call-start = ((), (), s32[]{:S(2)}) async-start(), calls=%async_computation.20 | async-start | bytes 122880
  854.8 94.9 %reduce-scatter.24.cloned.1.call-start = ((), (), s32[]{:S(2)}) async-start(), calls=%async_computation.17 | async-start | bytes 983040
  863.0 161.1 %all-reduce.28.cloned.1.call-start = ((), (), s32[]{:S(2)}) async-start(), calls=%async_computation.22 | async-start | bytes 4718592
  878.1 157.1 %reduce-scatter.26.cloned.1.call-start = ((), (), s32[]{:S(2)}) async-start(), calls=%async_computation.18 | async-start | bytes 491520
  921.5 115.2 %reduce-scatter.28.cloned.1.call-start = ((), (), s32[]{:S(2)}) async-start(), calls=%async_computation.19 | async-start | bytes 491520
  922.6 146.4 %reduce-scatter.22.cloned.1.call-start = ((), (), s32[]{:S(2)}) async-start(), calls=%async_computation.16 | async-start | bytes 2457600
  936.5 182.2 %reduce-scatter.20.cloned.1.call-start = ((), (), s32[]{:S(2)}) async-start(), calls=%async_computation.15 | async-start | bytes 2949120 | tf_op jit(solution)/shard_map/reduce_scatter | solution.py:295
  (206 other events, 4435.7 us)
Sparse Core Ops, SparseCore 0:
  131.1 49.1 all-reduce.15
  197.6 48.4 all-reduce.17
  281.7 50.8 all-reduce.19
  352.7 81.4 all-reduce.33
  481.9 82.8 all-reduce.31
  607.4 48.7 all-reduce.21
  672.4 49.3 all-reduce.23
  769.0 48.5 all-reduce.25
  835.8 81.5 all-reduce.29
  919.6 104.4 all-reduce.27
Sparse Core Ops, SparseCore 1:
  133.0 30.1 all-gather.2
  164.6 29.3 all-gather.4
  847.5 21.4 reduce-scatter.31
  871.2 17.0 reduce-scatter.29
  890.6 21.2 reduce-scatter.23
  921.6 52.7 reduce-scatter.25
  976.6 50.5 reduce-scatter.27
  1029.3 39.7 reduce-scatter.21
  1071.8 46.9 reduce-scatter.19
where the time goes:
time: 1130 us
  waiting for transfers between devices  692 us (61%)
  matrix products  142 us (13%)
  blocking collectives  98.8 us (9%)
  local copies, waits for them, and re-layouts  87 us (8%)
  other arithmetic  70.7 us (6%)
  between operations  24 us (2%)
  starting transfers between devices  12.5 us (1%)
    psum x6, waiting for transfers between devices, forward_total(): return lax.psum(partial_value, 'tensor')  327 us
    psum x3, waiting for transfers between devices, backward_total(): return lax.psum(partial_value, 'tensor')  135 us
    unnamed x26, waiting for transfers between devices  105 us
    ppermute x4, waiting for transfers between devices, from_behind(): lax.ppermute(value, axis, [(source, source + steps) for source in range(l...  74.4 us
    unnamed x441, local copies, waits for them, and re-layouts  50.7 us
    reduce_scatter x1, waiting for transfers between devices, local(): lax.psum_scatter(totals[2][None], 'dp', scatter_dimension=1, tiled=True)  47.4 us
    all_gather x1, blocking collectives, fetch_weights(): lax.all_gather(shards[0], 'dp', axis=2, tiled=True)  26.8 us
  transfers between devices with their start and end apart: 23, of which 17 were waited for; matrix products, arithmetic and copies ran while one was open for 12% of the time, Pallas kernels for 0%

commit v1 on v0

v1 whole, which is shorter than its diff:
```python
import functools

import jax
import jax.numpy as jnp
from jax import lax
from jax.experimental import pallas as pl
from jax.experimental.pallas import tpu as pltpu
from jax.sharding import PartitionSpec as P

HD = 64
EPS = 1e-05
MASKS = 4
F32 = jnp.float32
BF16 = jnp.bfloat16
ANY = pl.BlockSpec(memory_space=pl.ANY)
VMEM = pl.BlockSpec(memory_space=pltpu.VMEM)
SMEM = pl.BlockSpec(memory_space=pltpu.SMEM)


def flip(value, mask):
    count = lax.axis_size("tensor")
    return lax.ppermute(value, "tensor", [(i, i ^ mask) for i in range(count)])


def ring_next(value):
    count = lax.axis_size("dp")
    return lax.ppermute(value, "dp", [(i, (i + 1) % count) for i in range(count)])


def gather_pieces(shard):
    rows = [shard]
    for _ in range(lax.axis_size("dp") - 1):
        rows.append(ring_next(rows[-1]))
    pieces = []
    for own in rows:
        across = flip(own, 2)
        pieces.extend([own, flip(own, 1), across, flip(across, 1)])
    return pieces


def spread(value):
    across = flip(value, 2)
    return [value, flip(value, 1), across, flip(across, 1)]


def trade(blocks):
    return [blocks[0]] + [flip(blocks[m], m) for m in range(1, MASKS)]


def ring_scatter(blocks, me):
    count = blocks.shape[0]

    def block(step):
        return lax.dynamic_index_in_dim(blocks, (me - 1 - step) % count, 0, keepdims=False)

    moving = block(0)
    for step in range(1, count):
        moving = ring_next(moving.astype(BF16)).astype(F32) + block(step).astype(F32)
    return moving


def total(value):
    for mask in (1, 2):
        value = value + flip(value, mask)
    count = lax.axis_size("dp")
    step = 1
    while step < count:
        value = value + lax.ppermute(value, "dp", [(i, i ^ step) for i in range(count)])
        step *= 2
    return value


def load_pieces(pieces, scratch, sems, me):
    count = len(pieces) // MASKS
    rows = scratch.shape[1] // count
    copies = [[] for _ in range(MASKS)]
    for mask in range(MASKS):
        for step in range(count):
            index = step * MASKS + mask
            owner = lax.rem(me - step + count, count)
            copy = pltpu.make_async_copy(
                pieces[index],
                scratch.at[mask, pl.ds(pl.multiple_of(owner * rows, 16), rows)],
                sems.at[index],
            )
            copy.start()
            copies[mask].append(copy)
    return copies


def wait_all(copies):
    for copy in copies:
        copy.wait()


def dot(a, b):
    return lax.dot_general(a, b, (((1,), (0,)), ((), ())), preferred_element_type=F32)


def dot_nt(a, b):
    return lax.dot_general(a, b, (((1,), (1,)), ((), ())), preferred_element_type=F32)


def dot_tn(a, b):
    return lax.dot_general(a, b, (((0,), (0,)), ((), ())), preferred_element_type=F32)


def norm(x):
    average = jnp.mean(x, axis=-1, keepdims=True)
    centered = x - average
    spread_of = jnp.mean(centered * centered, axis=-1, keepdims=True)
    inv_std = lax.rsqrt(spread_of + EPS)
    return centered * inv_std, inv_std


def norm_pull(upstream, normal, inv_std, gains):
    scaled = upstream * gains
    return inv_std * (
        scaled
        - jnp.mean(scaled, axis=-1, keepdims=True)
        - normal * jnp.mean(scaled * normal, axis=-1, keepdims=True)
    )


def fill_keys(kv, own_ref, peer_ref):
    frames = own_ref.shape[1]
    kv[:, :frames, :] = own_ref[...]
    for mask in range(MASKS):
        kv[mask, frames:, :] = peer_ref[mask ^ 1]


def qkv_kernel(n, me_ref, x_ref, vec_ref, bias_ref, *refs):
    pieces = refs[: 4 * n]
    normed_ref, q_ref, kv_ref, w, sems = refs[4 * n :]
    copies = load_pieces(pieces, w, sems, me_ref[0])
    width = q_ref.shape[2]
    normal, _ = norm(x_ref[...].astype(F32))
    normed = (normal * vec_ref[0:1, :] + vec_ref[2:3, :]).astype(BF16)
    normed_ref[...] = normed
    for mask in range(MASKS):
        wait_all(copies[mask])
        out = dot(normed, w[mask, :, : 3 * width]) + bias_ref[mask : mask + 1, :]
        out = out.astype(BF16)
        q_ref[mask] = out[:, :width]
        kv_ref[mask] = out[:, width:]


def attend_kernel(n, keep, me_ref, x_ref, vec_ref, q_ref, kv_own_ref, kv_peer_ref, *refs):
    pieces = refs[: 4 * n]
    rest = refs[4 * n :]
    r_ref, c_ref = rest[:2]
    o_refs = rest[2:6] if keep else None
    p_ref = rest[6] if keep else None
    kv, w, sems = rest[-3:]
    copies = load_pieces(pieces, w, sems, me_ref[0])
    frames, width = q_ref.shape[1:]
    heads = width // HD
    fill_keys(kv, kv_own_ref, kv_peer_ref)
    r = x_ref[...].astype(F32) + vec_ref[4:5, :]
    for mask in range(MASKS):
        parts = []
        for head in range(heads):
            lo = head * HD
            q = q_ref[mask, :, lo : lo + HD]
            k = kv[mask, :, lo : lo + HD]
            v = kv[mask, :, width + lo : width + lo + HD]
            scores = dot_nt(q, k) * (HD**-0.5)
            e = jnp.exp(scores - jnp.max(scores, axis=-1, keepdims=True))
            p = (e * (1.0 / jnp.sum(e, axis=-1, keepdims=True))).astype(BF16)
            if keep:
                p_ref[mask * heads + head] = p
            parts.append(dot(p, v))
        o = jnp.concatenate(parts, axis=1).astype(BF16)
        if keep:
            o_refs[mask][...] = o
        wait_all(copies[mask])
        r = r + dot_nt(o, w[mask, :, 3 * width :])
    r_ref[...] = r
    normal, _ = norm(r)
    c_ref[...] = (normal * vec_ref[1:2, :] + vec_ref[3:4, :]).astype(BF16)


def hidden_kernel(n, keep, me_ref, r_ref, c_ref, vec_ref, fb_ref, *refs):
    p1, p2 = refs[: 4 * n], refs[4 * n : 8 * n]
    rest = refs[8 * n :]
    y_ref = rest[0]
    e_refs = rest[1:5] if keep else None
    g_ref = rest[5] if keep else None
    w1, w2, sems1, sems2 = rest[-4:]
    copies1 = load_pieces(p1, w1, sems1, me_ref[0])
    copies2 = load_pieces(p2, w2, sems2, me_ref[0])
    c = c_ref[...]
    y = r_ref[...] + vec_ref[5:6, :]
    for mask in range(MASKS):
        wait_all(copies1[mask])
        u = dot(c, w1[mask]) + fb_ref[mask : mask + 1, :]
        phi = 0.5 * (1.0 + lax.erf(u * (0.5**0.5)))
        e = (u * phi).astype(BF16)
        if keep:
            e_refs[mask][...] = e
            bell = jnp.exp(u * u * -0.5) * 0.3989422804014327
            g_ref[mask] = (phi + u * bell).astype(BF16)
        wait_all(copies2[mask])
        y = y + dot_nt(e, w2[mask])
    y_ref[...] = y.astype(BF16)


def hidden_back_kernel(n, me_ref, dy_ref, r_ref, vec_ref, g_ref, *refs):
    p2, p1, pa = refs[: 4 * n], refs[4 * n : 8 * n], refs[8 * n : 12 * n]
    rest = refs[12 * n :]
    du_refs = rest[:4]
    dr_ref, da_ref, do_ref, sums_ref, fsums_ref = rest[4:9]
    w2, w1, wa, sems2, sems1, semsa = rest[-6:]
    copies2 = load_pieces(p2, w2, sems2, me_ref[0])
    copies1 = load_pieces(p1, w1, sems1, me_ref[0])
    copiesa = load_pieces(pa, wa, semsa, me_ref[0])
    dm = dy_ref[...]
    dy = dm.astype(F32)
    width = do_ref.shape[2]
    dc = jnp.zeros(dy.shape, F32)
    for mask in range(MASKS):
        wait_all(copies2[mask])
        du = (dot(dm, w2[mask]) * g_ref[mask].astype(F32)).astype(BF16)
        du_refs[mask][...] = du
        fsums_ref[mask : mask + 1, :] = jnp.sum(du.astype(F32), axis=0, keepdims=True)
        wait_all(copies1[mask])
        dc = dc + dot_nt(du, w1[mask])
    normal, inv_std = norm(r_ref[...])
    dr = dy + norm_pull(dc, normal, inv_std, vec_ref[1:2, :])
    da = dr.astype(BF16)
    dr_ref[...] = dr
    da_ref[...] = da
    for mask in range(MASKS):
        wait_all(copiesa[mask])
        do_ref[mask] = dot(da, wa[mask, :, 3 * width :]).astype(BF16)
    sums_ref[...] = jnp.zeros(sums_ref.shape, F32)
    sums_ref[0:1, :] = jnp.sum(dy, axis=0, keepdims=True)
    sums_ref[1:2, :] = jnp.sum(dc * normal, axis=0, keepdims=True)
    sums_ref[2:3, :] = jnp.sum(dc, axis=0, keepdims=True)
    sums_ref[3:4, :] = jnp.sum(da.astype(F32), axis=0, keepdims=True)


def attend_back_kernel(do_ref, q_ref, kv_own_ref, kv_peer_ref, p_ref, dq_ref, own_ref, peer_ref, kv):
    frames, width = q_ref.shape[1:]
    heads = width // HD
    fill_keys(kv, kv_own_ref, kv_peer_ref)
    scale = HD**-0.5
    for mask in range(MASKS):
        dqs, dks, dvs = [], [], []
        for head in range(heads):
            lo = head * HD
            q = q_ref[mask, :, lo : lo + HD]
            k = kv[mask, :, lo : lo + HD]
            v = kv[mask, :, width + lo : width + lo + HD]
            do = do_ref[mask, :, lo : lo + HD]
            p_low = p_ref[mask * heads + head]
            p = p_low.astype(F32)
            dp = dot_nt(do, v)
            t = p * dp
            ds = (t - p * jnp.sum(t, axis=-1, keepdims=True)).astype(BF16)
            dqs.append(dot(ds, k) * scale)
            dks.append(dot_tn(q, ds) * scale)
            dvs.append(dot_tn(do, p_low))
        dq_ref[mask] = jnp.concatenate(dqs, axis=1).astype(BF16)
        both = jnp.concatenate(dks + dvs, axis=0)
        back = both.T
        own_ref[mask] = back[:frames]
        peer_ref[mask ^ 1] = back[frames:].astype(BF16)


def input_back_kernel(n, me_ref, x_ref, dr_ref, vec_ref, dq_ref, own_ref, recv_ref, *refs):
    pieces = refs[: 4 * n]
    rest = refs[4 * n :]
    dx_ref = rest[0]
    d_refs = rest[1:5]
    sums_ref, qsums_ref, w, sems = rest[5:]
    copies = load_pieces(pieces, w, sems, me_ref[0])
    width = dq_ref.shape[2]
    dn = jnp.zeros(dr_ref.shape, F32)
    for mask in range(MASKS):
        dkv = (own_ref[mask] + recv_ref[mask].astype(F32)).astype(BF16)
        d = jnp.concatenate([dq_ref[mask], dkv], axis=1)
        d_refs[mask][...] = d
        qsums_ref[mask : mask + 1, :] = jnp.sum(d.astype(F32), axis=0, keepdims=True)
        wait_all(copies[mask])
        dn = dn + dot_nt(d, w[mask, :, : 3 * width])
    normal, inv_std = norm(x_ref[...].astype(F32))
    dx = dr_ref[...] + norm_pull(dn, normal, inv_std, vec_ref[0:1, :])
    dx_ref[...] = dx.astype(BF16)
    sums_ref[...] = jnp.zeros(sums_ref.shape, F32)
    sums_ref[0:1, :] = jnp.sum(dn * normal, axis=0, keepdims=True)
    sums_ref[1:2, :] = jnp.sum(dn, axis=0, keepdims=True)


def weight_kernel(n, *refs):
    left, right, out_ref = refs[:MASKS], refs[MASKS : 2 * MASKS], refs[-1]
    acc = None
    for mask in range(MASKS):
        term = dot_tn(left[mask][...], right[mask][...])
        acc = term if acc is None else acc + term
    rows = out_ref.shape[1]
    for block in range(n):
        out_ref[block] = acc[block * rows : (block + 1) * rows].astype(BF16)


def shape(dims, dtype):
    return jax.ShapeDtypeStruct(dims, dtype)


def call(body, in_specs, out_shape, scratch, flops, name):
    return pl.pallas_call(
        body,
        in_specs=in_specs,
        out_specs=jax.tree.map(lambda _: VMEM, out_shape),
        out_shape=out_shape,
        scratch_shapes=scratch,
        compiler_params=pltpu.CompilerParams(vmem_limit_bytes=56 * 2**20),
        cost_estimate=pl.CostEstimate(flops=flops, bytes_accessed=8 * 2**20, transcendentals=0),
        name=name,
    )


def local(inputs, plan, cotangent, w_qkv, w_out, w_fc1, w_fc2, ln_gains, biases, qv_bias, fc1_bias):
    n = lax.axis_size("dp")
    me = lax.axis_index("dp")
    tensor = lax.axis_index("tensor")
    first = lax.axis_index("section") == 0
    frames = inputs.shape[1] // 2
    features = inputs.shape[2]
    width = w_qkv.shape[3]
    units = w_fc1.shape[2]
    heads = MASKS * width // HD
    part = features // n
    slot, half = tensor // 2, tensor % 2
    me_arr = jnp.reshape(me, (1,)).astype(jnp.int32)
    relative = jnp.arange(MASKS) ^ tensor

    shard_a = jnp.concatenate([w_qkv[0, 0], w_qkv[0, 1], w_qkv[0, 2], w_out[0].T], axis=1)
    shard_1 = w_fc1[0]
    shard_2 = w_fc2[0].T
    pa = gather_pieces(shard_a)
    p1 = gather_pieces(shard_1)
    p2 = gather_pieces(shard_2)

    qv_flat = qv_bias[0].reshape(1, -1)
    small = jnp.concatenate(
        [
            ln_gains[0],
            biases[0],
            fc1_bias[0],
            jnp.pad(qv_flat, ((0, 0), (0, part - qv_flat.shape[1]))),
        ],
        axis=0,
    )
    small = lax.all_gather(small, ("dp", "tensor"))
    small = small.reshape(n, MASKS, 8, part).astype(F32)
    vec = small[:, 0, :6].transpose(1, 0, 2).reshape(6, features)
    vec = jnp.concatenate([vec, jnp.zeros((2, features), F32)], axis=0)
    fb = small[:, :, 6].transpose(1, 0, 2).reshape(MASKS, units)
    qv = small[:, :, 7, : 2 * (width // n)].reshape(n, MASKS, 2, width // n)
    qv = qv.transpose(1, 2, 0, 3).reshape(MASKS, 2, width)
    qkvb = jnp.concatenate([qv[:, 0], jnp.zeros((MASKS, width), F32), qv[:, 1]], axis=1)
    fb = fb[relative]
    qkvb = qkvb[relative]

    w_scratch = pltpu.VMEM((MASKS, features, features), BF16)
    w_sems = pltpu.SemaphoreType.DMA((MASKS * n,))
    many = [ANY] * (MASKS * n)
    act = shape((frames, features), BF16)
    wide = shape((frames, units), BF16)

    def forward(x, keep):
        normed, q, kv = call(
            functools.partial(qkv_kernel, n),
            [SMEM, VMEM, VMEM, VMEM] + many,
            (act, shape((MASKS, frames, width), BF16), shape((MASKS, frames, 2 * width), BF16)),
            [w_scratch, w_sems],
            2 * frames * features * features * 3,
            "qkv",
        )(me_arr, x, vec, qkvb, *pa)
        kv_peer = flip(kv, 1)
        outs = [shape((frames, features), F32), act]
        if keep:
            outs += [shape((frames, width), BF16)] * MASKS
            outs += [shape((heads, frames, 2 * frames), BF16)]
        r, c, *kept = call(
            functools.partial(attend_kernel, n, keep),
            [SMEM] + [VMEM] * 5 + many,
            tuple(outs),
            [pltpu.VMEM((MASKS, 2 * frames, 2 * width), BF16), w_scratch, w_sems],
            2 * frames * features * features + 8 * frames * frames * features * 2,
            "attend",
        )(me_arr, x, vec, q, kv, kv_peer, *pa)
        outs = [act]
        if keep:
            outs += [wide] * MASKS + [shape((MASKS, frames, units), BF16)]
        y, *kept2 = call(
            functools.partial(hidden_kernel, n, keep),
            [SMEM] + [VMEM] * 4 + many * 2,
            tuple(outs),
            [w_scratch, w_scratch, w_sems, w_sems],
            4 * frames * features * units * MASKS,
            "hidden",
        )(me_arr, r, c, vec, fb, *p1, *p2)
        if not keep:
            return y, None
        return y, dict(
            x=x, normed=normed, q=q, kv=kv, kv_peer=kv_peer, r=r, c=c, o=kept[:4], p=kept[4], e=kept2[:4], g=kept2[4]
        )

    def backward(dy, s):
        *du, dr, da, do, sums, fsums = call(
            functools.partial(hidden_back_kernel, n),
            [SMEM] + [VMEM] * 4 + many * 3,
            (wide,) * MASKS
            + (
                shape((frames, features), F32),
                act,
                shape((MASKS, frames, width), BF16),
                shape((8, features), F32),
                shape((MASKS, units), F32),
            ),
            [w_scratch, w_scratch, w_scratch, w_sems, w_sems, w_sems],
            4 * frames * features * units * MASKS + 2 * frames * features * features,
            "hidden_back",
        )(me_arr, dy, s["r"], vec, s["g"], *p2, *p1, *pa)
        dq, own, peer = call(
            attend_back_kernel,
            [VMEM] * 5,
            (
                shape((MASKS, frames, width), BF16),
                shape((MASKS, frames, 2 * width), F32),
                shape((MASKS, frames, 2 * width), BF16),
            ),
            [pltpu.VMEM((MASKS, 2 * frames, 2 * width), BF16)],
            16 * frames * frames * features * 2,
            "attend_back",
        )(do, s["q"], s["kv"], s["kv_peer"], s["p"])
        recv = flip(peer, 1)
        dx, *rest = call(
            functools.partial(input_back_kernel, n),
            [SMEM] + [VMEM] * 6 + many,
            (act,)
            + (shape((frames, 3 * width), BF16),) * MASKS
            + (shape((8, features), F32), shape((MASKS, 3 * width), F32)),
            [w_scratch, w_sems],
            6 * frames * features * features,
            "input_back",
        )(me_arr, s["x"], dr, vec, dq, own, recv, *pa)
        dqkv, sums_one, qsums = rest[:4], rest[4], rest[5]
        return dx, dict(du=du, da=da, dqkv=dqkv, sums=sums, fsums=fsums, sums_one=sums_one, qsums=qsums)

    def weight_grad(left, right):
        cols = right[0].shape[1]
        blocks = call(
            functools.partial(weight_kernel, n),
            [VMEM] * (2 * MASKS),
            shape((n, part, cols), BF16),
            [],
            2 * MASKS * frames * features * cols,
            "weight_grad",
        )(*left, *right)
        return ring_scatter(blocks, me)

    x_clip = lax.dynamic_slice(inputs, (plan[0, slot], half * frames, 0), (1, frames, features))[0]
    out_grad = lax.dynamic_slice(cotangent, (slot, half * frames, 0), (1, frames, features))[0]
    mid, _ = forward(x_clip, False)
    relayed = lax.ppermute(mid, "section", [(0, 1)])
    x = jnp.where(first, x_clip, relayed)
    y, kept = forward(x, True)
    hidden_states = lax.all_gather(y, "tensor", axis=0, tiled=True)
    hidden_states = hidden_states.reshape(inputs.shape)[None]

    dx, _ = backward(out_grad, kept)
    relayed = lax.ppermute(dx, "section", [(1, 0)])
    dy = jnp.where(first, relayed, out_grad)
    normed_all = spread(kept["normed"])
    c_all = spread(kept["c"])
    o_all = trade(kept["o"])
    e_all = trade(kept["e"])
    dx, b = backward(dy, kept)

    dm_all = spread(dy)
    grad_2 = weight_grad(dm_all, e_all)
    grad_1 = weight_grad(c_all, trade(b["du"]))
    da_all = spread(b["da"])
    grad_o = weight_grad(da_all, o_all)
    grad_a = weight_grad(normed_all, trade(b["dqkv"]))

    grad_inputs = lax.all_gather(dx, "tensor", axis=0, tiled=True)
    grad_inputs = grad_inputs.reshape(inputs.shape).astype(F32)[None]

    qs = b["qsums"][relative]
    flat = jnp.concatenate(
        [
            b["sums_one"][:2],
            b["sums"][:4],
            b["fsums"][relative],
            qs[:, :width].reshape(1, features),
            qs[:, 2 * width :].reshape(1, features),
        ],
        axis=0,
    )
    flat = total(flat)
    rows = lax.dynamic_slice(flat[:6], (0, me * part), (6, part))
    grad_gains = jnp.stack([rows[0], rows[3]])[None]
    grad_biases = jnp.stack([rows[1], rows[4], rows[5], rows[2]])[None]
    grad_fb = lax.dynamic_slice(flat, (6 + tensor, me * part), (1, part))[None]
    grad_qv = lax.dynamic_slice(flat, (10, tensor * width + me * (width // n)), (2, width // n))
    grad_qv = grad_qv[None, :, None, :]

    grad_qkv = jnp.stack([grad_a[:, i * width : (i + 1) * width] for i in range(3)])[None]
    return (
        hidden_states,
        grad_inputs,
        grad_qkv,
        grad_o.T[None],
        grad_1[None],
        grad_2.T[None],
        grad_gains,
        grad_biases,
        grad_qv,
        grad_fb,
    )


def solution(mesh):
    placed = (
        P("dp", None, None),
        P("dp", None),
        P("dp", None, None),
        P("section", None, "dp", "tensor"),
        P("section", "tensor", "dp"),
        P("section", "dp", "tensor"),
        P("section", "tensor", "dp"),
        P("section", None, "dp"),
        P("section", None, "dp"),
        P("section", None, "tensor", "dp"),
        P("section", "tensor", "dp"),
    )
    return jax.shard_map(
        local,
        mesh=mesh,
        in_specs=placed,
        out_specs=(P("section", "dp", None, None), P("section", "dp", None, None)) + placed[3:],
        check_vma=False,
    )
```

time: 1130 us -> 465 us (0.41)
  waiting for transfers between devices: 692 us -> 172 us
  Pallas kernels: 0 us -> 148 us
  matrix products: 142 us -> 0 us
  blocking collectives: 98.8 us -> 21.9 us
  local copies, waits for them, and re-layouts: 87 us -> 28 us
  other arithmetic: 70.7 us -> 22.6 us
  starting transfers between devices: 12.5 us -> 48.4 us
    psum x9 -> x0, waiting for transfers between devices: 462 us -> none  [the longest x6 327 us: forward_total(): return lax.psum(partial_value, 'tensor')]
    pallas_call x0 -> x16, Pallas kernels: none -> 148 us  [the longest x2 27.1 us: backward(): call(functools.partial(hidden_back_kernel, n), [SMEM] + [VMEM] * 4 + many...]
    dot_general x54 -> x0, matrix products: 139 us -> none  [the longest x3 21.2 us: layer_backward(): jnp.einsum('fd,ad->fa', upstream_low, w_fc2, preferred_element_type=jnp.f...]
    unnamed x26 -> x2, waiting for transfers between devices: 105 us -> 0.03 us
    ppermute x4 -> x91, waiting for transfers between devices: 74.4 us -> 172 us  [the longest x21 87.5 us: ring_next(): lax.ppermute(value, 'dp', [(i, (i + 1) % count) for i in range(count)])]
    all_gather x5 -> x1, blocking collectives: 88.1 us -> 21.9 us  [local(): small = lax.all_gather(small, ('dp', 'tensor'))]
    reduce_scatter x1 -> x0, waiting for transfers between devices: 47.4 us -> none  [local(): lax.psum_scatter(totals[2][None], 'dp', scatter_dimension=1, tiled=True)]
    unnamed x441 -> x139, local copies, waits for them, and re-layouts: 50.7 us -> 7.88 us
  transfers between devices with their start and end apart: 23 -> 93, of which waited for: 17 -> 33; matrix products, arithmetic and copies ran while one was open for 12% -> 8% of each run, Pallas kernels for 0% -> 18%
where the time goes in v1:
time: 465 us; the launch traced here: 458 us
  waiting for transfers between devices  172 us (37%)
  Pallas kernels  148 us (32%)
  starting transfers between devices  48.4 us (10%)
  local copies, waits for them, and re-layouts  28 us (6%)
  other arithmetic  22.6 us (5%)
  blocking collectives  21.9 us (5%)
  between operations  17.3 us (4%)
    ppermute x21, waiting for transfers between devices, ring_next(): lax.ppermute(value, 'dp', [(i, (i + 1) % count) for i in range(count)])  87.5 us
    ppermute x66, waiting for transfers between devices, flip(): return lax.ppermute(value, 'tensor', [(i, i ^ mask) for i in range(count)])  52.8 us
    ppermute x66, starting transfers between devices, flip(): return lax.ppermute(value, 'tensor', [(i, i ^ mask) for i in range(count)])  27.7 us
    pallas_call x2, Pallas kernels, backward(): call(functools.partial(hidden_back_kernel, n), [SMEM] + [VMEM] * 4 + many...  27.1 us
    pallas_call x2, Pallas kernels, backward(): call(attend_back_kernel, [VMEM] * 5, (shape((MASKS, frames, width), BF16)...  26.7 us
    pallas_call x2, Pallas kernels, forward(): call(functools.partial(attend_kernel, n, keep), [SMEM] + [VMEM] * 5 + man...  25.3 us
    all_gather x1, blocking collectives, local(): small = lax.all_gather(small, ('dp', 'tensor'))  21.9 us
    pallas_call x4, Pallas kernels, weight_grad(): call(functools.partial(weight_kernel, n), [VMEM] * (2 * MASKS), shape((n,...  20.5 us
  transfers between devices with their start and end apart: 93, of which 33 were waited for; matrix products, arithmetic and copies ran while one was open for 8% of the time, Pallas kernels for 18%

profile of v1, /device:TPU:0, one launch (start us, length us, event | category | flops | bytes accessed | tf_op | source)
XLA Modules:
  0.0 458.0 jit_solution(7555040240697676987)
XLA Ops:
  28.8 6.3 %collective-permute-done.34.refs_20_.refs_4_ = bf16[192,768]{1,0:T(8,128)(2,1)} collective-permute-done((bf16[192,768]{1,0:T(8,128)(2,1)}, bf16[192,768]{1,0:T(8,128)(2,1)}, u32[]{:S(2)}, u32[]{:S(2)}) %collective-permute-start.34) | collective-permute-done | bytes 294944 | tf_op jit(solution)/shard_map/ppermute | solution.py:27
  44.0 21.9 %all-gather = bf16[128,192]{1,0:T(8,128)(2,1)S(1)} all-gather(bf16[8,192]{1,0:T(8,128)(2,1)S(1)} %fusion.12), channel_id=2, replica_groups=mesh['section'=2,'dp'=4,'tensor'=4] {'dp','tensor'}, dimensions={0}, use_global_device_ids=true | all-gather | bytes 52224 | tf_op jit(solution)/shard_map/all_gather | solution.py:355
  71.0 9.0 %collective-permute-done.23.refs_8_.refs_24_ = bf16[192,768]{1,0:T(8,128)(2,1)S(1)} collective-permute-done((bf16[192,768]{1,0:T(8,128)(2,1)}, bf16[192,768]{1,0:T(8,128)(2,1)S(1)}, u32[]{:S(2)}, u32[]{:S(2)}) %collective-permute-start.23) | collective-permute-done | bytes 294944 | tf_op jit(solution)/shard_map/ppermute | solution.py:27
  92.2 6.5 %qkv.2 = (bf16[320,768]{1,0:T(8,128)(2,1)}, bf16[4,320,192]{2,1,0:T(8,128)(2,1)}, bf16[4,320,384]{2,1,0:T(8,128)(2,1)}) custom-call(s32[1]{0:T(128)} %bitcast.me_ref, bf16[320,768]{1,0:T(8,128)(2,1)} %dynamic-slice_bitcast_fusion.1.x_ref, f32[8,768]{1,0:T(8,128)} %concatenate.16.vec_ref, f32[4,576]{1,0:T(4,128)} %gather_fusion, bf16[192,768]{1,0:T(8,128)(2,1)} %copy-done.2, ...), custom_call_target="tpu_custom_call" | custom-call | flops 1132462080 | bytes 8388608 | tf_op jit(solution)/shard_map/qkv/pallas_call | solution.py:373
  106.7 7.4 %collective-permute-done.27.refs_12_.refs_28_ = bf16[192,768]{1,0:T(8,128)(2,1)S(1)} collective-permute-done((bf16[192,768]{1,0:T(8,128)(2,1)S(1)}, bf16[192,768]{1,0:T(8,128)(2,1)S(1)}, u32[]{:S(2)}, u32[]{:S(2)}) %collective-permute-start.27) | collective-permute-done | bytes 294944 | tf_op jit(solution)/shard_map/ppermute | solution.py:27
  123.3 7.1 %collective-permute-done.29.refs_14_.refs_30_ = bf16[192,768]{1,0:T(8,128)(2,1)S(1)} collective-permute-done((bf16[192,768]{1,0:T(8,128)(2,1)S(1)}, bf16[192,768]{1,0:T(8,128)(2,1)S(1)}, u32[]{:S(2)}, u32[]{:S(2)}) %collective-permute-start.29) | collective-permute-done | bytes 294944 | tf_op jit(solution)/shard_map/ppermute | solution.py:22
  140.4 11.9 %attend.2 = (f32[320,768]{1,0:T(8,128)}, bf16[320,768]{1,0:T(8,128)(2,1)}) custom-call(s32[1]{0:T(128)} %bitcast.me_ref, bf16[320,768]{1,0:T(8,128)(2,1)} %dynamic-slice_bitcast_fusion.1.x_ref, f32[8,768]{1,0:T(8,128)} %concatenate.16.vec_ref, bf16[4,320,192]{2,1,0:T(8,128)(2,1)} %get-tuple-element.55.q_ref, ...), custom_call_target="tpu_custom_call" | custom-call | flops 1635778560 | bytes 8388608 | tf_op jit(solution)/shard_map/attend/pallas_call | solution.py:386
  152.5 9.7 %hidden.2 = bf16[320,768]{1,0:T(8,128)(2,1)} custom-call(s32[1]{0:T(128)} %bitcast.me_ref, f32[320,768]{1,0:T(8,128)} %get-tuple-element.57.r_ref, bf16[320,768]{1,0:T(8,128)(2,1)} %get-tuple-element.58.c_ref, f32[8,768]{1,0:T(8,128)} %concatenate.16.vec_ref, f32[4,768]{1,0:T(4,128)} %gather_fusion.1, bf16[192,768]{1,0:T(8,128)(2,1)} %bitcast.129, ...), custom_call_target="tpu_custom_call" | custom-call | flops 3019898880 | bytes 8388608 | tf_op jit(solution)/shard_map/hidden/pallas_call | solution.py:397
  165.6 11.2 %collective-permute-done.46 = bf16[320,768]{1,0:T(8,128)(2,1)S(1)} collective-permute-done((bf16[320,768]{1,0:T(8,128)(2,1)}, bf16[320,768]{1,0:T(8,128)(2,1)S(1)}, u32[]{:S(2)}, u32[]{:S(2)}) %collective-permute-start.46) | collective-permute-done | bytes 491552 | tf_op jit(solution)/shard_map/ppermute | solution.py:468
  178.8 6.5 %qkv.3 = (bf16[320,768]{1,0:T(8,128)(2,1)}, bf16[4,320,192]{2,1,0:T(8,128)(2,1)}, bf16[4,320,384]{2,1,0:T(8,128)(2,1)}) custom-call(s32[1]{0:T(128)} %bitcast.me_ref, bf16[320,768]{1,0:T(8,128)(2,1)} %broadcast_select_fusion.1.x_ref, f32[8,768]{1,0:T(8,128)} %concatenate.16.vec_ref, f32[4,576]{1,0:T(4,128)} %gather_fusion, bf16[192,768]{1,0:T(8,128)(2,1)} %copy-done.2, ...), custom_call_target="tpu_custom_call" | custom-call | flops 1132462080 | bytes 8388608 | tf_op jit(solution)/shard_map/qkv/pallas_call | solution.py:373
  189.2 13.4 %attend.3 = (f32[320,768]{1,0:T(8,128)}, bf16[320,768]{1,0:T(8,128)(2,1)}, bf16[320,192]{1,0:T(8,128)(2,1)}, bf16[320,192]{1,0:T(8,128)(2,1)}, bf16[320,192]{1,0...) custom-call(s32[1]{0:T(128)} %bitcast.me_ref, bf16[320,768]{1,0:T(8,128)(2,1)} %broadcast_select_fusion.1.x_ref, ...), custom_call_target="tpu_custom_call" | custom-call | flops 1635778560 | bytes 8388608 | tf_op jit(solution)/shard_map/attend/pallas_call | solution.py:386
  202.6 10.5 %hidden.3 = (bf16[320,768]{1,0:T(8,128)(2,1)}, bf16[320,768]{1,0:T(8,128)(2,1)}, bf16[320,768]{1,0:T(8,128)(2,1)}, bf16[320,768]{1,0:T(8,128)(2,1)}, bf16[320,76...) custom-call(s32[1]{0:T(128)} %bitcast.me_ref, f32[320,768]{1,0:T(8,128)} %get-tuple-element.61.r_ref, ...), custom_call_target="tpu_custom_call" | custom-call | flops 3019898880 | bytes 8388608 | tf_op jit(solution)/shard_map/hidden/pallas_call | solution.py:397
  213.1 13.6 %hidden_back.2 = (bf16[320,768]{1,0:T(8,128)(2,1)}, bf16[320,768]{1,0:T(8,128)(2,1)}, bf16[320,768]{1,0:T(8,128)(2,1)}, bf16[320,768]{1,0:T(8,128)(2,1)}, f32[32...) custom-call(s32[1]{0:T(128)} %bitcast.me_ref, ...), custom_call_target="tpu_custom_call" | custom-call | flops 3397386240 | bytes 8388608 | tf_op jit(solution)/shard_map/hidden_back/pallas_call | solution.py:412
  226.7 13.4 %attend_back.2 = (bf16[4,320,192]{2,1,0:T(8,128)(2,1)}, f32[4,320,384]{2,1,0:T(8,128)}, bf16[4,320,384]{2,1,0:T(8,128)(2,1)}) custom-call(bf16[4,320,192]{2,1,0:T(8,128)(2,1)} %get-tuple-element.66.do_ref, bf16[4,320,192]{2,1,0:T(8,128)(2,1)} %get-tuple-element.59.q_ref, bf16[4,320,384]{2,1,0:T(8,128)(2,1)} %get-tuple-element.60.kv_own_ref, ...), custom_call_target="tpu_custom_call" | custom-call | flops 2516582400 | bytes 8388608 | tf_op jit(solution)/shard_map/attend_back/pallas_call | solution.py:427
  243.9 7.6 %input_back.2 = (bf16[320,768]{1,0:T(8,128)(2,1)}, bf16[320,576]{1,0:T(8,128)(2,1)}, bf16[320,576]{1,0:T(8,128)(2,1)}, bf16[320,576]{1,0:T(8,128)(2,1)}, bf16[32...) custom-call(s32[1]{0:T(128)} %bitcast.me_ref, bf16[320,768]{1,0:T(8,128)(2,1)} %broadcast_select_fusion.1.x_ref, ...), custom_call_target="tpu_custom_call" | custom-call | flops 1132462080 | bytes 8388608 | tf_op jit(solution)/shard_map/input_back/pallas_call | solution.py:440
  255.5 11.4 %collective-permute-done.49 = bf16[320,768]{1,0:T(8,128)(2,1)S(1)} collective-permute-done((bf16[320,768]{1,0:T(8,128)(2,1)}, bf16[320,768]{1,0:T(8,128)(2,1)S(1)}, u32[]{:S(2)}, u32[]{:S(2)}) %collective-permute-start.49) | collective-permute-done | bytes 491552 | tf_op jit(solution)/shard_map/ppermute | solution.py:475
  267.8 13.6 %hidden_back.3 = (bf16[320,768]{1,0:T(8,128)(2,1)}, bf16[320,768]{1,0:T(8,128)(2,1)}, bf16[320,768]{1,0:T(8,128)(2,1)}, bf16[320,768]{1,0:T(8,128)(2,1)}, f32[32...) custom-call(s32[1]{0:T(128)} %bitcast.me_ref, ...), custom_call_target="tpu_custom_call" | custom-call | flops 3397386240 | bytes 8388608 | tf_op jit(solution)/shard_map/hidden_back/pallas_call | solution.py:412
  284.1 13.3 %attend_back.3 = (bf16[4,320,192]{2,1,0:T(8,128)(2,1)}, f32[4,320,384]{2,1,0:T(8,128)}, bf16[4,320,384]{2,1,0:T(8,128)(2,1)}) custom-call(bf16[4,320,192]{2,1,0:T(8,128)(2,1)} %get-tuple-element.73.do_ref, bf16[4,320,192]{2,1,0:T(8,128)(2,1)} %get-tuple-element.59.q_ref, bf16[4,320,384]{2,1,0:T(8,128)(2,1)} %get-tuple-element.60.kv_own_ref, ...), custom_call_target="tpu_custom_call" | custom-call | flops 2516582400 | bytes 8388608 | tf_op jit(solution)/shard_map/attend_back/pallas_call | solution.py:427
  306.7 10.6 %collective-permute-done.61.refs_2_ = bf16[320,768]{1,0:T(8,128)(2,1)S(1)} collective-permute-done((bf16[320,768]{1,0:T(8,128)(2,1)}, bf16[320,768]{1,0:T(8,128)(2,1)S(1)}, u32[]{:S(2)}, u32[]{:S(2)}) %collective-permute-start.61) | collective-permute-done | bytes 491552 | tf_op jit(solution)/shard_map/ppermute | solution.py:22
  343.3 7.6 %input_back.3 = (bf16[320,768]{1,0:T(8,128)(2,1)}, bf16[320,576]{1,0:T(8,128)(2,1)}, bf16[320,576]{1,0:T(8,128)(2,1)}, bf16[320,576]{1,0:T(8,128)(2,1)}, bf16[32...) custom-call(s32[1]{0:T(128)} %bitcast.me_ref, bf16[320,768]{1,0:T(8,128)(2,1)} %broadcast_select_fusion.1.x_ref, ...), custom_call_target="tpu_custom_call" | custom-call | flops 1132462080 | bytes 8388608 | tf_op jit(solution)/shard_map/input_back/pallas_call | solution.py:440
  370.6 7.0 %collective-permute-done.89 = f32[12,768]{1,0:T(8,128)S(1)} collective-permute-done((f32[12,768]{1,0:T(8,128)S(1)}, f32[12,768]{1,0:T(8,128)S(1)}, u32[]{:S(2)}, u32[]{:S(2)}) %collective-permute-start.89) | collective-permute-done | bytes 36896 | tf_op jit(solution)/shard_map/ppermute | solution.py:68
  414.8 7.2 %collective-permute-done.57 = bf16[192,576]{1,0:T(8,128)(2,1)S(1)} collective-permute-done((bf16[192,576]{1,0:T(8,128)(2,1)S(1)}, bf16[192,576]{1,0:T(8,128)(2,1)S(1)}, u32[]{:S(2)}, u32[]{:S(2)}) %collective-permute-start.57) | collective-permute-done | bytes 221216 | tf_op jit(solution)/shard_map/ppermute | solution.py:27
  424.6 8.8 %collective-permute-done.58 = bf16[192,576]{1,0:T(8,128)(2,1)} collective-permute-done((bf16[192,576]{1,0:T(8,128)(2,1)}, bf16[192,576]{1,0:T(8,128)(2,1)}, u32[]{:S(2)}, u32[]{:S(2)}) %collective-permute-start.58) | collective-permute-done | bytes 221216 | tf_op jit(solution)/shard_map/ppermute | solution.py:27
  436.4 8.3 %collective-permute-done.59 = bf16[192,576]{1,0:T(8,128)(2,1)S(1)} collective-permute-done((bf16[192,576]{1,0:T(8,128)(2,1)S(1)}, bf16[192,576]{1,0:T(8,128)(2,1)S(1)}, u32[]{:S(2)}, u32[]{:S(2)}) %collective-permute-start.59) | collective-permute-done | bytes 221216 | tf_op jit(solution)/shard_map/ppermute | solution.py:27
  (384 shorter events, 196.7 us)
Async XLA Ops:
  7.2 417.4 %all-gather.4.cloned.1.call-start = ((), (), s32[]{:S(2)}) async-start(), calls=%async_computation | async-start | bytes 2457600 | tf_op jit(solution)/shard_map/all_gather | solution.py:471
  35.1 33.1 %collective-permute-start.31 = (bf16[192,768]{1,0:T(8,128)(2,1)}, bf16[192,768]{1,0:T(8,128)(2,1)S(1)}, u32[]{:S(2)}, u32[]{:S(2)}) collective-permute-start(bf16[192,768]{1,0:T(8,128)(2,1)} %bitcast.135), channel_id=1, source_target_pairs={{0,1},{1,0},{2,3},{3,2},{4,5},{5,4},{6,7},{7,6},{8,9},{9,8},{10,11... | collective-permute-start | bytes 884744 | tf_op jit(solution)/shard_map/ppermute | solution.py:22
  35.1 33.1 %collective-permute-start.5 = (bf16[192,768]{1,0:T(8,128)(2,1)S(1)}, bf16[192,768]{1,0:T(8,128)(2,1)S(1)}, u32[]{:S(2)}, u32[]{:S(2)}) collective-permute-start(bf16[192,768]{1,0:T(8,128)(2,1)S(1)} %collective-permute-done.3.refs_4_.refs_36_), channel_id=1, source_target_pairs={{0,2},{1,3},{2,0},{3,1},{4,6},{5,7},{6,4},{7,5},{8,10},{9,11},{10,... | collective-permute-start | bytes 884744 | tf_op jit(solution)/shard_map/ppermute | solution.py:22
  36.9 32.0 %collective-permute-start.4 = (bf16[192,768]{1,0:T(8,128)(2,1)S(1)}, bf16[192,768]{1,0:T(8,128)(2,1)S(1)}, u32[]{:S(2)}, u32[]{:S(2)}) collective-permute-start(bf16[192,768]{1,0:T(8,128)(2,1)S(1)} %collective-permute-done.3.refs_4_.refs_36_), channel_id=1, source_target_pairs={{0,1},{1,0},{2,3},{3,2},{4,5},{5,4},{6,7},{7,6},{8,9},{9,8},{10,11... | collective-permute-start | bytes 884744 | tf_op jit(solution)/shard_map/ppermute | solution.py:22
  40.5 28.5 %collective-permute-start.11 = (bf16[192,768]{1,0:T(8,128)(2,1)S(1)}, bf16[192,768]{1,0:T(8,128)(2,1)S(1)}, u32[]{:S(2)}, u32[]{:S(2)}) collective-permute-start(bf16[192,768]{1,0:T(8,128)(2,1)S(1)} %collective-permute-done.7.refs_8_.refs_40_), channel_id=1, source_target_pairs={{0,4},{4,8},{8,12},{12,0},{1,5},{5,9},{9,13},{13,1},{2,6},{6,10},{... | collective-permute-start | bytes 884744 | tf_op jit(solution)/shard_map/ppermute | solution.py:27
  41.3 29.6 %collective-permute-start.2 = (bf16[192,768]{1,0:T(8,128)(2,1)S(1)}, bf16[192,768]{1,0:T(8,128)(2,1)S(1)}, u32[]{:S(2)}, u32[]{:S(2)}) collective-permute-start(bf16[192,768]{1,0:T(8,128)(2,1)S(1)} %collective-permute-done.1.refs_2_.refs_34_), channel_id=1, source_target_pairs={{0,1},{1,0},{2,3},{3,2},{4,5},{5,4},{6,7},{7,6},{8,9},{9,8},{10,11... | collective-permute-start | bytes 884744 | tf_op jit(solution)/shard_map/ppermute | solution.py:22
  98.7 38.1 %collective-permute-start.15 = (bf16[4,320,384]{2,1,0:T(8,128)(2,1)}, bf16[4,320,384]{2,1,0:T(8,128)(2,1)S(1)}, u32[]{:S(2)}, u32[]{:S(2)}) collective-permute-start(bf16[4,320,384]{2,1,0:T(8,128)(2,1)} %get-tuple-element.56.kv_own_ref), channel_id=1, source_target_pairs={{0,1},{1,0},{2,3},{3,2},{4,5},{5,4},{6,7},{7,6},{8,9},{9,8},{10,11... | collective-permute-start | bytes 2949128 | tf_op jit(solution)/shard_map/ppermute | solution.py:22
  122.7 29.7 %collective-permute-start.43 = (bf16[192,768]{1,0:T(8,128)(2,1)S(1)}, bf16[192,768]{1,0:T(8,128)(2,1)}, u32[]{:S(2)}, u32[]{:S(2)}) collective-permute-start(bf16[192,768]{1,0:T(8,128)(2,1)S(1)} %collective-permute-done.42.refs_28_.refs_12_), channel_id=1, source_target_pairs={{0,1},{1,0},{2,3},{3,2},{4,5},{5,4},{6,7},{7,6},{8,9},{9,8},{10,11... | collective-permute-start | bytes 884744 | tf_op jit(solution)/shard_map/ppermute | solution.py:22
  252.8 192.9 %all-gather.6.cloned.1.call-start = ((), (), s32[]{:S(2)}) async-start(), calls=%async_computation.1 | async-start | bytes 2457600 | tf_op jit(solution)/shard_map/all_gather | solution.py:490
  252.9 28.5 %collective-permute-start.52 = (bf16[320,768]{1,0:T(8,128)(2,1)S(1)}, bf16[320,768]{1,0:T(8,128)(2,1)}, u32[]{:S(2)}, u32[]{:S(2)}) collective-permute-start(bf16[320,768]{1,0:T(8,128)(2,1)S(1)} %copy-done.50), channel_id=1, source_target_pairs={{0,2},{1,3},{2,0},{3,1},{4,6},{5,7},{6,4},{7,5},{8,10},{9,11},{10,... | collective-permute-start | bytes 1474568 | tf_op jit(solution)/shard_map/ppermute | solution.py:22
  253.2 30.2 %collective-permute-start.69 = (bf16[320,768]{1,0:T(8,128)(2,1)}, bf16[320,768]{1,0:T(8,128)(2,1)S(1)}, u32[]{:S(2)}, u32[]{:S(2)}) collective-permute-start(bf16[320,768]{1,0:T(8,128)(2,1)} %get-tuple-element.62.c_ref.refs_0_), channel_id=1, source_target_pairs={{0,1},{1,0},{2,3},{3,2},{4,5},{5,4},{6,7},{7,6},{8,9},{9,8},{10,11... | collective-permute-start | bytes 1474568 | tf_op jit(solution)/shard_map/ppermute | solution.py:22
  253.2 28.7 %collective-permute-start.63 = (bf16[320,192]{1,0:T(8,128)(2,1)}, bf16[320,192]{1,0:T(8,128)(2,1)S(1)}, u32[]{:S(2)}, u32[]{:S(2)}) collective-permute-start(bf16[320,192]{1,0:T(8,128)(2,1)} %get-tuple-element.85), channel_id=1, source_target_pairs={{0,1},{1,0},{2,3},{3,2},{4,5},{5,4},{6,7},{7,6},{8,9},{9,8},{10,11... | collective-permute-start | bytes 368648 | tf_op jit(solution)/shard_map/ppermute | solution.py:22
  254.1 28.2 %collective-permute-start.64 = (bf16[320,192]{1,0:T(8,128)(2,1)S(1)}, bf16[320,192]{1,0:T(8,128)(2,1)S(1)}, u32[]{:S(2)}, u32[]{:S(2)}) collective-permute-start(bf16[320,192]{1,0:T(8,128)(2,1)S(1)} %copy-done.66), channel_id=1, source_target_pairs={{0,2},{1,3},{2,0},{3,1},{4,6},{5,7},{6,4},{7,5},{8,10},{9,11},{10,... | collective-permute-start | bytes 368648 | tf_op jit(solution)/shard_map/ppermute | solution.py:22
  266.9 30.5 %collective-permute-start.71 = (bf16[320,768]{1,0:T(8,128)(2,1)}, bf16[320,768]{1,0:T(8,128)(2,1)S(1)}, u32[]{:S(2)}, u32[]{:S(2)}) collective-permute-start(bf16[320,768]{1,0:T(8,128)(2,1)} %collective-permute-done.70.refs_2_), channel_id=1, source_target_pairs={{0,1},{1,0},{2,3},{3,2},{4,5},{5,4},{6,7},{7,6},{8,9},{9,8},{10,11... | collective-permute-start | bytes 1474568 | tf_op jit(solution)/shard_map/ppermute | solution.py:22
  283.4 33.9 %collective-permute-start.61 = (bf16[320,768]{1,0:T(8,128)(2,1)}, bf16[320,768]{1,0:T(8,128)(2,1)S(1)}, u32[]{:S(2)}, u32[]{:S(2)}) collective-permute-start(bf16[320,768]{1,0:T(8,128)(2,1)} %get-tuple-element.83.refs_0_), channel_id=1, source_target_pairs={{0,2},{1,3},{2,0},{3,1},{4,6},{5,7},{6,4},{7,5},{8,10},{9,11},{10,... | collective-permute-start | bytes 1474568 | tf_op jit(solution)/shard_map/ppermute | solution.py:22
  298.2 38.5 %collective-permute-start.50 = (bf16[4,320,384]{2,1,0:T(8,128)(2,1)}, bf16[4,320,384]{2,1,0:T(8,128)(2,1)S(1)}, u32[]{:S(2)}, u32[]{:S(2)}) collective-permute-start(bf16[4,320,384]{2,1,0:T(8,128)(2,1)} %get-tuple-element.76), channel_id=1, source_target_pairs={{0,1},{1,0},{2,3},{3,2},{4,5},{5,4},{6,7},{7,6},{8,9},{9,8},{10,11... | collective-permute-start | bytes 2949128 | tf_op jit(solution)/shard_map/ppermute | solution.py:22
  298.3 26.6 %collective-permute-start.65 = (bf16[320,192]{1,0:T(8,128)(2,1)}, bf16[320,192]{1,0:T(8,128)(2,1)}, u32[]{:S(2)}, u32[]{:S(2)}) collective-permute-start(bf16[320,192]{1,0:T(8,128)(2,1)} %get-tuple-element.87), channel_id=1, source_target_pairs={{0,3},{1,2},{2,1},{3,0},{4,7},{5,6},{6,5},{7,4},{8,11},{9,10},{10,... | collective-permute-start | bytes 368648 | tf_op jit(solution)/shard_map/ppermute | solution.py:22
  299.7 30.9 %collective-permute-start.79 = (bf16[320,768]{1,0:T(8,128)(2,1)S(1)}, bf16[320,768]{1,0:T(8,128)(2,1)}, u32[]{:S(2)}, u32[]{:S(2)}) collective-permute-start(bf16[320,768]{1,0:T(8,128)(2,1)S(1)} %copy-done.40), channel_id=1, source_target_pairs={{0,2},{1,3},{2,0},{3,1},{4,6},{5,7},{6,4},{7,5},{8,10},{9,11},{10,... | collective-permute-start | bytes 1474568 | tf_op jit(solution)/shard_map/ppermute | solution.py:22
  305.2 25.4 %collective-permute-start.60 = (bf16[320,768]{1,0:T(8,128)(2,1)S(1)}, bf16[320,768]{1,0:T(8,128)(2,1)S(1)}, u32[]{:S(2)}, u32[]{:S(2)}) collective-permute-start(bf16[320,768]{1,0:T(8,128)(2,1)S(1)} %copy-done.52), channel_id=1, source_target_pairs={{0,1},{1,0},{2,3},{3,2},{4,5},{5,4},{6,7},{7,6},{8,9},{9,8},{10,11... | collective-permute-start | bytes 1474568 | tf_op jit(solution)/shard_map/ppermute | solution.py:22
  353.3 37.1 %collective-permute-start.51 = (bf16[320,768]{1,0:T(8,128)(2,1)S(1)}, bf16[320,768]{1,0:T(8,128)(2,1)}, u32[]{:S(2)}, u32[]{:S(2)}) collective-permute-start(bf16[320,768]{1,0:T(8,128)(2,1)S(1)} %copy-done.51), channel_id=1, source_target_pairs={{0,1},{1,0},{2,3},{3,2},{4,5},{5,4},{6,7},{7,6},{8,9},{9,8},{10,11... | collective-permute-start | bytes 1474568 | tf_op jit(solution)/shard_map/ppermute | solution.py:22
  353.5 44.6 %collective-permute-start.53 = (bf16[320,768]{1,0:T(8,128)(2,1)}, bf16[320,768]{1,0:T(8,128)(2,1)}, u32[]{:S(2)}, u32[]{:S(2)}) collective-permute-start(bf16[320,768]{1,0:T(8,128)(2,1)} %collective-permute-done.52.refs_2_), channel_id=1, source_target_pairs={{0,1},{1,0},{2,3},{3,2},{4,5},{5,4},{6,7},{7,6},{8,9},{9,8},{10,11... | collective-permute-start | bytes 1474568 | tf_op jit(solution)/shard_map/ppermute | solution.py:22
  354.6 23.0 %collective-permute-start.76 = (bf16[192,768]{1,0:T(8,128)(2,1)}, bf16[192,768]{1,0:T(8,128)(2,1)}, u32[]{:S(2)}, u32[]{:S(2)}) collective-permute-start(bf16[192,768]{1,0:T(8,128)(2,1)} %fusion.5), channel_id=1, source_target_pairs={{0,4},{4,8},{8,12},{12,0},{1,5},{5,9},{9,13},{13,1},{2,6},{6,10},{... | collective-permute-start | bytes 884744 | tf_op jit(solution)/shard_map/ppermute | solution.py:27
  367.1 23.3 %collective-permute-start.84 = (bf16[192,768]{1,0:T(8,128)(2,1)}, bf16[192,768]{1,0:T(8,128)(2,1)S(1)}, u32[]{:S(2)}, u32[]{:S(2)}) collective-permute-start(bf16[192,768]{1,0:T(8,128)(2,1)} %dynamic-slice_bitcast_fusion.2), channel_id=1, source_target_pairs={{0,4},{4,8},{8,12},{12,0},{1,5},{5,9},{9,13},{13,1},{2,6},{6,10},{... | collective-permute-start | bytes 884744 | tf_op jit(solution)/shard_map/ppermute | solution.py:27
  398.2 25.6 %collective-permute-start.77 = (bf16[192,768]{1,0:T(8,128)(2,1)}, bf16[192,768]{1,0:T(8,128)(2,1)S(1)}, u32[]{:S(2)}, u32[]{:S(2)}) collective-permute-start(bf16[192,768]{1,0:T(8,128)(2,1)} %fusion.4), channel_id=1, source_target_pairs={{0,4},{4,8},{8,12},{12,0},{1,5},{5,9},{9,13},{13,1},{2,6},{6,10},{... | collective-permute-start | bytes 884744 | tf_op jit(solution)/shard_map/ppermute | solution.py:27
  (136 other events, 2115.0 us)
Sparse Core Ops, SparseCore 0:
  253.0 28.7 all-gather.3
  365.2 20.7 all-gather.5

commit v2 on v1

v2 whole, which is shorter than its diff:
```python
import functools

import jax
import jax.numpy as jnp
from jax import lax
from jax.experimental import pallas as pl
from jax.experimental.pallas import tpu as pltpu
from jax.sharding import PartitionSpec as P

HD = 64
EPS = 1e-05
MASKS = 4
COST_SCALE = 1.0
VMEM_MIB = {
    "params": 12,
    "qkv": 16,
    "attend": 22,
    "hidden": 22,
    "layer": 40,
    "both_back": 40,
    "hidden_back": 30,
    "attend_back": 22,
    "input_back": 22,
    "weight_grad": 18,
    "place": 12,
    "norm": 8,
}
COST = {
    "params": 0.5,
    "qkv": 40,
    "attend": 40,
    "hidden": 40,
    "layer": 40,
    "both_back": 40,
    "hidden_back": 40,
    "attend_back": 40,
    "input_back": 1,
    "weight_grad": 0.5,
    "place": 0.5,
    "norm": 1,
}
LOG2E = 1.4426950408889634
START = (0, 0, 1)
F32 = jnp.float32
BF16 = jnp.bfloat16
HBM = pl.BlockSpec(memory_space=pltpu.HBM)
VMEM = pl.BlockSpec(memory_space=pltpu.VMEM)
SMEM = pl.BlockSpec(memory_space=pltpu.SMEM)


def flip(value, mask):
    count = lax.axis_size("tensor")
    return lax.ppermute(value, "tensor", [(i, i ^ mask) for i in range(count)])


def ring_next(value):
    count = lax.axis_size("dp")
    return lax.ppermute(value, "dp", [(i, (i + 1) % count) for i in range(count)])


def after(value, *events):
    if not events:
        return value
    return lax.optimization_barrier((value,) + events)[0]


def flip_core(value):
    return flip(value, 1)


def flip_chip(value):
    return flip(value, 2)


def all_pieces(own, far):
    pieces = [p for a, b in zip(own, far) for p in (a, flip_core(a), b, flip_core(b))]
    return [pltpu.with_memory_space_constraint(piece, pltpu.HBM) for piece in pieces]


def flip_within(value, mask, section):
    count = lax.axis_size("tensor")
    pairs = [(section * count + i, section * count + (i ^ mask)) for i in range(count)]
    return lax.ppermute(value, ("section", "tensor"), pairs)


def dp_flip(value, step):
    count = lax.axis_size("dp")
    return lax.ppermute(value, "dp", [(i, i ^ step) for i in range(count)])


def spread(value):
    across = flip_chip(value)
    return [value, flip_core(value), across, flip_core(across)]


def trade(blocks):
    far = flip_chip(blocks[2])
    return [blocks[0], flip_core(blocks[1]), far, flip_core(far[1])]


def ring_steps(blocks, me):
    count = blocks.shape[0]

    def block(step):
        return lax.dynamic_index_in_dim(blocks, (me - 1 - step) % count, 0, keepdims=False)

    moving = block(0)
    for step in range(1, count):
        moving = yield ring_next(moving.astype(BF16))
        moving = moving.astype(F32) + block(step).astype(F32)
    yield moving


def ring_scatter(blocks, me, events=None):
    events = events or {}
    steps = ring_steps(blocks, me)
    value, received = next(steps), []
    for step in range(1, blocks.shape[0]):
        received.append(value)
        value = steps.send(after(value, *events.get(step, ())))
    return value, received


def put(refs, mask, value):
    if mask < 2:
        refs[mask][...] = value
    else:
        refs[2][mask - 2] = value


class Weights:
    def __init__(self, me, pieces, scratch, sems, start):
        count = len(pieces) // MASKS
        rows = scratch.shape[1] // count
        self.copies = [[] for _ in range(MASKS)]
        for step in range(count):
            owner = lax.rem(me - step + count, count)
            to = pl.ds(pl.multiple_of(owner * rows, 16), rows)
            for mask in range(MASKS):
                at = step * MASKS + mask
                piece = pieces[at].at[pl.ds(start * rows, rows)]
                self.copies[mask].append(pltpu.make_async_copy(piece, scratch.at[mask, to], sems.at[at]))

    def start(self, mask):
        if mask < MASKS:
            for copy in self.copies[mask]:
                copy.start()

    def wait(self, mask):
        wait_all(self.copies[mask])


def wait_all(copies):
    for copy in copies:
        copy.wait()


def dot(a, b):
    return lax.dot_general(a, b, (((1,), (0,)), ((), ())), preferred_element_type=F32)


def dot_nt(a, b):
    return lax.dot_general(a, b, (((1,), (1,)), ((), ())), preferred_element_type=F32)


def dot_tn(a, b):
    return lax.dot_general(a, b, (((0,), (0,)), ((), ())), preferred_element_type=F32)


def norm(x):
    average = jnp.mean(x, axis=-1, keepdims=True)
    centered = x - average
    spread_of = jnp.mean(centered * centered, axis=-1, keepdims=True)
    inv_std = lax.rsqrt(spread_of + EPS)
    return centered * inv_std, inv_std


def norm_kernel(x_ref, vec_ref, out_ref):
    normal, _ = norm(x_ref[...].astype(F32))
    out_ref[...] = (normal * vec_ref[0:1, :] + vec_ref[2:3, :]).astype(BF16)


def norm_pull(upstream, normal, inv_std, gains):
    scaled = upstream * gains
    return inv_std * (
        scaled
        - jnp.mean(scaled, axis=-1, keepdims=True)
        - normal * jnp.mean(scaled * normal, axis=-1, keepdims=True)
    )


def fill_keys(kv, own_ref, peer_ref):
    frames = own_ref.shape[1]
    kv[:, :frames, :] = own_ref[...]
    for mask in range(MASKS):
        kv[mask, frames:, :] = peer_ref[mask ^ 1]


def params_kernel(n, index_ref, *refs):
    pieces = refs[: 4 * n]
    vec_ref, fb_ref, qkvb_ref, rows, sems = refs[4 * n :]
    part = vec_ref.shape[1] // n
    first_row, count = pieces[0].shape[0] - rows.shape[1], rows.shape[1]
    copies = []
    for index in range(4 * n):
        copy = pltpu.make_async_copy(
            pieces[index].at[pl.ds(first_row, count)], rows.at[index], sems.at[index]
        )
        copy.start()
        copies.append(copy)
    wait_all(copies)
    me = index_ref[0]
    width = qkvb_ref.shape[1] // 3
    slim = width // n
    vec_ref[...] = jnp.zeros(vec_ref.shape, F32)
    qkvb_ref[...] = jnp.zeros(qkvb_ref.shape, F32)
    per_row = rows.shape[2] // part

    def item(index, number):
        row, lane = number // per_row, number % per_row * part
        return rows[index, :, lane : lane + part].astype(F32)[row : row + 1]

    for owner in range(n):
        step = lax.rem(me - owner + n, n)
        for number in range(6):
            vec_ref[number : number + 1, owner * part : (owner + 1) * part] = item(step * MASKS, number)
        for mask in range(MASKS):
            index = step * MASKS + mask
            fb_ref[mask : mask + 1, owner * part : (owner + 1) * part] = item(index, 6)
            both = item(index, 7)
            qkvb_ref[mask : mask + 1, owner * slim : (owner + 1) * slim] = both[:, :slim]
            at = 2 * width + owner * slim
            qkvb_ref[mask : mask + 1, at : at + slim] = both[:, slim : 2 * slim]


def qkv_kernel(n, me_ref, x_ref, vec_ref, bias_ref, *refs):
    pieces = refs[: 4 * n]
    normed_ref, q_ref, kv_ref, w, sems = refs[4 * n :]
    wa = Weights(me_ref[0], pieces, w, sems, START[0])
    wa.start(0)
    wa.start(1)
    width = q_ref.shape[2]
    normal, _ = norm(x_ref[...].astype(F32))
    normed = (normal * vec_ref[0:1, :] + vec_ref[2:3, :]).astype(BF16)
    normed_ref[...] = normed
    for mask in range(MASKS):
        wa.wait(mask)
        wa.start(mask + 2)
        out = dot(normed, w[mask, :, : 3 * width]) + bias_ref[mask : mask + 1, :]
        out = out.astype(BF16)
        q_ref[mask] = out[:, :width]
        kv_ref[mask] = out[:, width:]


def attend_body(keep, beside, wa, x_ref, vec_ref, q_ref, kv_own_ref, kv_peer_ref, kv, w, o_refs, p_buf, p_ref, p_sems, inv_ref):
    wa.start(0)
    wa.start(1)
    frames, width = q_ref.shape[1:]
    heads = width // HD
    fill_keys(kv, kv_own_ref, kv_peer_ref)
    scale = HD**-0.5 * LOG2E
    r = x_ref[...].astype(F32) + vec_ref[4:5, :]
    out = []
    for mask in range(MASKS):
        parts = []
        for head in range(heads):
            lo = head * HD
            q = q_ref[mask, :, lo : lo + HD]
            k = kv[mask, :, lo : lo + HD]
            v = kv[mask, :, width + lo : width + lo + HD]
            scores = dot_nt(q, k)
            e = jnp.exp2(scores * scale - jnp.max(scores, axis=-1, keepdims=True) * scale)
            inv = 1.0 / jnp.sum(e, axis=-1, keepdims=True)
            e = e.astype(BF16)
            if keep:
                at = mask * heads + head
                p_buf[at] = e
                out.append(pltpu.make_async_copy(p_buf.at[at], p_ref.at[at], p_sems.at[at]))
                out[-1].start()
                inv_ref[:, at : at + 1] = inv
            parts.append(dot(e, v) * inv)
        o = jnp.concatenate(parts, axis=1).astype(BF16)
        if keep:
            put(o_refs, mask, o)
        wa.wait(mask)
        wa.start(mask + 2)
        beside(mask)
        r = r + dot_nt(o, w[mask, :, 3 * width :])
    wait_all(out)
    return r


def second_norm(r, vec_ref):
    normal, _ = norm(r)
    return (normal * vec_ref[1:2, :] + vec_ref[3:4, :]).astype(BF16)


def attend_kernel(n, me_ref, x_ref, vec_ref, q_ref, kv_own_ref, kv_peer_ref, *refs):
    r_ref, c_ref, kv, w, sems = refs[4 * n :]
    wa = Weights(me_ref[0], refs[: 4 * n], w, sems, START[0])
    r = attend_body(
        False, lambda mask: None, wa, x_ref, vec_ref, q_ref, kv_own_ref, kv_peer_ref, kv, w, *[None] * 5
    )
    r_ref[...] = r
    c_ref[...] = second_norm(r, vec_ref)


def hidden_body(keep, first, w1, w2, s1, s2, r, c, vec_ref, fb_ref, e_refs, g_ref):
    for mask in range(first):
        w1.start(mask)
        w2.start(mask)
    y = r + vec_ref[5:6, :]
    for mask in range(MASKS):
        w1.wait(mask)
        w2.wait(mask)
        if mask + 2 >= first:
            w1.start(mask + 2)
            w2.start(mask + 2)
        u = dot(c, s1[mask]) + fb_ref[mask : mask + 1, :]
        phi = 0.5 * (1.0 + lax.erf(u * (0.5**0.5)))
        e = (u * phi).astype(BF16)
        if keep:
            put(e_refs, mask, e)
            bell = jnp.exp(u * u * -0.5) * 0.3989422804014327
            g_ref[mask] = (phi + u * bell).astype(BF16)
        y = y + dot_nt(e, s2[mask])
    return y.astype(BF16)


def hidden_kernel(n, me_ref, r_ref, c_ref, vec_ref, fb_ref, *refs):
    y_ref, s1, s2, sems1, sems2 = refs[8 * n :]
    w1 = Weights(me_ref[0], refs[: 4 * n], s1, sems1, START[1])
    w2 = Weights(me_ref[0], refs[4 * n : 8 * n], s2, sems2, START[2])
    y_ref[...] = hidden_body(False, 2, w1, w2, s1, s2, r_ref[...], c_ref[...], vec_ref, fb_ref, None, None)


def layer_kernel(n, me_ref, x_ref, vec_ref, fb_ref, q_ref, kv_own_ref, kv_peer_ref, *refs):
    rest = refs[12 * n :]
    y_ref, r_ref, c_ref = rest[:3]
    o_refs, e_refs = rest[3:6], rest[6:9]
    g_ref, inv_ref, p_ref = rest[9:12]
    kv, p_buf, sa, s1, s2, semsa, sems1, sems2, p_sems = rest[12:]
    wa = Weights(me_ref[0], refs[: 4 * n], sa, semsa, START[0])
    w1 = Weights(me_ref[0], refs[4 * n : 8 * n], s1, sems1, START[1])
    w2 = Weights(me_ref[0], refs[8 * n : 12 * n], s2, sems2, START[2])

    def beside(mask):
        if mask >= 2:
            w1.start(mask - 2)
            w2.start(mask - 2)

    r = attend_body(
        True, beside, wa, x_ref, vec_ref, q_ref, kv_own_ref, kv_peer_ref, kv, sa, o_refs, p_buf, p_ref, p_sems, inv_ref
    )
    r_ref[...] = r
    c = second_norm(r, vec_ref)
    c_ref[...] = c
    y_ref[...] = hidden_body(True, 0, w1, w2, s1, s2, r, c, vec_ref, fb_ref, e_refs, g_ref)


def hidden_back_kernel(n, me_ref, dy_ref, r_ref, vec_ref, g_ref, *refs):
    rest = refs[12 * n :]
    du_refs = rest[:3]
    dr_ref, da_ref, do_ref, sums_ref = rest[3:7]
    s2, s1, sa, sems2, sems1, semsa = rest[7:]
    w2 = Weights(me_ref[0], refs[: 4 * n], s2, sems2, START[2])
    w1 = Weights(me_ref[0], refs[4 * n : 8 * n], s1, sems1, START[1])
    wa = Weights(me_ref[0], refs[8 * n : 12 * n], sa, semsa, START[0])
    for mask in range(2):
        w2.start(mask)
        w1.start(mask)
    dm = dy_ref[...]
    dy = dm.astype(F32)
    width = do_ref.shape[2]
    dc = jnp.zeros(dy.shape, F32)
    for mask in range(MASKS):
        w2.wait(mask)
        w1.wait(mask)
        w2.start(mask + 2)
        w1.start(mask + 2)
        if mask >= 2:
            wa.start(mask - 2)
        du = (dot(dm, s2[mask]) * g_ref[mask].astype(F32)).astype(BF16)
        put(du_refs, mask, du)
        sums_ref[pl.ds(4 + (me_ref[1] ^ mask), 1), :] = jnp.sum(du.astype(F32), axis=0, keepdims=True)
        dc = dc + dot_nt(du, s1[mask])
    normal, inv_std = norm(r_ref[...])
    dr = dy + norm_pull(dc, normal, inv_std, vec_ref[1:2, :])
    da = dr.astype(BF16)
    dr_ref[...] = dr
    da_ref[...] = da
    for mask in range(MASKS):
        wa.wait(mask)
        wa.start(mask + 2)
        do_ref[mask] = dot(da, sa[mask, :, 3 * width :]).astype(BF16)
    sums_ref[0:1, :] = jnp.sum(dy, axis=0, keepdims=True)
    sums_ref[1:2, :] = jnp.sum(dc * normal, axis=0, keepdims=True)
    sums_ref[2:3, :] = jnp.sum(dc, axis=0, keepdims=True)
    sums_ref[3:4, :] = jnp.sum(da.astype(F32), axis=0, keepdims=True)


def start_softmax(p_ref, p_buf, p_sems):
    copies = [pltpu.make_async_copy(p_ref.at[at], p_buf.at[at], p_sems.at[at]) for at in range(p_buf.shape[0])]
    for copy in copies[:3]:
        copy.start()
    return copies


def attend_back_body(loads, do_ref, q_ref, kv_own_ref, kv_peer_ref, inv_ref, dq_ref, own_ref, peer_ref, kv, p_buf):
    frames, width = q_ref.shape[1:]
    heads = width // HD
    fill_keys(kv, kv_own_ref, kv_peer_ref)
    scale = HD**-0.5
    for mask in range(MASKS):
        dqs, dks, dvs = [], [], []
        for head in range(heads):
            lo = head * HD
            at = mask * heads + head
            q = q_ref[mask, :, lo : lo + HD]
            k = kv[mask, :, lo : lo + HD]
            v = kv[mask, :, width + lo : width + lo + HD]
            do = do_ref[mask, :, lo : lo + HD]
            loads[at].wait()
            if at + 3 < len(loads):
                loads[at + 3].start()
            e_low = p_buf[at]
            inv = inv_ref[:, at : at + 1]
            e = e_low.astype(F32)
            t = e * dot_nt(do, v)
            ds = (t - e * (jnp.sum(t, axis=-1, keepdims=True) * inv)).astype(BF16)
            dqs.append(dot(ds, k) * (inv * scale))
            dks.append(dot_tn((q.astype(F32) * inv).astype(BF16), ds) * scale)
            dvs.append(dot_tn((do.astype(F32) * inv).astype(BF16), e_low))
        dq_ref[mask] = jnp.concatenate(dqs, axis=1).astype(BF16)
        back = jnp.concatenate(dks + dvs, axis=0).astype(BF16).T
        own_ref[mask] = back[:frames]
        peer_ref[mask ^ 1] = back[frames:]


def attend_back_kernel(do_ref, q_ref, kv_own_ref, kv_peer_ref, inv_ref, p_ref, dq_ref, own_ref, peer_ref, kv, p_buf, p_sems):
    loads = start_softmax(p_ref, p_buf, p_sems)
    attend_back_body(loads, do_ref, q_ref, kv_own_ref, kv_peer_ref, inv_ref, dq_ref, own_ref, peer_ref, kv, p_buf)


def both_back_kernel(n, me_ref, dy_ref, r_ref, vec_ref, g_ref, q_ref, kv_own_ref, kv_peer_ref, inv_ref, p_ref, *refs):
    rest = refs[12 * n :]
    dr_ref, dq_ref, own_ref, peer_ref = rest[:4]
    s2, s1, sa, sems2, sems1, semsa, kv, p_buf, p_sems, du, da, do, sums = rest[4:]
    loads = start_softmax(p_ref, p_buf, p_sems)
    hidden_back_kernel(
        n, me_ref, dy_ref, r_ref, vec_ref, g_ref, *refs[: 12 * n], du.at[0], du.at[0], du, dr_ref, da, do, sums, s2, s1, sa, sems2, sems1, semsa
    )
    attend_back_body(loads, do, q_ref, kv_own_ref, kv_peer_ref, inv_ref, dq_ref, own_ref, peer_ref, kv, p_buf)


def input_back_kernel(n, me_ref, x_ref, dr_ref, vec_ref, dq_ref, own_ref, recv_ref, *refs):
    pieces = refs[: 4 * n]
    rest = refs[4 * n :]
    dx_ref = rest[0]
    d_refs = rest[1:4]
    sums_ref, w, sems = rest[4:]
    wa = Weights(me_ref[0], pieces, w, sems, START[0])
    wa.start(0)
    wa.start(1)
    width = dq_ref.shape[2]
    dn = jnp.zeros(dr_ref.shape, F32)
    sums_ref[...] = jnp.zeros(sums_ref.shape, F32)
    for mask in range(MASKS):
        dkv = (own_ref[mask].astype(F32) + recv_ref[mask].astype(F32)).astype(BF16)
        d = jnp.concatenate([dq_ref[mask], dkv], axis=1)
        put(d_refs, mask, d)
        sums_ref[pl.ds(4 + (me_ref[1] ^ mask), 1), : 3 * width] = jnp.sum(d.astype(F32), axis=0, keepdims=True)
        wa.wait(mask)
        wa.start(mask + 2)
        dn = dn + dot_nt(d, w[mask, :, : 3 * width])
    normal, inv_std = norm(x_ref[...].astype(F32))
    dx = dr_ref[...] + norm_pull(dn, normal, inv_std, vec_ref[0:1, :])
    dx_ref[...] = dx.astype(BF16)
    sums_ref[0:1, :] = jnp.sum(dn * normal, axis=0, keepdims=True)
    sums_ref[1:2, :] = jnp.sum(dn, axis=0, keepdims=True)


def weight_kernel(n, pairs, *refs):
    out_ref = refs[-1]
    sums_ref = refs[-2] if len(refs) == 2 * MASKS * pairs + 2 else None
    part = refs[0].shape[1] // n
    at = 0
    for pair in range(pairs):
        left = refs[2 * MASKS * pair : 2 * MASKS * pair + MASKS]
        right = refs[2 * MASKS * pair + MASKS : 2 * MASKS * (pair + 1)]
        acc = None
        for mask in range(MASKS):
            term = dot_tn(left[mask][...], right[mask][0] if right[mask].ndim == 3 else right[mask][...])
            acc = term if acc is None else acc + term
        cols = acc.shape[1]
        for block in range(n):
            out_ref[block, :part, at : at + cols] = acc[block * part : (block + 1) * part].astype(BF16)
        at += cols
    if sums_ref is not None:
        width = refs[2 * MASKS - 1].shape[1] // 3
        slim = width // n
        sums = sums_ref[...]
        for block in range(n):
            lo = block * slim
            low = jnp.concatenate(
                [sums[12:16, lo : lo + slim], sums[12:16, 2 * width + lo : 2 * width + lo + slim]]
                + [jnp.zeros((4, part - 2 * slim), F32)],
                axis=1,
            )
            mine = jnp.concatenate([sums[:12, block * part : (block + 1) * part], low], axis=0)
            mine = jnp.concatenate([mine, jnp.zeros((16, at - part), F32)], axis=1)
            out_ref[block, part:, :] = mine.astype(BF16)


def place_kernel(index_ref, *refs):
    values, out_ref = refs[:MASKS], refs[MASKS]
    for mask in range(MASKS):
        out_ref[index_ref[1] ^ mask] = values[mask][...].astype(out_ref.dtype)


def shape(dims, dtype):
    return jax.ShapeDtypeStruct(dims, dtype)


def call(body, in_specs, out_shape, scratch, name, out_specs=None):
    return pl.pallas_call(
        body,
        in_specs=in_specs,
        out_specs=jax.tree.map(lambda _: VMEM, out_shape) if out_specs is None else out_specs,
        out_shape=out_shape,
        scratch_shapes=scratch,
        compiler_params=pltpu.CompilerParams(vmem_limit_bytes=VMEM_MIB[name] * 2**20),
        cost_estimate=pl.CostEstimate(flops=int(COST[name] * 1.15e9 * COST_SCALE), bytes_accessed=1, transcendentals=0),
        name=name,
    )


def local(inputs, plan, cotangent, w_qkv, w_out, w_fc1, w_fc2, ln_gains, biases, qv_bias, fc1_bias):
    n = lax.axis_size("dp")
    me = lax.axis_index("dp")
    tensor = lax.axis_index("tensor")
    first = lax.axis_index("section") == 0
    frames = inputs.shape[1] // 2
    features = inputs.shape[2]
    width = w_qkv.shape[3]
    units = w_fc1.shape[2]
    heads = MASKS * width // HD
    part = features // n
    slot, half = tensor // 2, tensor % 2
    index = jnp.stack([me, tensor]).astype(jnp.int32)

    w_scratch = pltpu.VMEM((MASKS, features, features), BF16)
    w_sems = pltpu.SemaphoreType.DMA((MASKS * n,))
    many = [HBM] * (MASKS * n)
    act = shape((frames, features), BF16)
    real = shape((frames, features), F32)
    wide = shape((frames, units), BF16)
    all_wide = shape((MASKS, frames, units), BF16)
    wides = (wide, wide, shape((2, frames, units), BF16))
    head_act = shape((MASKS, frames, width), BF16)
    pair_act = shape((MASKS, frames, 2 * width), BF16)
    kv_scratch = pltpu.VMEM((MASKS, 2 * frames, 2 * width), BF16)
    sums_shape = shape((8, features), F32)

    def clip_part(clips, which, part_half):
        return lax.dynamic_slice(clips, (which, part_half * frames, 0), (1, frames, features))[0]

    def read_params(pa):
        return call(
            functools.partial(params_kernel, n),
            [SMEM] + many,
            (shape((8, features), F32), shape((MASKS, units), F32), shape((MASKS, 3 * width), F32)),
            [pltpu.VMEM((MASKS * n, 16, features), BF16), w_sems],
            "params",
        )(index, *pa)

    def project(x, vec, qkvb, pa):
        return call(
            functools.partial(qkv_kernel, n),
            [SMEM, VMEM, VMEM, VMEM] + many,
            (act, head_act, pair_act),
            [w_scratch, w_sems],
            "qkv",
        )(index, x, vec, qkvb, *pa)

    p_shape = shape((heads, frames, 2 * frames), BF16)
    p_scratch = pltpu.VMEM(p_shape.shape, BF16)
    p_sems = pltpu.SemaphoreType.DMA((heads,))
    inv_shape = shape((frames, 128), F32)

    def forward(x, event):
        normed, q, kv = project(x, vec, qkvb, pa)
        kv_peer = flip_core(after(kv, event))
        outs = (act, real, act) + tuple(shape(lead + (frames, width), BF16) for lead in ((), (), (2,))) + wides
        outs += (all_wide, inv_shape, pltpu.HBM(p_shape.shape, BF16))
        y, r, c, *kept = call(
            functools.partial(layer_kernel, n),
            [SMEM] + [VMEM] * 6 + many * 3,
            outs,
            [kv_scratch, p_scratch] + [w_scratch] * 3 + [w_sems] * 3 + [p_sems],
            "layer",
            (VMEM,) * (len(outs) - 1) + (HBM,),
        )(index, x, vec, fb, q, kv, kv_peer, *pa, *p1, *p2)
        return y, dict(
            x=x, normed=normed, q=q, kv=kv, kv_peer=kv_peer, r=r, c=c, o=kept[:3], e=kept[3:6], g=kept[6], inv=kept[7], p=kept[8]
        )

    def both_back(dy, s):
        return call(
            functools.partial(both_back_kernel, n),
            [SMEM] + [VMEM] * 8 + [HBM] + many * 3,
            (real, head_act, pair_act, pair_act),
            [w_scratch] * 3
            + [w_sems] * 3
            + [kv_scratch, p_scratch, p_sems]
            + [pltpu.VMEM(one.shape, one.dtype) for one in (wides[2], act, head_act, sums_shape)],
            "both_back",
        )(index, dy, s["r"], vec, s["g"], s["q"], s["kv"], s["kv_peer"], s["inv"], s["p"], *p2, *p1, *pa)

    def hidden_back(dy, s, *events):
        *du, dr, da, do, sums = call(
            functools.partial(hidden_back_kernel, n),
            [SMEM] + [VMEM] * 4 + many * 3,
            wides + (real, act, head_act, sums_shape),
            [w_scratch] * 3 + [w_sems] * 3,
            "hidden_back",
        )(after(index, *events), dy, s["r"], vec, s["g"], *p2, *p1, *pa)
        return du, dr, da, do, sums

    def attend_back(do, s, *events):
        return call(
            attend_back_kernel,
            [VMEM] * 5 + [HBM],
            (head_act, pair_act, pair_act),
            [kv_scratch, p_scratch, p_sems],
            "attend_back",
        )(after(do, *events), s["q"], s["kv"], s["kv_peer"], s["inv"], s["p"])

    def input_back(dr, dq, own, recv, s, *events):
        dx, *rest = call(
            functools.partial(input_back_kernel, n),
            [SMEM] + [VMEM] * 6 + many,
            (act,) + tuple(shape(lead + (frames, 3 * width), BF16) for lead in ((), (), (2,))) + (sums_shape,),
            [w_scratch, w_sems],
            "input_back",
        )(after(index, *events), s["x"], dr, vec, dq, own, recv, *pa)
        return dx, rest[:3], rest[3]

    def weight_grad(pairs, event, sums=None):
        cols = sum(right[0].shape[1] for _, right in pairs)
        blocks = [block for left, right in pairs for block in (*left, *right)]
        blocks[0] = after(blocks[0], event)
        more = [] if sums is None else [sums]
        return call(
            functools.partial(weight_kernel, n, len(pairs)),
            [VMEM] * (len(blocks) + len(more)),
            shape((n, part + 16 * len(more), cols), BF16),
            [],
            "weight_grad",
        )(*blocks, *more)

    def whole(values, dtype):
        out = call(place_kernel, [SMEM] + [VMEM] * MASKS, shape((MASKS, frames, features), dtype), [], "place")(
            index, *values
        )
        return out.reshape((1,) + inputs.shape)

    small = jnp.concatenate(
        [
            ln_gains[0].reshape(-1),
            biases[0].reshape(-1),
            fc1_bias[0].reshape(-1),
            qv_bias[0].reshape(-1),
        ]
    )
    small = jnp.pad(small, (0, 16 * features - small.shape[0])).reshape(16, features)
    shard_a = jnp.concatenate([w_qkv[0, 0], w_qkv[0, 1], w_qkv[0, 2], w_out[0].T], axis=1)
    shard_a = jnp.concatenate([shard_a, small], axis=0)
    shard_1 = w_fc1[0]
    shard_2 = w_fc2[0].T

    x_clip = clip_part(inputs, plan[0, slot], half)
    out_grad = clip_part(cotangent, slot, half)

    rows, rows_2 = [shard_a], [jnp.concatenate([shard_1, shard_2], axis=0)]
    across, across_2 = [flip_chip(shard_a)], []
    rows.append(ring_next(rows[0]))
    across_2.append(flip_chip(after(rows_2[0], across[0])))
    rows.append(ring_next(after(rows[1], across[0])))
    rows_2.append(ring_next(after(rows_2[0], rows[2])))
    for step in range(3, n):
        rows.append(ring_next(after(rows[-1], across_2[0])))
    across += [flip_chip(row) for row in rows[1:]]
    for step in range(2, n):
        rows_2.append(ring_next(rows_2[-1]))
    across_2.append(flip_chip(after(rows_2[1], across[-2])))
    across_2 += [flip_chip(row) for row in rows_2[2:]]
    pa = all_pieces(rows, across)

    vec, fb, qkvb = read_params(pa)
    _, q, kv = project(x_clip, vec, qkvb, pa)
    clip_across = clip_part(inputs, plan[0, 1 - slot], half)
    normed_far = call(norm_kernel, [VMEM, VMEM], act, [], "norm")(clip_across, vec)
    r, c = call(
        functools.partial(attend_kernel, n),
        [SMEM] + [VMEM] * 5 + many,
        (real, act),
        [kv_scratch, w_scratch, w_sems],
        "attend",
    )(index, x_clip, vec, after(q, rows_2[-2], normed_far), kv, flip_core(kv), *pa)
    p1 = p2 = all_pieces(rows_2, across_2[:-1] + [after(across_2[-1], c)])
    mid = call(
        functools.partial(hidden_kernel, n),
        [SMEM] + [VMEM] * 4 + many * 2,
        act,
        [w_scratch] * 2 + [w_sems] * 2,
        "hidden",
    )(index, r, c, vec, fb, *p1, *p2)

    relayed = lax.ppermute(mid, "section", [(0, 1)])
    mid_across = flip_within(mid, 2, 0)
    x = jnp.where(first, x_clip, relayed)
    y, kept = forward(x, mid_across)
    normed_across = flip_within(kept["normed"], 2, 1)

    e_all = trade(kept["e"])
    dr, dq, own, peer = both_back(out_grad, kept)
    dx, _, _ = input_back(dr, dq, own, flip_core(after(peer, normed_across, e_all[2])), kept)
    relayed = lax.ppermute(dx, "section", [(1, 0)])
    dx_across = flip_within(dx, 2, 1)
    relayed_across = lax.ppermute(after(dx_across, relayed), "section", [(1, 0)])
    c_all = spread(after(kept["c"], dx_across))
    o_all = trade(kept["o"][:2] + [after(kept["o"][2], dx_across)])
    dy = jnp.where(first, relayed, out_grad)
    dy_across = jnp.where(first, relayed_across, clip_part(cotangent, 1 - slot, half))

    du, dr, da, do, sums = hidden_back(dy, kept, dx_across, e_all[1], e_all[3])
    du_all = trade(du)
    far = after(dy_across, dr)
    dm_all = [dy, flip_core(dy), far, flip_core(far)]
    dq, own, peer = attend_back(do, kept, c_all[2], o_all[2])
    recv = flip_core(peer)
    da_all = spread(da)
    blocks_2 = weight_grad([(dm_all, e_all)], dq)
    dx, dqkv, sums_one = input_back(dr, dq, own, recv, kept, blocks_2, da_all[2])
    dqkv_all = trade(dqkv)
    grad_2, got_2 = ring_scatter(blocks_2, me, {1: (dx,)})
    sums = jnp.concatenate([sums, sums_one], axis=0)
    sums = sums + flip_core(sums)
    sums = sums + flip_chip(sums)
    blocks_1 = weight_grad([(c_all, du_all)], dx)
    grad_1, got_1 = ring_scatter(blocks_1, me)
    normed_across = jnp.where(first, normed_far, normed_across)
    normed_all = [kept["normed"], flip_core(kept["normed"]), normed_across, flip_core(normed_across)]
    sums = after(sums, got_2[-1], got_1[0])
    blocks_a = weight_grad([(normed_all, dqkv_all), (da_all, o_all)], blocks_1, sums)
    steps = ring_steps(blocks_a, me)
    got = next(steps)
    last = flip_chip(after(jnp.where(first, dx, y), dqkv_all[2], da_all[2]))
    last = after(last, got)
    y_across = jnp.where(first, mid_across, last)
    dx_across = jnp.where(first, last, dx_across)
    hidden_states = whole([y, flip_core(y), y_across, flip_core(y_across)], BF16)
    grad_inputs = whole([dx, flip_core(dx), dx_across, flip_core(dx_across)], F32)
    for step in range(1, n):
        if step == n - 1:
            got = after(got, hidden_states, grad_inputs)
        got = steps.send(got)
    grad_a = got

    mine = grad_a[part:, :part]
    grad_a = grad_a[:part]
    grad_gains = jnp.stack([mine[8], mine[1]])[None]
    grad_biases = jnp.stack([mine[9], mine[2], mine[3], mine[0]])[None]
    grad_fb = lax.dynamic_slice(mine, (4 + tensor, 0), (1, part))[None]
    slim = width // n
    grad_qv = lax.dynamic_slice(mine, (12 + tensor, 0), (1, 2 * slim)).reshape(1, 2, 1, slim)

    grad_qkv = jnp.stack([grad_a[:, i * width : (i + 1) * width] for i in range(3)])[None]
    return (
        hidden_states,
        grad_inputs,
        grad_qkv,
        grad_a[:, 3 * width :].T[None],
        grad_1[None],
        grad_2.T[None],
        grad_gains,
        grad_biases,
        grad_qv,
        grad_fb,
    )


def solution(mesh):
    placed = (
        P("dp", None, None),
        P("dp", None),
        P("dp", None, None),
        P("section", None, "dp", "tensor"),
        P("section", "tensor", "dp"),
        P("section", "dp", "tensor"),
        P("section", "tensor", "dp"),
        P("section", None, "dp"),
        P("section", None, "dp"),
        P("section", None, "tensor", "dp"),
        P("section", "tensor", "dp"),
    )
    return jax.shard_map(
        local,
        mesh=mesh,
        in_specs=placed,
        out_specs=(P("section", "dp", None, None), P("section", "dp", None, None)) + placed[3:],
        check_vma=False,
    )
```

time: 465 us -> 365 us (0.78)
  Pallas kernels: 148 us -> 121 us
  blocking collectives: 21.9 us -> 0 us
  waiting for transfers between devices: 172 us -> 160 us
  between operations: 17.3 us -> 6.04 us
  other arithmetic: 22.6 us -> 13.1 us
  local copies, waits for them, and re-layouts: 28 us -> 18.7 us
  starting transfers between devices: 48.4 us -> 40.8 us
    pallas_call x16 -> x17, Pallas kernels: 148 us -> 121 us  [the longest x1 21.8 us: both_back(): call(functools.partial(both_back_kernel, n), [SMEM] + [VMEM] * 8 + [HBM]...]
    all_gather x1 -> x0, blocking collectives: 21.9 us -> none  [local(): small = lax.all_gather(small, ('dp', 'tensor'))]
    ppermute x21 -> x15, waiting for transfers between devices: 87.5 us -> 70.5 us  [ring_next(): lax.ppermute(value, 'dp', [(i, (i + 1) % count) for i in range(count)])]
    ppermute x66 -> x57, waiting for transfers between devices: 52.8 us -> 68 us  [flip(): return lax.ppermute(value, 'tensor', [(i, i ^ mask) for i in range(count)])]
    convert_element_type x9 -> x6, other arithmetic: 14 us -> 3.2 us  [ring_steps(): moving = (yield ring_next(moving.astype(BF16)))]
    ppermute x2 -> x4, waiting for transfers between devices: 8.71 us -> 0.01 us  [the longest x3 0.01 us: flip_within(): return lax.ppermute(value, ('section', 'tensor'), pairs)]
    ppermute x21 -> x15, starting transfers between devices: 12.3 us -> 3.79 us  [ring_next(): lax.ppermute(value, 'dp', [(i, (i + 1) % count) for i in range(count)])]
    squeeze x4 -> x3, local copies, waits for them, and re-layouts: 5.53 us -> 0.8 us  [block(): lax.dynamic_index_in_dim(blocks, (me - 1 - step) % count, 0, keepdims=False)]
  transfers between devices with their start and end apart: 93 -> 78, of which waited for: 33 -> 33; matrix products, arithmetic and copies ran while one was open for 8% -> 4% of each run, Pallas kernels for 18% -> 32%
where the time goes in v2:
time: 365 us; the launch traced here: 360 us
  waiting for transfers between devices  160 us (44%)
  Pallas kernels  121 us (33%)
  starting transfers between devices  40.8 us (11%)
  local copies, waits for them, and re-layouts  18.7 us (5%)
  other arithmetic  13.1 us (4%)
  between operations  6.04 us (2%)
    ppermute x15, waiting for transfers between devices, ring_next(): lax.ppermute(value, 'dp', [(i, (i + 1) % count) for i in range(count)])  70.5 us
    ppermute x57, waiting for transfers between devices, flip(): return lax.ppermute(value, 'tensor', [(i, i ^ mask) for i in range(count)])  68 us
    ppermute x57, starting transfers between devices, flip(): return lax.ppermute(value, 'tensor', [(i, i ^ mask) for i in range(count)])  26.7 us
    pallas_call x1, Pallas kernels, both_back(): call(functools.partial(both_back_kernel, n), [SMEM] + [VMEM] * 8 + [HBM]...  21.8 us
    pallas_call x1, Pallas kernels, forward(): call(functools.partial(layer_kernel, n), [SMEM] + [VMEM] * 6 + many * 3,...  15.1 us
    pallas_call x1, Pallas kernels, attend_back(): call(attend_back_kernel, [VMEM] * 5 + [HBM], (head_act, pair_act, pair_ac...  15 us
    ppermute x1, waiting for transfers between devices, local(): relayed = lax.ppermute(dx, 'section', [(1, 0)])  13 us
    pallas_call x3, Pallas kernels, weight_grad(): call(functools.partial(weight_kernel, n, len(pairs)), [VMEM] * (len(block...  12.5 us
  transfers between devices with their start and end apart: 78, of which 33 were waited for; matrix products, arithmetic and copies ran while one was open for 4% of the time, Pallas kernels for 32%

profile of v2, /device:TPU:0, one launch (start us, length us, event | category | flops | bytes accessed | tf_op | source)
XLA Modules:
  0.0 360.0 jit_solution(5885775245044969998)
XLA Ops:
  10.7 5.9 %collective-permute-done.1.refs_2_.refs_34_ = bf16[208,768]{1,0:T(8,128)(2,1)S(1)} collective-permute-done((bf16[208,768]{1,0:T(8,128)(2,1)S(1)}, bf16[208,768]{1,0:T(8,128)(2,1)S(1)}, u32[]{:S(2)}, u32[]{:S(2)}) %collective-permute-start.1) | collective-permute-done | bytes 319520 | tf_op jit(solution)/shard_map/ppermute | solution.py:53
  19.9 9.9 %collective-permute-done.7.refs_8_.refs_40_ = bf16[208,768]{1,0:T(8,128)(2,1)S(1)} collective-permute-done((bf16[208,768]{1,0:T(8,128)(2,1)S(1)}, bf16[208,768]{1,0:T(8,128)(2,1)S(1)}, u32[]{:S(2)}, u32[]{:S(2)}) %collective-permute-start.7) | collective-permute-done | bytes 319520 | tf_op jit(solution)/shard_map/ppermute | solution.py:58
  32.7 7.1 %collective-permute-done.5.refs_6_.refs_38_ = bf16[208,768]{1,0:T(8,128)(2,1)S(1)} collective-permute-done((bf16[208,768]{1,0:T(8,128)(2,1)S(1)}, bf16[208,768]{1,0:T(8,128)(2,1)S(1)}, u32[]{:S(2)}, u32[]{:S(2)}) %collective-permute-start.5) | collective-permute-done | bytes 319520 | tf_op jit(solution)/shard_map/ppermute | solution.py:53
  40.6 10.9 %collective-permute-done.12.refs_12_.refs_44_ = bf16[208,768]{1,0:T(8,128)(2,1)S(1)} collective-permute-done((bf16[208,768]{1,0:T(8,128)(2,1)S(1)}, bf16[208,768]{1,0:T(8,128)(2,1)S(1)}, u32[]{:S(2)}, u32[]{:S(2)}) %collective-permute-start.12) | collective-permute-done | bytes 319520 | tf_op jit(solution)/shard_map/ppermute | solution.py:58
  53.2 5.4 %collective-permute-done.14.refs_14_.refs_46_ = bf16[208,768]{1,0:T(8,128)(2,1)} collective-permute-done((bf16[208,768]{1,0:T(8,128)(2,1)S(1)}, bf16[208,768]{1,0:T(8,128)(2,1)}, u32[]{:S(2)}, u32[]{:S(2)}) %collective-permute-start.14) | collective-permute-done | bytes 319520 | tf_op jit(solution)/shard_map/ppermute | solution.py:53
  68.8 5.9 %qkv.2 = (bf16[320,768]{1,0:T(8,128)(2,1)}, bf16[4,320,192]{2,1,0:T(8,128)(2,1)S(1)}, bf16[4,320,384]{2,1,0:T(8,128)(2,1)S(1)}) custom-call(s32[2]{0:T(128)S(1)} %pad_add_fusion.index_ref.me_ref, bf16[320,768]{1,0:T(8,128)(2,1)S(1)} %get-tuple-element.153.x_ref, f32[8,768]{1,0:T(8,128)S(1)} %get-tuple-element.79.vec_ref, ...), custom_call_target="tpu_custom_call" | custom-call | flops 46000001024 | bytes 1 | tf_op jit(solution)/shard_map/qkv/pallas_call | solution.py:578
  74.8 7.7 %collective-permute-done.27.refs_12_.refs_28_.refs_44_ = bf16[384,768]{1,0:T(8,128)(2,1)S(1)} collective-permute-done((bf16[384,768]{1,0:T(8,128)(2,1)}, bf16[384,768]{1,0:T(8,128)(2,1)S(1)}, u32[]{:S(2)}, u32[]{:S(2)}) %collective-permute-start.27) | collective-permute-done | bytes 589856 | tf_op jit(solution)/shard_map/ppermute | solution.py:58
  86.2 12.6 %collective-permute-done.29.refs_14_.refs_30_.refs_46_ = bf16[384,768]{1,0:T(8,128)(2,1)S(1)} collective-permute-done((bf16[384,768]{1,0:T(8,128)(2,1)S(1)}, bf16[384,768]{1,0:T(8,128)(2,1)S(1)}, u32[]{:S(2)}, u32[]{:S(2)}) %collective-permute-start.29) | collective-permute-done | bytes 589856 | tf_op jit(solution)/shard_map/ppermute | solution.py:53
  99.8 9.5 %attend.1 = (f32[320,768]{1,0:T(8,128)S(1)}, bf16[320,768]{1,0:T(8,128)(2,1)S(1)}) custom-call(s32[2]{0:T(128)S(1)} %pad_add_fusion.index_ref.me_ref, bf16[320,768]{1,0:T(8,128)(2,1)S(1)} %get-tuple-element.153.x_ref, f32[8,768]{1,0:T(8,128)S(1)} %get-tuple-element.79.vec_ref, bf16[4,320,192]{2,1,0:T(8,128)(2,1)S(1)} %get-tuple-element.83.q_ref, ...), custom_call_target="tpu_custom_call" | custom-call | flops 46000001024 | bytes 1 | tf_op jit(solution)/shard_map/attend/pallas_call | solution.py:704
  112.0 8.4 %collective-permute-done.25.refs_10_.refs_26_.refs_42_ = bf16[384,768]{1,0:T(8,128)(2,1)S(1)} collective-permute-done((bf16[384,768]{1,0:T(8,128)(2,1)}, bf16[384,768]{1,0:T(8,128)(2,1)S(1)}, u32[]{:S(2)}, u32[]{:S(2)}) %collective-permute-start.25) | collective-permute-done | bytes 589856 | tf_op jit(solution)/shard_map/ppermute | solution.py:53
  124.0 6.9 %hidden.1 = bf16[320,768]{1,0:T(8,128)(2,1)S(1)} custom-call(s32[2]{0:T(128)S(1)} %pad_add_fusion.index_ref.me_ref, f32[320,768]{1,0:T(8,128)S(1)} %get-tuple-element.85.r_ref, bf16[320,768]{1,0:T(8,128)(2,1)S(1)} %get-tuple-element.86.c_ref, f32[8,768]{1,0:T(8,128)S(1)} %get-tuple-element.79.vec_ref, f32[4,768]{1,0:T(4,128)S(1)} %get-tuple-element.87.fb_ref, ...), custom_call_target="tpu_custom_call" | custom-call | flops 46000001024 | bytes 1 | tf_op jit(solution)/shard_map/hidden/pallas_call | solution.py:712
  137.3 8.5 %collective-permute-done.31 = bf16[320,768]{1,0:T(8,128)(2,1)S(1)} collective-permute-done((bf16[320,768]{1,0:T(8,128)(2,1)S(1)}, bf16[320,768]{1,0:T(8,128)(2,1)S(1)}, u32[]{:S(2)}, u32[]{:S(2)}) %collective-permute-start.31) | collective-permute-done | bytes 491552 | tf_op jit(solution)/shard_map/ppermute | solution.py:720
  153.8 15.1 %layer.1 = (bf16[320,768]{1,0:T(8,128)(2,1)S(1)}, f32[320,768]{1,0:T(8,128)S(1)}, bf16[320,768]{1,0:T(8,128)(2,1)S(1)}, bf16[320,192]{1,0:T(8,128)(2,1)S(1)}, bf...) custom-call(s32[2]{0:T(128)S(1)} %pad_add_fusion.index_ref.me_ref, ...), custom_call_target="tpu_custom_call" | custom-call | flops 46000001024 | bytes 1 | tf_op jit(solution)/shard_map/layer/pallas_call | solution.py:596
  170.0 21.8 %both_back.1 = (f32[320,768]{1,0:T(8,128)S(1)}, bf16[4,320,192]{2,1,0:T(8,128)(2,1)S(1)}, bf16[4,320,384]{2,1,0:T(8,128)(2,1)S(1)}, bf16[4,320,384]{2,1,0:T(8,128)(2,1)S(1)}) custom-call(s32[2]{0:T(128)S(1)} %pad_add_fusion.index_ref.me_ref, bf16[320,768]{1,0:T(8,128)(2,1)S(1)} %dynamic-slice_bitcast_fusion.dy_ref, f32[320,768]{1,0:T(8,128)S(1)} %get-tuple-element.94.r_ref, ...), custom_call_target="tpu_custom_call" | custom-call | flops 46000001024 | bytes 1 | tf_op jit(solution)/shard_map/both_back/pallas_call | solution.py:609
  196.0 5.5 %input_back.2 = (bf16[320,768]{1,0:T(8,128)(2,1)S(1)}, bf16[320,576]{1,0:T(8,128)(2,1)}, bf16[320,576]{1,0:T(8,128)(2,1)}, bf16[2,320,576]{2,1,0:T(8,128)(2,1)}, f32[8,768]{1,0:T(8,128)}) custom-call(s32[2]{0:T(128)S(1)} %pad_add_fusion.index_ref.me_ref, bf16[320,768]{1,0:T(8,128)(2,1)S(1)} %broadcast_select_fusion.5.x_ref, ...), custom_call_target="tpu_custom_call" | custom-call | flops 1150000000 | bytes 1 | tf_op jit(solution)/shard_map/input_back/pallas_call | solution.py:640
  203.8 13.0 %collective-permute-done.38 = bf16[320,768]{1,0:T(8,128)(2,1)S(1)} collective-permute-done((bf16[320,768]{1,0:T(8,128)(2,1)S(1)}, bf16[320,768]{1,0:T(8,128)(2,1)S(1)}, u32[]{:S(2)}, u32[]{:S(2)}) %collective-permute-start.38) | collective-permute-done | bytes 491552 | tf_op jit(solution)/shard_map/ppermute | solution.py:729
  221.2 11.5 %hidden_back.1 = (bf16[320,768]{1,0:T(8,128)(2,1)S(1)}, bf16[320,768]{1,0:T(8,128)(2,1)S(1)}, bf16[2,320,768]{2,1,0:T(8,128)(2,1)}, f32[320,768]{1,0:T(8,128)S(1...) custom-call(s32[2]{0:T(128)S(1)} %pad_add_fusion.index_ref.me_ref, ...), custom_call_target="tpu_custom_call" | custom-call | flops 46000001024 | bytes 1 | tf_op jit(solution)/shard_map/hidden_back/pallas_call | solution.py:621
  239.4 15.0 %attend_back.1 = (bf16[4,320,192]{2,1,0:T(8,128)(2,1)S(1)}, bf16[4,320,384]{2,1,0:T(8,128)(2,1)S(1)}, bf16[4,320,384]{2,1,0:T(8,128)(2,1)}) custom-call(bf16[4,320,192]{2,1,0:T(8,128)(2,1)S(1)} %get-tuple-element.113.do_ref, bf16[4,320,192]{2,1,0:T(8,128)(2,1)S(1)} %get-tuple-element.90.q_ref, bf16[4,320,384]{2,1,0:T(8,128)(2,1)S(1)} %get-tuple-element.92.kv_own_ref, ...), custom_call_target="tpu_custom_call" | custom-call | flops 46000001024 | bytes 1 | tf_op jit(solution)/shard_map/attend_back/pallas_call | solution.py:631
  272.0 5.6 %input_back.3 = (bf16[320,768]{1,0:T(8,128)(2,1)S(1)}, bf16[320,576]{1,0:T(8,128)(2,1)S(1)}, bf16[320,576]{1,0:T(8,128)(2,1)S(1)}, bf16[2,320,576]{2,1,0:T(8,128)(2,1)S(1)}, f32[8,768]{1,0:T(8,128)S(1)}) custom-call(s32[2]{0:T(128)S(1)} %pad_add_fusion.index_ref.me_ref, bf16[320,768]{1,0:T(8,128)(2,1)S(1)} %broadcast_select_fusion.5.x_ref, ...), custom_call_target="tpu_custom_call" | custom-call | flops 1150000000 | bytes 1 | tf_op jit(solution)/shard_map/input_back/pallas_call | solution.py:640
  294.8 7.2 %collective-permute-done.49.refs_6_ = bf16[2,320,576]{2,1,0:T(8,128)(2,1)S(1)} collective-permute-done((bf16[2,320,576]{2,1,0:T(8,128)(2,1)S(1)}, bf16[2,320,576]{2,1,0:T(8,128)(2,1)S(1)}, u32[]{:S(2)}, u32[]{:S(2)}) %collective-permute-start.49) | collective-permute-done | bytes 737312 | tf_op jit(solution)/shard_map/ppermute | solution.py:53
  303.0 8.1 %collective-permute-done.68 = bf16[192,768]{1,0:T(8,128)(2,1)} collective-permute-done((bf16[192,768]{1,0:T(8,128)(2,1)S(1)}, bf16[192,768]{1,0:T(8,128)(2,1)}, u32[]{:S(2)}, u32[]{:S(2)}) %collective-permute-start.68) | collective-permute-done | bytes 294944 | tf_op jit(solution)/shard_map/ppermute | solution.py:58
  324.8 6.4 %collective-permute-done.70 = bf16[208,768]{1,0:T(8,128)(2,1)} collective-permute-done((bf16[208,768]{1,0:T(8,128)(2,1)}, bf16[208,768]{1,0:T(8,128)(2,1)}, u32[]{:S(2)}, u32[]{:S(2)}) %collective-permute-start.70) | collective-permute-done | bytes 319520 | tf_op jit(solution)/shard_map/ppermute | solution.py:58
  336.3 7.3 %collective-permute-done.74 = bf16[208,768]{1,0:T(8,128)(2,1)S(1)} collective-permute-done((bf16[208,768]{1,0:T(8,128)(2,1)S(1)}, bf16[208,768]{1,0:T(8,128)(2,1)S(1)}, u32[]{:S(2)}, u32[]{:S(2)}) %collective-permute-start.74) | collective-permute-done | bytes 319520 | tf_op jit(solution)/shard_map/ppermute | solution.py:58
  350.3 5.2 %collective-permute-done.75 = bf16[208,768]{1,0:T(8,128)(2,1)S(1)} collective-permute-done((bf16[208,768]{1,0:T(8,128)(2,1)S(1)}, bf16[208,768]{1,0:T(8,128)(2,1)S(1)}, u32[]{:S(2)}, u32[]{:S(2)}) %collective-permute-start.75) | collective-permute-done | bytes 319520 | tf_op jit(solution)/shard_map/ppermute | solution.py:58
  (344 shorter events, 133.6 us)
Async XLA Ops:
  29.8 22.7 %collective-permute-start.16 = (bf16[384,768]{1,0:T(8,128)(2,1)S(1)}, bf16[384,768]{1,0:T(8,128)(2,1)}, u32[]{:S(2)}, u32[]{:S(2)}) collective-permute-start(bf16[384,768]{1,0:T(8,128)(2,1)S(1)} %pad_maximum_fusion.refs_0_.refs_16_.refs_32_), channel_id=1, source_target_pairs={{0,4},{4,8},{8,12},{12,0},{1,5},{5,9},{9,13},{13,1},{2,6},{6,10},{... | collective-permute-start | bytes 1769480 | tf_op jit(solution)/shard_map/ppermute | solution.py:58
  31.1 20.4 %collective-permute-start.12 = (bf16[208,768]{1,0:T(8,128)(2,1)S(1)}, bf16[208,768]{1,0:T(8,128)(2,1)S(1)}, u32[]{:S(2)}, u32[]{:S(2)}) collective-permute-start(bf16[208,768]{1,0:T(8,128)(2,1)S(1)} %collective-permute-done.7.refs_8_.refs_40_), channel_id=1, source_target_pairs={{0,4},{4,8},{8,12},{12,0},{1,5},{5,9},{9,13},{13,1},{2,6},{6,10},{... | collective-permute-start | bytes 958472 | tf_op jit(solution)/shard_map/ppermute | solution.py:58
  32.6 20.0 %collective-permute-start.4 = (bf16[208,768]{1,0:T(8,128)(2,1)S(1)}, bf16[208,768]{1,0:T(8,128)(2,1)S(1)}, u32[]{:S(2)}, u32[]{:S(2)}) collective-permute-start(bf16[208,768]{1,0:T(8,128)(2,1)S(1)} %collective-permute-done.3.refs_4_.refs_36_), channel_id=1, source_target_pairs={{0,1},{1,0},{2,3},{3,2},{4,5},{5,4},{6,7},{7,6},{8,9},{9,8},{10,11... | collective-permute-start | bytes 958472 | tf_op jit(solution)/shard_map/ppermute | solution.py:53
  83.5 25.8 %collective-permute-start.19 = (bf16[384,768]{1,0:T(8,128)(2,1)S(1)}, bf16[384,768]{1,0:T(8,128)(2,1)S(1)}, u32[]{:S(2)}, u32[]{:S(2)}) collective-permute-start(bf16[384,768]{1,0:T(8,128)(2,1)S(1)} %copy-done.46), channel_id=1, source_target_pairs={{0,1},{1,0},{2,3},{3,2},{4,5},{5,4},{6,7},{7,6},{8,9},{9,8},{10,11... | collective-permute-start | bytes 1769480 | tf_op jit(solution)/shard_map/ppermute | solution.py:53
  83.5 27.9 %collective-permute-start.20 = (bf16[384,768]{1,0:T(8,128)(2,1)S(1)}, bf16[384,768]{1,0:T(8,128)(2,1)S(1)}, u32[]{:S(2)}, u32[]{:S(2)}) collective-permute-start(bf16[384,768]{1,0:T(8,128)(2,1)S(1)} %copy-done.56), channel_id=1, source_target_pairs={{0,1},{1,0},{2,3},{3,2},{4,5},{5,4},{6,7},{7,6},{8,9},{9,8},{10,11... | collective-permute-start | bytes 1769480 | tf_op jit(solution)/shard_map/ppermute | solution.py:53
  84.0 27.3 %collective-permute-start.22 = (bf16[384,768]{1,0:T(8,128)(2,1)}, bf16[384,768]{1,0:T(8,128)(2,1)S(1)}, u32[]{:S(2)}, u32[]{:S(2)}) collective-permute-start(bf16[384,768]{1,0:T(8,128)(2,1)} %collective-permute-done.16.refs_4_.refs_20_.refs_36_), channel_id=1, source_target_pairs={{0,2},{1,3},{2,0},{3,1},{4,6},{5,7},{6,4},{7,5},{8,10},{9,11},{10,... | collective-permute-start | bytes 1769480 | tf_op jit(solution)/shard_map/ppermute | solution.py:53
  86.2 34.2 %collective-permute-start.21 = (bf16[384,768]{1,0:T(8,128)(2,1)}, bf16[384,768]{1,0:T(8,128)(2,1)S(1)}, u32[]{:S(2)}, u32[]{:S(2)}) collective-permute-start(bf16[384,768]{1,0:T(8,128)(2,1)} %collective-permute-done.16.refs_4_.refs_20_.refs_36_), channel_id=1, source_target_pairs={{0,1},{1,0},{2,3},{3,2},{4,5},{5,4},{6,7},{7,6},{8,9},{9,8},{10,11... | collective-permute-start | bytes 1769480 | tf_op jit(solution)/shard_map/ppermute | solution.py:53
  98.7 21.6 %collective-permute-start.25 = (bf16[384,768]{1,0:T(8,128)(2,1)}, bf16[384,768]{1,0:T(8,128)(2,1)S(1)}, u32[]{:S(2)}, u32[]{:S(2)}) collective-permute-start(bf16[384,768]{1,0:T(8,128)(2,1)} %collective-permute-done.17.refs_8_.refs_24_.refs_40_), channel_id=1, source_target_pairs={{0,2},{1,3},{2,0},{3,1},{4,6},{5,7},{6,4},{7,5},{8,10},{9,11},{10,... | collective-permute-start | bytes 1769480 | tf_op jit(solution)/shard_map/ppermute | solution.py:53
  151.3 40.5 %collective-permute-start.35 = (bf16[320,768]{1,0:T(8,128)(2,1)S(1)}, bf16[320,768]{1,0:T(8,128)(2,1)S(1)}, u32[]{:S(2)}, u32[]{:S(2)}) collective-permute-start(bf16[320,768]{1,0:T(8,128)(2,1)S(1)} %get-tuple-element.131.refs_0_), channel_id=1, source_target_pairs={{16,18},{17,19},{18,16},{19,17},{20,22},{21,23},{22,20},{23,21},{2... | collective-permute-start | bytes 1474568 | tf_op jit(solution)/shard_map/ppermute | solution.py:83
  169.7 23.8 %collective-permute-start.36 = (bf16[2,320,768]{2,1,0:T(8,128)(2,1)S(1)}, bf16[2,320,768]{2,1,0:T(8,128)(2,1)S(1)}, u32[]{:S(2)}, u32[]{:S(2)}) collective-permute-start(bf16[2,320,768]{2,1,0:T(8,128)(2,1)S(1)} %get-tuple-element.103), channel_id=1, source_target_pairs={{0,2},{1,3},{2,0},{3,1},{4,6},{5,7},{6,4},{7,5},{8,10},{9,11},{10,... | collective-permute-start | bytes 2949128 | tf_op jit(solution)/shard_map/ppermute | solution.py:53
  193.5 24.7 %collective-permute-start.40 = (bf16[320,768]{1,0:T(8,128)(2,1)S(1)}, bf16[320,768]{1,0:T(8,128)(2,1)S(1)}, u32[]{:S(2)}, u32[]{:S(2)}) collective-permute-start(bf16[320,768]{1,0:T(8,128)(2,1)S(1)} %get-tuple-element.106), channel_id=1, source_target_pairs={{0,1},{1,0},{2,3},{3,2},{4,5},{5,4},{6,7},{7,6},{8,9},{9,8},{10,11... | collective-permute-start | bytes 1474568 | tf_op jit(solution)/shard_map/ppermute | solution.py:53
  216.9 38.5 %collective-permute-start.45 = (bf16[320,768]{1,0:T(8,128)(2,1)S(1)}, bf16[320,768]{1,0:T(8,128)(2,1)S(1)}, u32[]{:S(2)}, u32[]{:S(2)}) collective-permute-start(bf16[320,768]{1,0:T(8,128)(2,1)S(1)} %collective-permute-done.39), channel_id=1, source_target_pairs={{16,0},{17,1},{18,2},{19,3},{20,4},{21,5},{22,6},{23,7},{24,8},{25... | collective-permute-start | bytes 1474568 | tf_op jit(solution)/shard_map/ppermute | solution.py:731
  218.2 16.3 %collective-permute-start.43 = (bf16[2,320,192]{2,1,0:T(8,128)(2,1)S(1)}, bf16[2,320,192]{2,1,0:T(8,128)(2,1)S(1)}, u32[]{:S(2)}, u32[]{:S(2)}) collective-permute-start(bf16[2,320,192]{2,1,0:T(8,128)(2,1)S(1)} %get-tuple-element.112), channel_id=1, source_target_pairs={{0,2},{1,3},{2,0},{3,1},{4,6},{5,7},{6,4},{7,5},{8,10},{9,11},{10,... | collective-permute-start | bytes 737288 | tf_op jit(solution)/shard_map/ppermute | solution.py:53
  219.9 19.6 %collective-permute-start.42 = (bf16[320,768]{1,0:T(8,128)(2,1)S(1)}, bf16[320,768]{1,0:T(8,128)(2,1)S(1)}, u32[]{:S(2)}, u32[]{:S(2)}) collective-permute-start(bf16[320,768]{1,0:T(8,128)(2,1)S(1)} %get-tuple-element.127.refs_0_), channel_id=1, source_target_pairs={{0,2},{1,3},{2,0},{3,1},{4,6},{5,7},{6,4},{7,5},{8,10},{9,11},{10,... | collective-permute-start | bytes 1474568 | tf_op jit(solution)/shard_map/ppermute | solution.py:53
  221.2 36.8 %collective-permute-start.44 = (bf16[320,768]{1,0:T(8,128)(2,1)}, bf16[320,768]{1,0:T(8,128)(2,1)}, u32[]{:S(2)}, u32[]{:S(2)}) collective-permute-start(bf16[320,768]{1,0:T(8,128)(2,1)} %broadcast_select_fusion.4.dy_ref.refs_0_), channel_id=1, source_target_pairs={{0,1},{1,0},{2,3},{3,2},{4,5},{5,4},{6,7},{7,6},{8,9},{9,8},{10,11... | collective-permute-start | bytes 1474568 | tf_op jit(solution)/shard_map/ppermute | solution.py:53
  232.8 37.5 %collective-permute-start.54 = (bf16[2,320,768]{2,1,0:T(8,128)(2,1)}, bf16[2,320,768]{2,1,0:T(8,128)(2,1)}, u32[]{:S(2)}, u32[]{:S(2)}) collective-permute-start(bf16[2,320,768]{2,1,0:T(8,128)(2,1)} %get-tuple-element.130), channel_id=1, source_target_pairs={{0,2},{1,3},{2,0},{3,1},{4,6},{5,7},{6,4},{7,5},{8,10},{9,11},{10,... | collective-permute-start | bytes 2949128 | tf_op jit(solution)/shard_map/ppermute | solution.py:53
  258.9 24.3 %collective-permute-start.51 = (bf16[320,768]{1,0:T(8,128)(2,1)S(1)}, bf16[320,768]{1,0:T(8,128)(2,1)S(1)}, u32[]{:S(2)}, u32[]{:S(2)}) collective-permute-start(bf16[320,768]{1,0:T(8,128)(2,1)S(1)} %copy-done.18), channel_id=1, source_target_pairs={{0,1},{1,0},{2,3},{3,2},{4,5},{5,4},{6,7},{7,6},{8,9},{9,8},{10,11... | collective-permute-start | bytes 1474568 | tf_op jit(solution)/shard_map/ppermute | solution.py:53
  259.2 24.2 %collective-permute-start.53 = (bf16[320,768]{1,0:T(8,128)(2,1)}, bf16[320,768]{1,0:T(8,128)(2,1)S(1)}, u32[]{:S(2)}, u32[]{:S(2)}) collective-permute-start(bf16[320,768]{1,0:T(8,128)(2,1)} %copy-done.31), channel_id=1, source_target_pairs={{0,1},{1,0},{2,3},{3,2},{4,5},{5,4},{6,7},{7,6},{8,9},{9,8},{10,11... | collective-permute-start | bytes 1474568 | tf_op jit(solution)/shard_map/ppermute | solution.py:53
  281.6 20.4 %collective-permute-start.49 = (bf16[2,320,576]{2,1,0:T(8,128)(2,1)S(1)}, bf16[2,320,576]{2,1,0:T(8,128)(2,1)S(1)}, u32[]{:S(2)}, u32[]{:S(2)}) collective-permute-start(bf16[2,320,576]{2,1,0:T(8,128)(2,1)S(1)} %get-tuple-element.125), channel_id=1, source_target_pairs={{0,2},{1,3},{2,0},{3,1},{4,6},{5,7},{6,4},{7,5},{8,10},{9,11},{10,... | collective-permute-start | bytes 2211848 | tf_op jit(solution)/shard_map/ppermute | solution.py:53
  293.8 18.7 %collective-permute-start.60 = (bf16[320,768]{1,0:T(8,128)(2,1)}, bf16[320,768]{1,0:T(8,128)(2,1)S(1)}, u32[]{:S(2)}, u32[]{:S(2)}) collective-permute-start(bf16[320,768]{1,0:T(8,128)(2,1)} %get-tuple-element.120.refs_8_), channel_id=1, source_target_pairs={{0,1},{1,0},{2,3},{3,2},{4,5},{5,4},{6,7},{7,6},{8,9},{9,8},{10,11... | collective-permute-start | bytes 1474568 | tf_op jit(solution)/shard_map/ppermute | solution.py:53
  293.9 18.6 %collective-permute-start.61 = (bf16[320,768]{1,0:T(8,128)(2,1)}, bf16[320,768]{1,0:T(8,128)(2,1)S(1)}, u32[]{:S(2)}, u32[]{:S(2)}) collective-permute-start(bf16[320,768]{1,0:T(8,128)(2,1)} %collective-permute-done.47.refs_10_), channel_id=1, source_target_pairs={{0,1},{1,0},{2,3},{3,2},{4,5},{5,4},{6,7},{7,6},{8,9},{9,8},{10,11... | collective-permute-start | bytes 1474568 | tf_op jit(solution)/shard_map/ppermute | solution.py:53
  321.2 27.1 %collective-permute-start.34 = (bf16[320,768]{1,0:T(8,128)(2,1)S(1)}, bf16[320,768]{1,0:T(8,128)(2,1)S(1)}, u32[]{:S(2)}, u32[]{:S(2)}) collective-permute-start(bf16[320,768]{1,0:T(8,128)(2,1)S(1)} %get-tuple-element.93.refs_0_), channel_id=1, source_target_pairs={{0,1},{1,0},{2,3},{3,2},{4,5},{5,4},{6,7},{7,6},{8,9},{9,8},{10,11... | collective-permute-start | bytes 1474568 | tf_op jit(solution)/shard_map/ppermute | solution.py:53
  321.2 24.3 %collective-permute-start.72 = (bf16[320,768]{1,0:T(8,128)(2,1)}, bf16[320,768]{1,0:T(8,128)(2,1)S(1)}, u32[]{:S(2)}, u32[]{:S(2)}) collective-permute-start(bf16[320,768]{1,0:T(8,128)(2,1)} %copy-done.1), channel_id=1, source_target_pairs={{0,1},{1,0},{2,3},{3,2},{4,5},{5,4},{6,7},{7,6},{8,9},{9,8},{10,11... | collective-permute-start | bytes 1474568 | tf_op jit(solution)/shard_map/ppermute | solution.py:53
  324.8 18.9 %collective-permute-start.77 = (bf16[192,768]{1,0:T(8,128)(2,1)S(1)}, bf16[192,768]{1,0:T(8,128)(2,1)S(1)}, u32[]{:S(2)}, u32[]{:S(2)}) collective-permute-start(bf16[192,768]{1,0:T(8,128)(2,1)S(1)} %fusion.4), channel_id=1, source_target_pairs={{0,4},{4,8},{8,12},{12,0},{1,5},{5,9},{9,13},{13,1},{2,6},{6,10},{... | collective-permute-start | bytes 884744 | tf_op jit(solution)/shard_map/ppermute | solution.py:58
  (125 other events, 1665.6 us)

commit v3 on v2

--- a/solution.py
+++ b/solution.py
@@ -19,11 +19,12 @@
     "layer": 40,
     "both_back": 40,
     "hidden_back": 30,
-    "attend_back": 22,
+    "attend_back": 32,
     "input_back": 22,
-    "weight_grad": 18,
+    "weight_grad": 24,
     "place": 12,
     "norm": 8,
+    "finish": 12,
 }
 COST = {
     "params": 0.5,
@@ -34,10 +35,11 @@
     "both_back": 40,
     "hidden_back": 40,
     "attend_back": 40,
-    "input_back": 1,
+    "input_back": 40,
     "weight_grad": 0.5,
     "place": 0.5,
     "norm": 1,
+    "finish": 1,
 }
 LOG2E = 1.4426950408889634
 START = (0, 0, 1)
@@ -481,23 +483,33 @@
 
 
 def weight_kernel(n, pairs, *refs):
-    out_ref = refs[-1]
-    sums_ref = refs[-2] if len(refs) == 2 * MASKS * pairs + 2 else None
-    part = refs[0].shape[1] // n
+    count = 2 * MASKS * pairs
+    blocks, out_ref, held, sems = refs[:count], refs[-count - 2], refs[-count - 1 : -1], refs[-1]
+    sums_ref = refs[count] if len(refs) == 2 * count + 3 else None
+    copies = {}
+    for pair in range(pairs):
+        for mask in range(MASKS):
+            for side in range(2):
+                i = (2 * pair + side) * MASKS + mask
+                block = blocks[i].at[0] if len(blocks[i].shape) == 3 else blocks[i]
+                copies[i] = pltpu.make_async_copy(block, held[i], sems.at[i])
+                copies[i].start()
+    part = held[0].shape[1] // n
+    width = held[MASKS].shape[1] // 3
     at = 0
     for pair in range(pairs):
-        left = refs[2 * MASKS * pair : 2 * MASKS * pair + MASKS]
-        right = refs[2 * MASKS * pair + MASKS : 2 * MASKS * (pair + 1)]
         acc = None
         for mask in range(MASKS):
-            term = dot_tn(left[mask][...], right[mask][0] if right[mask].ndim == 3 else right[mask][...])
+            left, right = 2 * pair * MASKS + mask, (2 * pair + 1) * MASKS + mask
+            copies[left].wait()
+            copies[right].wait()
+            term = dot_tn(held[left][...], held[right][...])
             acc = term if acc is None else acc + term
         cols = acc.shape[1]
         for block in range(n):
             out_ref[block, :part, at : at + cols] = acc[block * part : (block + 1) * part].astype(BF16)
         at += cols
     if sums_ref is not None:
-        width = refs[2 * MASKS - 1].shape[1] // 3
         slim = width // n
         sums = sums_ref[...]
         for block in range(n):
@@ -516,6 +528,25 @@
     values, out_ref = refs[:MASKS], refs[MASKS]
     for mask in range(MASKS):
         out_ref[index_ref[1] ^ mask] = values[mask][...].astype(out_ref.dtype)
+
+
+def finish_kernel(n, index_ref, got_ref, block_ref, qkv_ref, out_ref, gains_ref, biases_ref, qv_ref, fb_ref):
+    part, width = qkv_ref.shape[1:]
+    total = got_ref[...].astype(F32) + block_ref[...].astype(F32)
+    for i in range(3):
+        qkv_ref[i] = total[:part, i * width : (i + 1) * width]
+    out_ref[...] = total[:part, 3 * width :].T
+    small = total[part:, :part]
+    gains_ref[...] = jnp.concatenate([small[8:9], small[1:2]], axis=0)
+    biases_ref[...] = jnp.concatenate([small[9:10], small[2:4], small[0:1]], axis=0)
+    slim = width // n
+    for owner in range(MASKS):
+
+        @pl.when(index_ref[1] == owner)
+        def _():
+            fb_ref[...] = small[4 + owner : 5 + owner]
+            row = small[12 + owner : 13 + owner]
+            qv_ref[...] = jnp.concatenate([row[:, :slim], row[:, slim : 2 * slim]], axis=0)
 
 
 def shape(dims, dtype):
@@ -646,16 +677,18 @@
         )(after(index, *events), s["x"], dr, vec, dq, own, recv, *pa)
         return dx, rest[:3], rest[3]
 
-    def weight_grad(pairs, event, sums=None):
-        cols = sum(right[0].shape[1] for _, right in pairs)
+    def weight_grad(pairs, events, sums=None):
+        cols = sum(right[0].shape[-1] for _, right in pairs)
         blocks = [block for left, right in pairs for block in (*left, *right)]
-        blocks[0] = after(blocks[0], event)
+        held = [pltpu.VMEM(block.shape[-2:], BF16) for block in blocks]
+        blocks = [pltpu.with_memory_space_constraint(block, pltpu.HBM) for block in blocks]
+        blocks[0] = after(blocks[0], *events)
         more = [] if sums is None else [sums]
         return call(
             functools.partial(weight_kernel, n, len(pairs)),
-            [VMEM] * (len(blocks) + len(more)),
+            [HBM] * len(blocks) + [VMEM] * len(more),
             shape((n, part + 16 * len(more), cols), BF16),
-            [],
+            held + [pltpu.SemaphoreType.DMA((len(blocks),))],
             "weight_grad",
         )(*blocks, *more)
 
@@ -687,14 +720,15 @@
     rows.append(ring_next(rows[0]))
     across_2.append(flip_chip(after(rows_2[0], across[0])))
     rows.append(ring_next(after(rows[1], across[0])))
-    rows_2.append(ring_next(after(rows_2[0], rows[2])))
     for step in range(3, n):
-        rows.append(ring_next(after(rows[-1], across_2[0])))
+        rows.append(ring_next(rows[-1]))
     across += [flip_chip(row) for row in rows[1:]]
+    rows_2.append(ring_next(after(rows_2[0], across[1], across_2[0])))
     for step in range(2, n):
         rows_2.append(ring_next(rows_2[-1]))
     across_2.append(flip_chip(after(rows_2[1], across[-2])))
-    across_2 += [flip_chip(row) for row in rows_2[2:]]
+    for row in rows_2[2:]:
+        across_2.append(flip_chip(after(row, across_2[-1])))
     pa = all_pieces(rows, across)
 
     vec, fb, qkvb = read_params(pa)
@@ -707,7 +741,7 @@
         (real, act),
         [kv_scratch, w_scratch, w_sems],
         "attend",
-    )(index, x_clip, vec, after(q, rows_2[-2], normed_far), kv, flip_core(kv), *pa)
+    )(index, x_clip, vec, after(q, across_2[1], normed_far), kv, flip_core(kv), *pa)
     p1 = p2 = all_pieces(rows_2, across_2[:-1] + [after(across_2[-1], c)])
     mid = call(
         functools.partial(hidden_kernel, n),
@@ -729,31 +763,30 @@
     relayed = lax.ppermute(dx, "section", [(1, 0)])
     dx_across = flip_within(dx, 2, 1)
     relayed_across = lax.ppermute(after(dx_across, relayed), "section", [(1, 0)])
-    c_all = spread(after(kept["c"], dx_across))
-    o_all = trade(kept["o"][:2] + [after(kept["o"][2], dx_across)])
+    c_all = spread(after(kept["c"], e_all[2]))
+    o_all = trade(kept["o"][:2] + [after(kept["o"][2], dx)])
     dy = jnp.where(first, relayed, out_grad)
     dy_across = jnp.where(first, relayed_across, clip_part(cotangent, 1 - slot, half))
 
-    du, dr, da, do, sums = hidden_back(dy, kept, dx_across, e_all[1], e_all[3])
+    du, dr, da, do, sums = hidden_back(dy, kept, dx_across, e_all[1], e_all[3], c_all[2])
     du_all = trade(du)
     far = after(dy_across, dr)
     dm_all = [dy, flip_core(dy), far, flip_core(far)]
-    dq, own, peer = attend_back(do, kept, c_all[2], o_all[2])
+    dq, own, peer = attend_back(do, kept, o_all[2])
     recv = flip_core(peer)
     da_all = spread(da)
-    blocks_2 = weight_grad([(dm_all, e_all)], dq)
-    dx, dqkv, sums_one = input_back(dr, dq, own, recv, kept, blocks_2, da_all[2])
+    blocks_2 = weight_grad([(dm_all, e_all)], (dq, du_all[2]))
+    dx, dqkv, sums_one = input_back(dr, dq, own, recv, kept, blocks_2)
     dqkv_all = trade(dqkv)
     grad_2, got_2 = ring_scatter(blocks_2, me, {1: (dx,)})
     sums = jnp.concatenate([sums, sums_one], axis=0)
     sums = sums + flip_core(sums)
     sums = sums + flip_chip(sums)
-    blocks_1 = weight_grad([(c_all, du_all)], dx)
+    blocks_1 = weight_grad([(c_all, du_all)], (dx, da_all[2]))
     grad_1, got_1 = ring_scatter(blocks_1, me)
     normed_across = jnp.where(first, normed_far, normed_across)
     normed_all = [kept["normed"], flip_core(kept["normed"]), normed_across, flip_core(normed_across)]
-    sums = after(sums, got_2[-1], got_1[0])
-    blocks_a = weight_grad([(normed_all, dqkv_all), (da_all, o_all)], blocks_1, sums)
+    blocks_a = weight_grad([(normed_all, dqkv_all), (da_all, o_all)], (blocks_1, got_2[-1], got_1[0]), sums)
     steps = ring_steps(blocks_a, me)
     got = next(steps)
     last = flip_chip(after(jnp.where(first, dx, y), dqkv_all[2], da_all[2]))
@@ -762,32 +795,34 @@
     dx_across = jnp.where(first, last, dx_across)
     hidden_states = whole([y, flip_core(y), y_across, flip_core(y_across)], BF16)
     grad_inputs = whole([dx, flip_core(dx), dx_across, flip_core(dx_across)], F32)
-    for step in range(1, n):
-        if step == n - 1:
-            got = after(got, hidden_states, grad_inputs)
-        got = steps.send(got)
-    grad_a = got
-
-    mine = grad_a[part:, :part]
-    grad_a = grad_a[:part]
-    grad_gains = jnp.stack([mine[8], mine[1]])[None]
-    grad_biases = jnp.stack([mine[9], mine[2], mine[3], mine[0]])[None]
-    grad_fb = lax.dynamic_slice(mine, (4 + tensor, 0), (1, part))[None]
-    slim = width // n
-    grad_qv = lax.dynamic_slice(mine, (12 + tensor, 0), (1, 2 * slim)).reshape(1, 2, 1, slim)
-
-    grad_qkv = jnp.stack([grad_a[:, i * width : (i + 1) * width] for i in range(3)])[None]
+    for step in range(1, n - 1):
+        got = steps.send(after(got, hidden_states, grad_inputs) if step == n - 2 else got)
+    block = lax.dynamic_index_in_dim(blocks_a, me, 0, keepdims=False)
+    grad_qkv, grad_out, grad_gains, grad_biases, grad_qv, grad_fb = call(
+        functools.partial(finish_kernel, n),
+        [SMEM, VMEM, VMEM],
+        (
+            shape((3, part, width), F32),
+            shape((width, part), F32),
+            shape((2, part), F32),
+            shape((4, part), F32),
+            shape((2, width // n), F32),
+            shape((1, part), F32),
+        ),
+        [],
+        "finish",
+    )(index, got, block)
     return (
         hidden_states,
         grad_inputs,
-        grad_qkv,
-        grad_a[:, 3 * width :].T[None],
+        grad_qkv[None],
+        grad_out[None],
         grad_1[None],
         grad_2.T[None],
-        grad_gains,
-        grad_biases,
-        grad_qv,
-        grad_fb,
+        grad_gains[None],
+        grad_biases[None],
+        grad_qv[None, :, None],
+        grad_fb[None],
     )
 
 

time: 365 us -> 359 us (0.984)
  waiting for transfers between devices: 160 us -> 148 us
  Pallas kernels: 121 us -> 129 us
    ppermute x15, waiting for transfers between devices: 70.5 us -> 58.9 us  [ring_next(): lax.ppermute(value, 'dp', [(i, (i + 1) % count) for i in range(count)])]
    pallas_call x3 -> x4, Pallas kernels: 12.5 us -> 19.6 us  [the longest x3 17.9 us: weight_grad(): call(functools.partial(weight_kernel, n, len(pairs)), [HBM] * len(blocks)...]
    unnamed x145 -> x156, local copies, waits for them, and re-layouts: 9.99 us -> 9.75 us
  transfers between devices with their start and end apart: 78 -> 78, of which waited for: 33 -> 34; matrix products, arithmetic and copies ran while one was open for 4% -> 4% of each run, Pallas kernels for 32% -> 34%
where the time goes in v3:
time: 359 us; the launch traced here: 354 us
  waiting for transfers between devices  148 us (41%)
  Pallas kernels  129 us (36%)
  starting transfers between devices  44.3 us (12%)
  local copies, waits for them, and re-layouts  16.1 us (4%)
  other arithmetic  11.1 us (3%)
  between operations  6.06 us (2%)
    ppermute x57, waiting for transfers between devices, flip(): return lax.ppermute(value, 'tensor', [(i, i ^ mask) for i in range(count)])  67.2 us
    ppermute x15, waiting for transfers between devices, ring_next(): lax.ppermute(value, 'dp', [(i, (i + 1) % count) for i in range(count)])  58.9 us
    ppermute x57, starting transfers between devices, flip(): return lax.ppermute(value, 'tensor', [(i, i ^ mask) for i in range(count)])  27.8 us
    pallas_call x1, Pallas kernels, both_back(): call(functools.partial(both_back_kernel, n), [SMEM] + [VMEM] * 8 + [HBM]...  21.8 us
    pallas_call x3, Pallas kernels, weight_grad(): call(functools.partial(weight_kernel, n, len(pairs)), [HBM] * len(blocks)...  17.9 us
    pallas_call x1, Pallas kernels, forward(): call(functools.partial(layer_kernel, n), [SMEM] + [VMEM] * 6 + many * 3,...  15.5 us
    pallas_call x1, Pallas kernels, attend_back(): call(attend_back_kernel, [VMEM] * 5 + [HBM], (head_act, pair_act, pair_ac...  15 us
    ppermute x1, waiting for transfers between devices, local(): relayed = lax.ppermute(dx, 'section', [(1, 0)])  14.5 us
  transfers between devices with their start and end apart: 78, of which 34 were waited for; matrix products, arithmetic and copies ran while one was open for 4% of the time, Pallas kernels for 34%

profile of v3, /device:TPU:0, one launch (start us, length us, event | category | flops | bytes accessed | tf_op | source)
XLA Modules:
  0.0 354.0 jit_solution(17841648574289113306)
XLA Ops:
  20.5 9.5 %collective-permute-done.7.refs_8_.refs_40_ = bf16[208,768]{1,0:T(8,128)(2,1)} collective-permute-done((bf16[208,768]{1,0:T(8,128)(2,1)S(1)}, bf16[208,768]{1,0:T(8,128)(2,1)}, u32[]{:S(2)}, u32[]{:S(2)}) %collective-permute-start.7) | collective-permute-done | bytes 319520 | tf_op jit(solution)/shard_map/ppermute | solution.py:60
  30.1 8.3 %collective-permute-done.5.refs_6_.refs_38_ = bf16[208,768]{1,0:T(8,128)(2,1)} collective-permute-done((bf16[208,768]{1,0:T(8,128)(2,1)S(1)}, bf16[208,768]{1,0:T(8,128)(2,1)}, u32[]{:S(2)}, u32[]{:S(2)}) %collective-permute-start.5) | collective-permute-done | bytes 319520 | tf_op jit(solution)/shard_map/ppermute | solution.py:55
  43.9 8.0 %collective-permute-done.9.refs_10_.refs_42_ = bf16[208,768]{1,0:T(8,128)(2,1)} collective-permute-done((bf16[208,768]{1,0:T(8,128)(2,1)}, bf16[208,768]{1,0:T(8,128)(2,1)}, u32[]{:S(2)}, u32[]{:S(2)}) %collective-permute-start.9) | collective-permute-done | bytes 319520 | tf_op jit(solution)/shard_map/ppermute | solution.py:55
  51.9 6.0 %collective-permute-done.13.refs_14_.refs_46_ = bf16[208,768]{1,0:T(8,128)(2,1)} collective-permute-done((bf16[208,768]{1,0:T(8,128)(2,1)}, bf16[208,768]{1,0:T(8,128)(2,1)}, u32[]{:S(2)}, u32[]{:S(2)}) %collective-permute-start.13) | collective-permute-done | bytes 319520 | tf_op jit(solution)/shard_map/ppermute | solution.py:55
  68.0 5.9 %qkv.2 = (bf16[320,768]{1,0:T(8,128)(2,1)}, bf16[4,320,192]{2,1,0:T(8,128)(2,1)S(1)}, bf16[4,320,384]{2,1,0:T(8,128)(2,1)S(1)}) custom-call(s32[2]{0:T(128)S(1)} %pad_add_fusion.index_ref.me_ref, bf16[320,768]{1,0:T(8,128)(2,1)S(1)} %get-tuple-element.165.x_ref, f32[8,768]{1,0:T(8,128)S(1)} %get-tuple-element.83.vec_ref, ...), custom_call_target="tpu_custom_call" | custom-call | flops 46000001024 | bytes 1 | tf_op jit(solution)/shard_map/qkv/pallas_call | solution.py:609
  83.2 12.4 %collective-permute-done.25.refs_10_.refs_26_.refs_42_ = bf16[384,768]{1,0:T(8,128)(2,1)S(1)} collective-permute-done((bf16[384,768]{1,0:T(8,128)(2,1)S(1)}, bf16[384,768]{1,0:T(8,128)(2,1)S(1)}, u32[]{:S(2)}, u32[]{:S(2)}) %collective-permute-start.25) | collective-permute-done | bytes 589856 | tf_op jit(solution)/shard_map/ppermute | solution.py:55
  99.4 9.5 %attend.1 = (f32[320,768]{1,0:T(8,128)S(1)}, bf16[320,768]{1,0:T(8,128)(2,1)S(1)}) custom-call(s32[2]{0:T(128)S(1)} %pad_add_fusion.index_ref.me_ref, bf16[320,768]{1,0:T(8,128)(2,1)S(1)} %get-tuple-element.165.x_ref, f32[8,768]{1,0:T(8,128)S(1)} %get-tuple-element.83.vec_ref, bf16[4,320,192]{2,1,0:T(8,128)(2,1)S(1)} %get-tuple-element.89.q_ref, ...), custom_call_target="tpu_custom_call" | custom-call | flops 46000001024 | bytes 1 | tf_op jit(solution)/shard_map/attend/pallas_call | solution.py:738
  119.0 6.4 %hidden.1 = bf16[320,768]{1,0:T(8,128)(2,1)S(1)} custom-call(s32[2]{0:T(128)S(1)} %pad_add_fusion.index_ref.me_ref, f32[320,768]{1,0:T(8,128)S(1)} %get-tuple-element.91.r_ref, bf16[320,768]{1,0:T(8,128)(2,1)S(1)} %get-tuple-element.92.c_ref, f32[8,768]{1,0:T(8,128)S(1)} %get-tuple-element.83.vec_ref, f32[4,768]{1,0:T(4,128)S(1)} %get-tuple-element.93.fb_ref, ...), custom_call_target="tpu_custom_call" | custom-call | flops 46000001024 | bytes 1 | tf_op jit(solution)/shard_map/hidden/pallas_call | solution.py:746
  132.3 7.3 %collective-permute-done.31 = bf16[320,768]{1,0:T(8,128)(2,1)S(1)} collective-permute-done((bf16[320,768]{1,0:T(8,128)(2,1)S(1)}, bf16[320,768]{1,0:T(8,128)(2,1)S(1)}, u32[]{:S(2)}, u32[]{:S(2)}) %collective-permute-start.31) | collective-permute-done | bytes 491552 | tf_op jit(solution)/shard_map/ppermute | solution.py:754
  147.5 15.5 %layer.1 = (bf16[320,768]{1,0:T(8,128)(2,1)S(1)}, f32[320,768]{1,0:T(8,128)S(1)}, bf16[320,768]{1,0:T(8,128)(2,1)}, bf16[320,192]{1,0:T(8,128)(2,1)S(1)}, bf16[3...) custom-call(s32[2]{0:T(128)S(1)} %pad_add_fusion.index_ref.me_ref, ...), custom_call_target="tpu_custom_call" | custom-call | flops 46000001024 | bytes 1 | tf_op jit(solution)/shard_map/layer/pallas_call | solution.py:627
  165.4 21.8 %both_back.1 = (f32[320,768]{1,0:T(8,128)S(1)}, bf16[4,320,192]{2,1,0:T(8,128)(2,1)S(1)}, bf16[4,320,384]{2,1,0:T(8,128)(2,1)S(1)}, bf16[4,320,384]{2,1,0:T(8,128)(2,1)S(1)}) custom-call(s32[2]{0:T(128)S(1)} %pad_add_fusion.index_ref.me_ref, bf16[320,768]{1,0:T(8,128)(2,1)S(1)} %dynamic-slice_bitcast_fusion.dy_ref, f32[320,768]{1,0:T(8,128)S(1)} %get-tuple-element.101.r_ref, ...), custom_call_target="tpu_custom_call" | custom-call | flops 46000001024 | bytes 1 | tf_op jit(solution)/shard_map/both_back/pallas_call | solution.py:640
  190.3 5.8 %input_back.2 = (bf16[320,768]{1,0:T(8,128)(2,1)S(1)}, bf16[320,576]{1,0:T(8,128)(2,1)}, bf16[320,576]{1,0:T(8,128)(2,1)}, bf16[2,320,576]{2,1,0:T(8,128)(2,1)}, f32[8,768]{1,0:T(8,128)}) custom-call(s32[2]{0:T(128)S(1)} %pad_add_fusion.index_ref.me_ref, bf16[320,768]{1,0:T(8,128)(2,1)S(1)} %broadcast_select_fusion.5.x_ref, ...), custom_call_target="tpu_custom_call" | custom-call | flops 46000001024 | bytes 1 | tf_op jit(solution)/shard_map/input_back/pallas_call | solution.py:671
  198.4 14.5 %collective-permute-done.38 = bf16[320,768]{1,0:T(8,128)(2,1)S(1)} collective-permute-done((bf16[320,768]{1,0:T(8,128)(2,1)S(1)}, bf16[320,768]{1,0:T(8,128)(2,1)S(1)}, u32[]{:S(2)}, u32[]{:S(2)}) %collective-permute-start.38) | collective-permute-done | bytes 491552 | tf_op jit(solution)/shard_map/ppermute | solution.py:763
  215.7 9.9 %hidden_back.1 = (bf16[320,768]{1,0:T(8,128)(2,1)S(1)}, bf16[320,768]{1,0:T(8,128)(2,1)S(1)}, bf16[2,320,768]{2,1,0:T(8,128)(2,1)S(1)}, f32[320,768]{1,0:T(8,128...) custom-call(s32[2]{0:T(128)S(1)} %pad_add_fusion.index_ref.me_ref, ...), custom_call_target="tpu_custom_call" | custom-call | flops 46000001024 | bytes 1 | tf_op jit(solution)/shard_map/hidden_back/pallas_call | solution.py:652
  228.7 15.0 %attend_back.1 = (bf16[4,320,192]{2,1,0:T(8,128)(2,1)S(1)}, bf16[4,320,384]{2,1,0:T(8,128)(2,1)S(1)}, bf16[4,320,384]{2,1,0:T(8,128)(2,1)}) custom-call(bf16[4,320,192]{2,1,0:T(8,128)(2,1)S(1)} %get-tuple-element.120.do_ref, bf16[4,320,192]{2,1,0:T(8,128)(2,1)S(1)} %get-tuple-element.97.q_ref, bf16[4,320,384]{2,1,0:T(8,128)(2,1)S(1)} %get-tuple-element.99.kv_own_ref, ...), custom_call_target="tpu_custom_call" | custom-call | flops 46000001024 | bytes 1 | tf_op jit(solution)/shard_map/attend_back/pallas_call | solution.py:662
  252.1 5.4 %weight_grad.3 = bf16[4,192,768]{2,1,0:T(8,128)(2,1)S(1)} custom-call(bf16[320,768]{1,0:T(8,128)(2,1)} %copy-done.3, bf16[320,768]{1,0:T(8,128)(2,1)} %collective-permute-done.45.refs_1_, bf16[320,768]{1,0:T(8,128)(2,1)} %bitcast_select_fusion.refs_2_, bf16[320,768]{1,0:T(8,128)(2,1)} %collective-permute-done.47.refs_3_, bf16[320,768]{1,0:T(8,128)(2,1)} %copy-done.10, ...), custom_call_target="tpu_custom_call" | custom-call | flops 575000000 | bytes 1 | tf_op jit(solution)/shard_map/weight_grad/pallas_call | solution.py:687
  257.6 6.4 %input_back.3 = (bf16[320,768]{1,0:T(8,128)(2,1)}, bf16[320,576]{1,0:T(8,128)(2,1)S(1)}, bf16[320,576]{1,0:T(8,128)(2,1)S(1)}, bf16[2,320,576]{2,1,0:T(8,128)(2,1)S(1)}, f32[8,768]{1,0:T(8,128)S(1)}) custom-call(s32[2]{0:T(128)S(1)} %pad_add_fusion.index_ref.me_ref, bf16[320,768]{1,0:T(8,128)(2,1)S(1)} %copy-done.8, f32[320,768]{1,0:T(8,128)S(1)} %copy-done.18, ...), custom_call_target="tpu_custom_call" | custom-call | flops 46000001024 | bytes 1 | tf_op jit(solution)/shard_map/input_back/pallas_call | solution.py:671
  271.9 5.2 %weight_grad.4 = bf16[4,192,768]{2,1,0:T(8,128)(2,1)S(1)} custom-call(bf16[320,768]{1,0:T(8,128)(2,1)} %get-tuple-element.135.refs_0_, bf16[320,768]{1,0:T(8,128)(2,1)} %copy-done.43, bf16[320,768]{1,0:T(8,128)(2,1)} %collective-permute-done.42.refs_2_, bf16[320,768]{1,0:T(8,128)(2,1)} %copy-done.44, bf16[320,768]{1,0:T(8,128)(2,1)} %copy-done.9, ...), custom_call_target="tpu_custom_call" | custom-call | flops 575000000 | bytes 1 | tf_op jit(solution)/shard_map/weight_grad/pallas_call | solution.py:687
  282.9 7.0 %collective-permute-done.49.refs_6_ = bf16[2,320,576]{2,1,0:T(8,128)(2,1)S(1)} collective-permute-done((bf16[2,320,576]{2,1,0:T(8,128)(2,1)S(1)}, bf16[2,320,576]{2,1,0:T(8,128)(2,1)S(1)}, u32[]{:S(2)}, u32[]{:S(2)}) %collective-permute-start.49) | collective-permute-done | bytes 737312 | tf_op jit(solution)/shard_map/ppermute | solution.py:55
  291.6 7.7 %collective-permute-done.58 = bf16[192,768]{1,0:T(8,128)(2,1)S(1)} collective-permute-done((bf16[192,768]{1,0:T(8,128)(2,1)S(1)}, bf16[192,768]{1,0:T(8,128)(2,1)S(1)}, u32[]{:S(2)}, u32[]{:S(2)}) %collective-permute-start.58) | collective-permute-done | bytes 294944 | tf_op jit(solution)/shard_map/ppermute | solution.py:60
  302.6 7.3 %weight_grad.5 = bf16[4,208,768]{2,1,0:T(8,128)(2,1)S(1)} custom-call(bf16[320,768]{1,0:T(8,128)(2,1)} %copy-done.4, bf16[320,768]{1,0:T(8,128)(2,1)} %copy-done.36, bf16[320,768]{1,0:T(8,128)(2,1)} %copy-done.24, bf16[320,768]{1,0:T(8,128)(2,1)} %copy-done.37, bf16[320,576]{1,0:T(8,128)(2,1)} %copy-done.11, bf16[320,576]{1,0:T(8,128)(2,1)} %copy-done.47, ...), custom_call_target="tpu_custom_call" | custom-call | flops 575000000 | bytes 1 | tf_op jit(solution)/shard_map/weight_grad/pallas_call | solution.py:687
  314.2 8.9 %collective-permute-done.70 = bf16[208,768]{1,0:T(8,128)(2,1)} collective-permute-done((bf16[208,768]{1,0:T(8,128)(2,1)S(1)}, bf16[208,768]{1,0:T(8,128)(2,1)}, u32[]{:S(2)}, u32[]{:S(2)}) %collective-permute-start.70) | collective-permute-done | bytes 319520 | tf_op jit(solution)/shard_map/ppermute | solution.py:60
  335.2 5.5 %collective-permute-done.74 = bf16[208,768]{1,0:T(8,128)(2,1)S(1)} collective-permute-done((bf16[208,768]{1,0:T(8,128)(2,1)S(1)}, bf16[208,768]{1,0:T(8,128)(2,1)S(1)}, u32[]{:S(2)}, u32[]{:S(2)}) %collective-permute-start.74) | collective-permute-done | bytes 319520 | tf_op jit(solution)/shard_map/ppermute | solution.py:60
  341.8 5.3 %collective-permute-done.77 = bf16[192,768]{1,0:T(8,128)(2,1)S(1)} collective-permute-done((bf16[192,768]{1,0:T(8,128)(2,1)S(1)}, bf16[192,768]{1,0:T(8,128)(2,1)S(1)}, u32[]{:S(2)}, u32[]{:S(2)}) %collective-permute-start.77) | collective-permute-done | bytes 294944 | tf_op jit(solution)/shard_map/ppermute | solution.py:60
  (345 shorter events, 133.5 us)
Async XLA Ops:
  16.7 21.7 %collective-permute-start.15 = (bf16[384,768]{1,0:T(8,128)(2,1)}, bf16[384,768]{1,0:T(8,128)(2,1)S(1)}, u32[]{:S(2)}, u32[]{:S(2)}) collective-permute-start(bf16[384,768]{1,0:T(8,128)(2,1)} %pad_maximum_fusion.refs_0_.refs_16_.refs_32_), channel_id=1, source_target_pairs={{0,2},{1,3},{2,0},{3,1},{4,6},{5,7},{6,4},{7,5},{8,10},{9,11},{10,... | collective-permute-start | bytes 1769480 | tf_op jit(solution)/shard_map/ppermute | solution.py:55
  20.0 18.4 %collective-permute-start.5 = (bf16[208,768]{1,0:T(8,128)(2,1)S(1)}, bf16[208,768]{1,0:T(8,128)(2,1)}, u32[]{:S(2)}, u32[]{:S(2)}) collective-permute-start(bf16[208,768]{1,0:T(8,128)(2,1)S(1)} %collective-permute-done.3.refs_4_.refs_36_), channel_id=1, source_target_pairs={{0,2},{1,3},{2,0},{3,1},{4,6},{5,7},{6,4},{7,5},{8,10},{9,11},{10,... | collective-permute-start | bytes 958472 | tf_op jit(solution)/shard_map/ppermute | solution.py:55
  20.5 20.7 %collective-permute-start = (bf16[208,768]{1,0:T(8,128)(2,1)S(1)}, bf16[208,768]{1,0:T(8,128)(2,1)S(1)}, u32[]{:S(2)}, u32[]{:S(2)}) collective-permute-start(bf16[208,768]{1,0:T(8,128)(2,1)S(1)} %pad_maximum_fusion.1.refs_0_.refs_32_), channel_id=1, source_target_pairs={{0,1},{1,0},{2,3},{3,2},{4,5},{5,4},{6,7},{7,6},{8,9},{9,8},{10,11... | collective-permute-start | bytes 958472 | tf_op jit(solution)/shard_map/ppermute | solution.py:55
  39.2 18.7 %collective-permute-start.16 = (bf16[384,768]{1,0:T(8,128)(2,1)}, bf16[384,768]{1,0:T(8,128)(2,1)}, u32[]{:S(2)}, u32[]{:S(2)}) collective-permute-start(bf16[384,768]{1,0:T(8,128)(2,1)} %pad_maximum_fusion.refs_0_.refs_16_.refs_32_), channel_id=1, source_target_pairs={{0,4},{4,8},{8,12},{12,0},{1,5},{5,9},{9,13},{13,1},{2,6},{6,10},{... | collective-permute-start | bytes 1769480 | tf_op jit(solution)/shard_map/ppermute | solution.py:60
  43.2 19.8 %collective-permute-start.8 = (bf16[208,768]{1,0:T(8,128)(2,1)}, bf16[208,768]{1,0:T(8,128)(2,1)}, u32[]{:S(2)}, u32[]{:S(2)}) collective-permute-start(bf16[208,768]{1,0:T(8,128)(2,1)} %collective-permute-done.7.refs_8_.refs_40_), channel_id=1, source_target_pairs={{0,1},{1,0},{2,3},{3,2},{4,5},{5,4},{6,7},{7,6},{8,9},{9,8},{10,11... | collective-permute-start | bytes 958472 | tf_op jit(solution)/shard_map/ppermute | solution.py:55
  43.3 21.3 %collective-permute-start.6 = (bf16[208,768]{1,0:T(8,128)(2,1)}, bf16[208,768]{1,0:T(8,128)(2,1)}, u32[]{:S(2)}, u32[]{:S(2)}) collective-permute-start(bf16[208,768]{1,0:T(8,128)(2,1)} %collective-permute-done.5.refs_6_.refs_38_), channel_id=1, source_target_pairs={{0,1},{1,0},{2,3},{3,2},{4,5},{5,4},{6,7},{7,6},{8,9},{9,8},{10,11... | collective-permute-start | bytes 958472 | tf_op jit(solution)/shard_map/ppermute | solution.py:55
  73.9 24.0 %collective-permute-start.18 = (bf16[4,320,384]{2,1,0:T(8,128)(2,1)S(1)}, bf16[4,320,384]{2,1,0:T(8,128)(2,1)S(1)}, u32[]{:S(2)}, u32[]{:S(2)}) collective-permute-start(bf16[4,320,384]{2,1,0:T(8,128)(2,1)S(1)} %get-tuple-element.90.kv_own_ref), channel_id=1, source_target_pairs={{0,1},{1,0},{2,3},{3,2},{4,5},{5,4},{6,7},{7,6},{8,9},{9,8},{10,11... | collective-permute-start | bytes 2949128 | tf_op jit(solution)/shard_map/ppermute | solution.py:55
  82.3 31.4 %collective-permute-start.19 = (bf16[384,768]{1,0:T(8,128)(2,1)}, bf16[384,768]{1,0:T(8,128)(2,1)S(1)}, u32[]{:S(2)}, u32[]{:S(2)}) collective-permute-start(bf16[384,768]{1,0:T(8,128)(2,1)} %pad_maximum_fusion.refs_0_.refs_16_.refs_32_), channel_id=1, source_target_pairs={{0,1},{1,0},{2,3},{3,2},{4,5},{5,4},{6,7},{7,6},{8,9},{9,8},{10,11... | collective-permute-start | bytes 1769480 | tf_op jit(solution)/shard_map/ppermute | solution.py:55
  82.4 31.8 %collective-permute-start.20 = (bf16[384,768]{1,0:T(8,128)(2,1)S(1)}, bf16[384,768]{1,0:T(8,128)(2,1)S(1)}, u32[]{:S(2)}, u32[]{:S(2)}) collective-permute-start(bf16[384,768]{1,0:T(8,128)(2,1)S(1)} %copy-done.61), channel_id=1, source_target_pairs={{0,1},{1,0},{2,3},{3,2},{4,5},{5,4},{6,7},{7,6},{8,9},{9,8},{10,11... | collective-permute-start | bytes 1769480 | tf_op jit(solution)/shard_map/ppermute | solution.py:55
  95.7 18.7 %collective-permute-start.21 = (bf16[384,768]{1,0:T(8,128)(2,1)}, bf16[384,768]{1,0:T(8,128)(2,1)S(1)}, u32[]{:S(2)}, u32[]{:S(2)}) collective-permute-start(bf16[384,768]{1,0:T(8,128)(2,1)} %collective-permute-done.16.refs_4_.refs_20_.refs_36_), channel_id=1, source_target_pairs={{0,1},{1,0},{2,3},{3,2},{4,5},{5,4},{6,7},{7,6},{8,9},{9,8},{10,11... | collective-permute-start | bytes 1769480 | tf_op jit(solution)/shard_map/ppermute | solution.py:55
  145.0 42.2 %collective-permute-start.35 = (bf16[320,768]{1,0:T(8,128)(2,1)S(1)}, bf16[320,768]{1,0:T(8,128)(2,1)S(1)}, u32[]{:S(2)}, u32[]{:S(2)}) collective-permute-start(bf16[320,768]{1,0:T(8,128)(2,1)S(1)} %get-tuple-element.139.refs_0_), channel_id=1, source_target_pairs={{16,18},{17,19},{18,16},{19,17},{20,22},{21,23},{22,20},{23,21},{2... | collective-permute-start | bytes 1474568 | tf_op jit(solution)/shard_map/ppermute | solution.py:85
  163.9 23.8 %collective-permute-start.36 = (bf16[2,320,768]{2,1,0:T(8,128)(2,1)S(1)}, bf16[2,320,768]{2,1,0:T(8,128)(2,1)S(1)}, u32[]{:S(2)}, u32[]{:S(2)}) collective-permute-start(bf16[2,320,768]{2,1,0:T(8,128)(2,1)S(1)} %get-tuple-element.110), channel_id=1, source_target_pairs={{0,2},{1,3},{2,0},{3,1},{4,6},{5,7},{6,4},{7,5},{8,10},{9,11},{10,... | collective-permute-start | bytes 2949128 | tf_op jit(solution)/shard_map/ppermute | solution.py:55
  187.7 27.0 %collective-permute-start.40 = (bf16[320,768]{1,0:T(8,128)(2,1)S(1)}, bf16[320,768]{1,0:T(8,128)(2,1)S(1)}, u32[]{:S(2)}, u32[]{:S(2)}) collective-permute-start(bf16[320,768]{1,0:T(8,128)(2,1)S(1)} %get-tuple-element.113), channel_id=1, source_target_pairs={{0,1},{1,0},{2,3},{3,2},{4,5},{5,4},{6,7},{7,6},{8,9},{9,8},{10,11... | collective-permute-start | bytes 1474568 | tf_op jit(solution)/shard_map/ppermute | solution.py:55
  188.2 26.5 %collective-permute-start.42 = (bf16[320,768]{1,0:T(8,128)(2,1)}, bf16[320,768]{1,0:T(8,128)(2,1)}, u32[]{:S(2)}, u32[]{:S(2)}) collective-permute-start(bf16[320,768]{1,0:T(8,128)(2,1)} %get-tuple-element.135.refs_0_), channel_id=1, source_target_pairs={{0,2},{1,3},{2,0},{3,1},{4,6},{5,7},{6,4},{7,5},{8,10},{9,11},{10,... | collective-permute-start | bytes 1474568 | tf_op jit(solution)/shard_map/ppermute | solution.py:55
  213.4 32.6 %collective-permute-start.46 = (bf16[320,768]{1,0:T(8,128)(2,1)S(1)}, bf16[320,768]{1,0:T(8,128)(2,1)S(1)}, u32[]{:S(2)}, u32[]{:S(2)}) collective-permute-start(bf16[320,768]{1,0:T(8,128)(2,1)S(1)} %collective-permute-done.39), channel_id=1, source_target_pairs={{16,0},{17,1},{18,2},{19,3},{20,4},{21,5},{22,6},{23,7},{24,8},{25... | collective-permute-start | bytes 1474568 | tf_op jit(solution)/shard_map/ppermute | solution.py:765
  227.2 23.1 %collective-permute-start.44 = (bf16[2,320,768]{2,1,0:T(8,128)(2,1)S(1)}, bf16[2,320,768]{2,1,0:T(8,128)(2,1)}, u32[]{:S(2)}, u32[]{:S(2)}) collective-permute-start(bf16[2,320,768]{2,1,0:T(8,128)(2,1)S(1)} %get-tuple-element.122), channel_id=1, source_target_pairs={{0,2},{1,3},{2,0},{3,1},{4,6},{5,7},{6,4},{7,5},{8,10},{9,11},{10,... | collective-permute-start | bytes 2949128 | tf_op jit(solution)/shard_map/ppermute | solution.py:55
  247.0 21.6 %collective-permute-start.52 = (bf16[320,768]{1,0:T(8,128)(2,1)}, bf16[320,768]{1,0:T(8,128)(2,1)S(1)}, u32[]{:S(2)}, u32[]{:S(2)}) collective-permute-start(bf16[320,768]{1,0:T(8,128)(2,1)} %get-tuple-element.135.refs_0_), channel_id=1, source_target_pairs={{0,1},{1,0},{2,3},{3,2},{4,5},{5,4},{6,7},{7,6},{8,9},{9,8},{10,11... | collective-permute-start | bytes 1474568 | tf_op jit(solution)/shard_map/ppermute | solution.py:55
  250.4 18.7 %collective-permute-start.53 = (bf16[320,768]{1,0:T(8,128)(2,1)}, bf16[320,768]{1,0:T(8,128)(2,1)S(1)}, u32[]{:S(2)}, u32[]{:S(2)}) collective-permute-start(bf16[320,768]{1,0:T(8,128)(2,1)} %collective-permute-done.42.refs_2_), channel_id=1, source_target_pairs={{0,1},{1,0},{2,3},{3,2},{4,5},{5,4},{6,7},{7,6},{8,9},{9,8},{10,11... | collective-permute-start | bytes 1474568 | tf_op jit(solution)/shard_map/ppermute | solution.py:55
  250.4 19.4 %collective-permute-start.50 = (bf16[320,768]{1,0:T(8,128)(2,1)S(1)}, bf16[320,768]{1,0:T(8,128)(2,1)S(1)}, u32[]{:S(2)}, u32[]{:S(2)}) collective-permute-start(bf16[320,768]{1,0:T(8,128)(2,1)S(1)} %get-tuple-element.133.refs_8_), channel_id=1, source_target_pairs={{0,2},{1,3},{2,0},{3,1},{4,6},{5,7},{6,4},{7,5},{8,10},{9,11},{10,... | collective-permute-start | bytes 1474568 | tf_op jit(solution)/shard_map/ppermute | solution.py:55
  251.9 19.0 %collective-permute-start.54 = (bf16[320,768]{1,0:T(8,128)(2,1)}, bf16[320,768]{1,0:T(8,128)(2,1)S(1)}, u32[]{:S(2)}, u32[]{:S(2)}) collective-permute-start(bf16[320,768]{1,0:T(8,128)(2,1)} %copy-done.14), channel_id=1, source_target_pairs={{0,1},{1,0},{2,3},{3,2},{4,5},{5,4},{6,7},{7,6},{8,9},{9,8},{10,11... | collective-permute-start | bytes 1474568 | tf_op jit(solution)/shard_map/ppermute | solution.py:55
  269.1 20.8 %collective-permute-start.49 = (bf16[2,320,576]{2,1,0:T(8,128)(2,1)S(1)}, bf16[2,320,576]{2,1,0:T(8,128)(2,1)S(1)}, u32[]{:S(2)}, u32[]{:S(2)}) collective-permute-start(bf16[2,320,576]{2,1,0:T(8,128)(2,1)S(1)} %get-tuple-element.132), channel_id=1, source_target_pairs={{0,2},{1,3},{2,0},{3,1},{4,6},{5,7},{6,4},{7,5},{8,10},{9,11},{10,... | collective-permute-start | bytes 2211848 | tf_op jit(solution)/shard_map/ppermute | solution.py:55
  270.9 19.1 %collective-permute-start.61 = (bf16[320,768]{1,0:T(8,128)(2,1)S(1)}, bf16[320,768]{1,0:T(8,128)(2,1)S(1)}, u32[]{:S(2)}, u32[]{:S(2)}) collective-permute-start(bf16[320,768]{1,0:T(8,128)(2,1)S(1)} %broadcast_select_fusion.2.refs_2_), channel_id=1, source_target_pairs={{0,1},{1,0},{2,3},{3,2},{4,5},{5,4},{6,7},{7,6},{8,9},{9,8},{10,11... | collective-permute-start | bytes 1474568 | tf_op jit(solution)/shard_map/ppermute | solution.py:55
  271.1 19.0 %collective-permute-start.66 = (bf16[320,192]{1,0:T(8,128)(2,1)S(1)}, bf16[320,192]{1,0:T(8,128)(2,1)S(1)}, u32[]{:S(2)}, u32[]{:S(2)}) collective-permute-start(bf16[320,192]{1,0:T(8,128)(2,1)S(1)} %copy-done.16), channel_id=1, source_target_pairs={{0,1},{1,0},{2,3},{3,2},{4,5},{5,4},{6,7},{7,6},{8,9},{9,8},{10,11... | collective-permute-start | bytes 368648 | tf_op jit(solution)/shard_map/ppermute | solution.py:55
  310.8 18.8 %collective-permute-start.72 = (bf16[320,768]{1,0:T(8,128)(2,1)}, bf16[320,768]{1,0:T(8,128)(2,1)}, u32[]{:S(2)}, u32[]{:S(2)}) collective-permute-start(bf16[320,768]{1,0:T(8,128)(2,1)} %get-tuple-element.131.refs_0_), channel_id=1, source_target_pairs={{0,1},{1,0},{2,3},{3,2},{4,5},{5,4},{6,7},{7,6},{8,9},{9,8},{10,11... | collective-permute-start | bytes 1474568 | tf_op jit(solution)/shard_map/ppermute | solution.py:55
  (131 other events, 1702.9 us)
